TPU v7x, 256 devices: a whole 4x4x8 slice. The times are simulated.
256 devices in a mesh: dp: 8 (over x, core), expert: 32 (over z, y).
Axes of the slice: x: 4, y: 4, z: 8, core: 2. Of those that a mesh axis runs over, the one named last changes fastest.
Arguments:
- tokens: bfloat16 [32768, 8192], P(('dp', 'expert')), may hold values from -6 to 6
- cotangent: bfloat16 [32768, 8192], P(('dp', 'expert')), may hold values from -0.125 to 0.125
- routes: int32 [32768, 2], P(('dp', 'expert')), may hold values from 0 to 31, all different within a row; in each aligned block of 128 rows (0 to 127, 128 to 255, ...) at most 9 rows name the same one
- combine_weights: float32 [32768, 2], P(('dp', 'expert')), may hold values from 0.2 to 1
- gate_dense: bfloat16 [8192, 14336], P(('dp', 'expert')), may hold values from -0.0625 to 0.0625
- up_dense: bfloat16 [8192, 14336], P(('dp', 'expert')), may hold values from -0.0625 to 0.0625
- down_dense: bfloat16 [8192, 14336], P(('dp', 'expert')), may hold values from -0.25 to 0.25
Outputs:
- grad_gate: float32 [8192, 14336], P('dp', 'expert')
- grad_up: float32 [8192, 14336], P('dp', 'expert')
- grad_down: float32 [8192, 14336], P('dp', 'expert')
Inputs may be any that keep to these rules, and one draw needn't show every extreme that they name: `routes`: the 2 experts of a token differ. Among the tokens of one device no expert is chosen more than 9 times, and in some device one expert is chosen exactly 9 times.
All inputs are finite; a program needn't handle non-finite values.
Results may differ from a plain program's by a relative error of at most 0.004.
Values may be sent and summed in bfloat16 or wider, within the bound.
No kernel may reach another device: no remote copies, remote signals or barrier semaphores. Data moves between devices by JAX's collectives and lax.ppermute only.
A program may use at most 192 MiB of HBM per device.

v0:
```python
import jax
import jax.numpy as jnp
from jax import lax
from jax.sharding import PartitionSpec as P


def silu_parts(gate_vals):
    sigma = jax.nn.sigmoid(gate_vals)
    return (gate_vals * sigma, sigma * (1.0 + gate_vals * (1.0 - sigma)))


def contract_rows(left, right):
    return lax.dot_general(
        left, right, (((0,), (0,)), ((), ())), preferred_element_type=jnp.float32
    )


def per_device(tokens, cotangent, routes, combine_weights, gate_dense, up_dense, down_dense):
    w_gate, w_up, w_down = (
        lax.all_to_all(gate_dense, "expert", split_axis=1, concat_axis=0, tiled=True),
        lax.all_to_all(up_dense, "expert", split_axis=1, concat_axis=0, tiled=True),
        lax.all_to_all(down_dense, "expert", split_axis=1, concat_axis=0, tiled=True),
    )
    owners = lax.axis_size("expert")
    tok_rows = tokens.shape[0]
    choose = routes.shape[1]
    width = tokens.shape[1]
    hidden_width = w_gate.shape[1]
    amount = tok_rows * choose
    capacity = (9 * choose * tok_rows + 8 * owners - 1) // (8 * owners)
    flat_routes = routes.reshape(amount)
    one_hot = (flat_routes[:, None] == jnp.arange(owners, dtype=jnp.int32)[None, :]).astype(
        jnp.int32
    )
    rank_in = jnp.cumsum(one_hot, axis=0, dtype=jnp.int32) - 1
    slot_pos = jnp.sum(one_hot * rank_in, axis=1, dtype=jnp.int32)
    position = slot_pos * owners + flat_routes
    row_index = (
        jnp.full((capacity * owners,), amount, jnp.int32)
        .at[position]
        .set(jnp.arange(amount, dtype=jnp.int32))
    )
    valid = (row_index < amount).astype(jnp.bfloat16)[:, None]
    safe = jnp.minimum(row_index, amount - 1)
    token_of = safe // choose
    x_send = (jnp.take(tokens, token_of, axis=0) * valid).reshape(capacity, owners, width)
    scaled = (combine_weights.T[:, :, None] * cotangent[None, :, :].astype(jnp.float32)).astype(
        jnp.bfloat16
    )
    scaled = scaled.reshape(amount, width)
    scaled_index = safe % choose * tok_rows + token_of
    dy_send = (jnp.take(scaled, scaled_index, axis=0) * valid).reshape(capacity, owners, width)
    x_cols, dy_cols = (
        lax.all_to_all(
            lax.all_to_all(x_send, "dp", split_axis=2, concat_axis=0, tiled=True),
            "expert",
            split_axis=1,
            concat_axis=1,
            tiled=True,
        ),
        lax.all_to_all(
            lax.all_to_all(dy_send, "dp", split_axis=2, concat_axis=0, tiled=True),
            "expert",
            split_axis=1,
            concat_axis=1,
            tiled=True,
        ),
    )
    total_rows = x_cols.shape[0] * x_cols.shape[1]
    x_cols = x_cols.reshape(total_rows, x_cols.shape[2])
    dy_cols = dy_cols.reshape(total_rows, dy_cols.shape[2])
    w_pair = jnp.concatenate([w_gate, w_up], axis=1)
    piece = x_cols
    pair = lax.psum_scatter(
        jnp.dot(piece, w_pair, preferred_element_type=jnp.float32),
        "dp",
        scatter_dimension=0,
        tiled=True,
    )
    gate_vals = pair[:, :hidden_width]
    up_vals = pair[:, hidden_width:]
    active, slope = silu_parts(gate_vals)
    piece = dy_cols
    back = lax.psum_scatter(
        jnp.dot(piece, w_down, preferred_element_type=jnp.float32),
        "dp",
        scatter_dimension=0,
        tiled=True,
    )
    d_pair = jnp.concatenate(
        [(back * up_vals * slope).astype(jnp.bfloat16), (back * active).astype(jnp.bfloat16)],
        axis=1,
    )
    hidden_share = (active * up_vals).astype(jnp.bfloat16)
    grad_down = contract_rows(dy_cols, lax.all_gather(hidden_share, "dp", axis=0, tiled=True))
    grad_pair = contract_rows(x_cols, lax.all_gather(d_pair, "dp", axis=0, tiled=True))
    return (grad_pair[:, :hidden_width], grad_pair[:, hidden_width:], grad_down)


def solution(mesh):
    return jax.shard_map(
        per_device,
        mesh=mesh,
        in_specs=(
            P(("dp", "expert"), None),
            P(("dp", "expert"), None),
            P(("dp", "expert"), None),
            P(("dp", "expert"), None),
            P(("dp", "expert"), None),
            P(("dp", "expert"), None),
            P(("dp", "expert"), None),
        ),
        out_specs=(P("dp", "expert"), P("dp", "expert"), P("dp", "expert")),
        check_vma=False,
    )
```

profile of v0, /device:TPU:1, one launch (start us, length us, event | category | flops | bytes accessed | tf_op | source)
XLA Modules:
  0.0 738.7 jit_solution(15185901229758014826)
XLA Ops:
  11.3 12.0 %all-to-all-start.5 = ((bf16[32,32,448]{2,0,1:T(8,128)(2,1)}), bf16[32,32,448]{2,0,1:T(8,128)(2,1)S(1)}, u32[]{:S(2)}, u32[]{:S(2)}) async-start(bf16[32,32,448]{2,0,1:T(8,128)(2,1)} %copy.56), calls=%async_computation.6 | async-start | bytes 2097152 | tf_op jit(solution)/shard_map/all_to_all | solution.py:20
  33.3 33.9 %copy.45 = bf16[9,32,8192]{1,0,2:T(8,128)(2,1)} copy(bf16[9,32,8192]{2,1,0:T(8,128)(2,1)} %bitcast.65) | data formatting | bytes 9437184 | tf_op jit(solution)/shard_map/jit(_take)/gather | solution.py:46
  70.7 17.0 %gather_fusion.1 = bf16[288,8192]{1,0:T(8,128)(2,1)} fusion(bf16[256,8192]{1,0:T(8,128)(2,1)} %fusion, s32[1024]{0:T(1024)S(1)} %pad_clamp_fusion), kind=kCustom, calls=%fused_computation.1 | custom fusion | bytes 9438336 | tf_op jit(solution)/shard_map/jit(_take)/gather | solution.py:52
  87.8 34.3 %copy.50 = bf16[9,32,8192]{1,0,2:T(8,128)(2,1)} copy(bf16[9,32,8192]{2,1,0:T(8,128)(2,1)} %bitcast.64) | data formatting | bytes 9437184 | tf_op jit(solution)/shard_map/jit(_take)/gather | solution.py:52
  125.1 9.2 %all-to-all-start.4 = ((bf16[32,32,448]{2,0,1:T(8,128)(2,1)}), bf16[32,32,448]{2,0,1:T(8,128)(2,1)S(1)}, u32[]{:S(2)}, u32[]{:S(2)}) async-start(bf16[32,32,448]{2,0,1:T(8,128)(2,1)} %copy.55), calls=%async_computation.4 | async-start | bytes 2097152 | tf_op jit(solution)/shard_map/all_to_all | solution.py:22
  134.3 43.2 %select_multiply_fusion = (bf16[9,32,8192]{1,0,2:T(8,128)(2,1)}, bf16[9,32,8192]{1,0,2:T(8,128)(2,1)}) fusion(bf16[9,32,8192]{1,0,2:T(8,128)(2,1)} %copy.50, pred[9,32]{1,0:T(8,128)(4,1)S(1)} %broadcast_in_dim.35, bf16[9,32]{1,0:T(8,128)(2,1)S(1)} %reshape.117, bf16[9,32,8192]{1,0,2:T(8,128)(2,1)} %copy.45, pred[9,32]{1,0:T(8,128)(4,1)S(1)} %broadcast_in_dim.31), kind=kLoop, calls=%fused_computation.3 | loop fusion | flops 9437184 | bytes 18875520 | tf_op jit(solution)/shard_map/mul | solution.py:52
  177.6 21.9 %reshape.149 = bf16[8,2,147456]{2,1,0:T(2,128)(2,1)} reshape(bf16[8192,9,32]{2,1,0:T(8,128)(2,1)} %bitcast.61) | data formatting | bytes 9437184
  205.5 21.9 %reshape.147 = bf16[8,2,147456]{2,1,0:T(2,128)(2,1)} reshape(bf16[8192,9,32]{2,1,0:T(8,128)(2,1)} %bitcast.60) | data formatting | bytes 9437184
  227.4 32.6 %all-to-all-done.2 = bf16[8,2,147456]{2,1,0:T(2,128)(2,1)} async-done(((bf16[8,2,147456]{2,1,0:T(2,128)(2,1)}), bf16[8,2,147456]{2,1,0:T(2,128)(2,1)}, u32[]{:S(2)}, u32[]{:S(2)}) %all-to-all-start.2) | async-done | bytes 4718624 | tf_op jit(solution)/shard_map/all_to_all | solution.py:62
  265.6 22.4 %reshape.150 = bf16[8192,9,32]{2,1,0:T(8,128)(2,1)} reshape(bf16[8,2,147456]{2,1,0:T(2,128)(2,1)} %all-to-all-done.2) | data formatting | bytes 9437184
  288.0 30.9 %copy.52 = bf16[8,9,32,1024]{3,2,1,0:T(8,128)(2,1)} copy(bf16[8,9,32,1024]{2,1,3,0:T(8,128)(2,1)} %bitcast.58) | data formatting | bytes 9437184 | tf_op jit(solution)/shard_map/all_to_all | solution.py:62
  326.1 9.6 %all-to-all-start.3 = ((bf16[72,32,1024]{2,0,1:T(8,128)(2,1)}), bf16[72,32,1024]{2,0,1:T(8,128)(2,1)}, u32[]{:S(2)}, u32[]{:S(2)}) async-start(bf16[72,32,1024]{2,0,1:T(8,128)(2,1)} %copy.53), calls=%async_computation.3 | async-start | bytes 9437184 | tf_op jit(solution)/shard_map/all_to_all | solution.py:61
  335.7 22.4 %reshape.148 = bf16[8192,9,32]{2,1,0:T(8,128)(2,1)} reshape(bf16[8,2,147456]{2,1,0:T(2,128)(2,1)} %all-to-all-done) | data formatting | bytes 9437184
  358.1 30.9 %copy.47 = bf16[8,9,32,1024]{3,2,1,0:T(8,128)(2,1)} copy(bf16[8,9,32,1024]{2,1,3,0:T(8,128)(2,1)} %bitcast.59) | data formatting | bytes 9437184 | tf_op jit(solution)/shard_map/all_to_all | solution.py:55
  396.0 45.0 %all-to-all-done.3 = bf16[72,32,1024]{2,0,1:T(8,128)(2,1)} async-done(((bf16[72,32,1024]{2,0,1:T(8,128)(2,1)}), bf16[72,32,1024]{2,0,1:T(8,128)(2,1)}, u32[]{:S(2)}, u32[]{:S(2)}) %all-to-all-start.3) | async-done | bytes 4718624 | tf_op jit(solution)/shard_map/all_to_all | solution.py:61
  441.0 9.4 %all-to-all-start.1 = ((bf16[72,32,1024]{2,0,1:T(8,128)(2,1)}), bf16[72,32,1024]{2,0,1:T(8,128)(2,1)}, u32[]{:S(2)}, u32[]{:S(2)}) async-start(bf16[72,32,1024]{2,0,1:T(8,128)(2,1)} %copy.48), calls=%async_computation.1 | async-start | bytes 9437184 | tf_op jit(solution)/shard_map/all_to_all | solution.py:54
  466.0 87.7 %all-to-all-done.1 = bf16[72,32,1024]{2,0,1:T(8,128)(2,1)} async-done(((bf16[72,32,1024]{2,0,1:T(8,128)(2,1)}), bf16[72,32,1024]{2,0,1:T(8,128)(2,1)}, u32[]{:S(2)}, u32[]{:S(2)}) %all-to-all-start.1) | async-done | bytes 4718624 | tf_op jit(solution)/shard_map/all_to_all | solution.py:54
  553.6 9.3 %all-to-all-start.6 = ((bf16[32,32,448]{2,0,1:T(8,128)(2,1)}), bf16[32,32,448]{2,0,1:T(8,128)(2,1)S(1)}, u32[]{:S(2)}, u32[]{:S(2)}) async-start(bf16[32,32,448]{2,0,1:T(8,128)(2,1)} %copy.57), calls=%async_computation.7 | async-start | bytes 2097152 | tf_op jit(solution)/shard_map/all_to_all | solution.py:21
  570.0 19.1 %all-to-all-done.6 = bf16[32,32,448]{2,0,1:T(8,128)(2,1)S(1)} async-done(((bf16[32,32,448]{2,0,1:T(8,128)(2,1)}), bf16[32,32,448]{2,0,1:T(8,128)(2,1)S(1)}, u32[]{:S(2)}, u32[]{:S(2)}) %all-to-all-start.6) | async-done | bytes 917536 | tf_op jit(solution)/shard_map/all_to_all | solution.py:21
  589.1 9.8 %fusion.1 = f32[2304,896]{1,0:T(8,128)} fusion(bf16[2304,1024]{1,0:T(8,128)(2,1)} %bitcast.68, bf16[1024,448]{1,0:T(8,128)(2,1)S(1)} %bitcast.72, bf16[1024,448]{1,0:T(8,128)(2,1)S(1)} %bitcast.70), kind=kOutput, calls=%fused_computation.7 | convolution fusion | flops 4231528448 | bytes 14811136 | tf_op jit(solution)/shard_map/dot_general | solution.py:75
  599.1 54.0 %reduce-scatter.5.cloned.1.call-done = f32[288,896]{1,0:T(8,128)} async-done(((f32[2304,896]{1,0:T(8,128)}), f32[288,896]{1,0:T(8,128)}) %reduce-scatter.5.cloned.1.call-update) | async-done | bytes 1032208 | tf_op jit(solution)/shard_map/reduce_scatter | solution.py:74
  656.8 27.6 %all-gather.5.cloned.1.call-done = bf16[2304,448]{1,0:T(8,128)(2,1)} async-done(((bf16[288,448]{1,0:T(8,128)(2,1)}), bf16[2304,448]{1,0:T(8,128)(2,1)}) %all-gather.5.cloned.1.call-update) | async-done | bytes 2064400 | tf_op jit(solution)/shard_map/all_gather | solution.py:95
  691.2 30.7 %all-gather.3.cloned.1.call-done = bf16[2304,896]{1,0:T(8,128)(2,1)} async-done(((bf16[288,896]{1,0:T(8,128)(2,1)}), bf16[2304,896]{1,0:T(8,128)(2,1)}) %all-gather.3.cloned.1.call-update) | async-done | bytes 4128784 | tf_op jit(solution)/shard_map/all_gather | solution.py:96
  721.9 7.7 %fusion.17 = f32[1024,896]{0,1:T(8,128)S(1)} fusion(bf16[2304,1024]{1,0:T(8,128)(2,1)} %bitcast.69, bf16[2304,896]{1,0:T(8,128)(2,1)} %all-gather.3.cloned.1.call-done), kind=kOutput, calls=%fused_computation.50 | convolution fusion | flops 4227858432 | bytes 12517376 | tf_op jit(solution)/shard_map/dot_general | solution.py:13
  (70 shorter events, 81.9 us)
Async XLA Ops:
  7.2 19.1 %copy-start = (bf16[128,8192]{1,0:T(8,128)(2,1)S(1)}, bf16[128,8192]{1,0:T(8,128)(2,1)}, u32[]{:S(2)}) copy-start(bf16[128,8192]{1,0:T(8,128)(2,1)} %param.7) | copy-start | bytes 6291460
  7.2 16.2 %copy-start.6 = (s32[128,2]{0,1:T(2,128)S(1)}, s32[128,2]{0,1:T(2,128)}, u32[]{:S(2)}) copy-start(s32[128,2]{0,1:T(2,128)} %param.9) | copy-start | bytes 3076
  11.3 113.8 %all-to-all-start.5 = ((bf16[32,32,448]{2,0,1:T(8,128)(2,1)}), bf16[32,32,448]{2,0,1:T(8,128)(2,1)S(1)}, u32[]{:S(2)}, u32[]{:S(2)}) async-start(bf16[32,32,448]{2,0,1:T(8,128)(2,1)} %copy.56), calls=%async_computation.6 | async-start | bytes 2097152 | tf_op jit(solution)/shard_map/all_to_all | solution.py:20
  33.3 34.0 %copy-start.3 = (bf16[128,8192]{1,0:T(8,128)(2,1)S(1)}, bf16[128,8192]{1,0:T(8,128)(2,1)}, u32[]{:S(2)}) copy-start(bf16[128,8192]{1,0:T(8,128)(2,1)} %param.8) | copy-start | bytes 6291460
  67.2 0.7 copy-start.7
  87.8 34.5 %copy-start.4 = (bf16[32,14336]{1,0:T(8,128)(2,1)S(1)}, bf16[32,14336]{1,0:T(8,128)(2,1)}, u32[]{:S(2)}) copy-start(bf16[32,14336]{1,0:T(8,128)(2,1)} %param.13) | copy-start | bytes 2752516
  125.1 74.4 %all-to-all-start.4 = ((bf16[32,32,448]{2,0,1:T(8,128)(2,1)}), bf16[32,32,448]{2,0,1:T(8,128)(2,1)S(1)}, u32[]{:S(2)}, u32[]{:S(2)}) async-start(bf16[32,32,448]{2,0,1:T(8,128)(2,1)} %copy.55), calls=%async_computation.4 | async-start | bytes 2097152 | tf_op jit(solution)/shard_map/all_to_all | solution.py:22
  199.5 60.6 %all-to-all-start.2 = ((bf16[8,2,147456]{2,1,0:T(2,128)(2,1)}), bf16[8,2,147456]{2,1,0:T(2,128)(2,1)}, u32[]{:S(2)}, u32[]{:S(2)}) async-start(bf16[8,2,147456]{2,1,0:T(2,128)(2,1)} %reshape.149), calls=%async_computation.2 | async-start | bytes 9437184 | tf_op jit(solution)/shard_map/all_to_all | solution.py:62
  260.1 66.0 %all-to-all-start = ((bf16[8,2,147456]{2,1,0:T(2,128)(2,1)}), bf16[8,2,147456]{2,1,0:T(2,128)(2,1)}, u32[]{:S(2)}, u32[]{:S(2)}) async-start(bf16[8,2,147456]{2,1,0:T(2,128)(2,1)} %reshape.147), calls=%async_computation | async-start | bytes 9437184 | tf_op jit(solution)/shard_map/all_to_all | solution.py:55
  326.1 114.9 %all-to-all-start.3 = ((bf16[72,32,1024]{2,0,1:T(8,128)(2,1)}), bf16[72,32,1024]{2,0,1:T(8,128)(2,1)}, u32[]{:S(2)}, u32[]{:S(2)}) async-start(bf16[72,32,1024]{2,0,1:T(8,128)(2,1)} %copy.53), calls=%async_computation.3 | async-start | bytes 9437184 | tf_op jit(solution)/shard_map/all_to_all | solution.py:61
  441.0 112.7 %all-to-all-start.1 = ((bf16[72,32,1024]{2,0,1:T(8,128)(2,1)}), bf16[72,32,1024]{2,0,1:T(8,128)(2,1)}, u32[]{:S(2)}, u32[]{:S(2)}) async-start(bf16[72,32,1024]{2,0,1:T(8,128)(2,1)} %copy.48), calls=%async_computation.1 | async-start | bytes 9437184 | tf_op jit(solution)/shard_map/all_to_all | solution.py:54
  450.3 148.7 %reduce-scatter.3.cloned.1.call-start = ((), (), s32[]{:S(2)}) async-start(), calls=%async_computation.9 | async-start | bytes 5308416 | tf_op jit(solution)/shard_map/reduce_scatter | solution.py:84
  455.5 2.2 copy-start.2
  462.0 1.2 copy-start.5
  553.6 35.5 %all-to-all-start.6 = ((bf16[32,32,448]{2,0,1:T(8,128)(2,1)}), bf16[32,32,448]{2,0,1:T(8,128)(2,1)S(1)}, u32[]{:S(2)}, u32[]{:S(2)}) async-start(bf16[32,32,448]{2,0,1:T(8,128)(2,1)} %copy.57), calls=%async_computation.7 | async-start | bytes 2097152 | tf_op jit(solution)/shard_map/all_to_all | solution.py:21
  562.9 90.1 %reduce-scatter.5.cloned.1.call-start = ((), (), s32[]{:S(2)}) async-start(), calls=%async_computation.10 | async-start | bytes 9289728 | tf_op jit(solution)/shard_map/reduce_scatter | solution.py:74
  599.0 85.5 %all-gather.5.cloned.1.call-start = ((), (), s32[]{:S(2)}) async-start(), calls=%async_computation.12 | async-start | bytes 2654208 | tf_op jit(solution)/shard_map/all_gather | solution.py:95
  655.6 66.3 %all-gather.3.cloned.1.call-start = ((), (), s32[]{:S(2)}) async-start(), calls=%async_computation.11 | async-start | bytes 4644864 | tf_op jit(solution)/shard_map/all_gather | solution.py:96
  721.9 10.0 %copy-start.1 = (bf16[128,8192]{1,0:T(8,128)(2,1)S(1)}, bf16[128,8192]{1,0:T(8,128)(2,1)}, u32[]{:S(2)}) copy-start(bf16[128,8192]{1,0:T(8,128)(2,1)} %param.7) | copy-start | bytes 6291460
Sparse Core Ops, SparseCore 0:
  462.1 40.5 reduce-scatter.2
  599.1 53.8 reduce-scatter.4
  655.7 28.7 all-gather.4
  686.9 34.9 all-gather.2
where the time goes:
time: 747 us; the launch traced here: 739 us
  waiting for transfers between devices  297 us (40%)
  local copies, waits for them, and re-layouts  287 us (38%)
  starting transfers between devices  61.7 us (8%)
  other arithmetic  50.8 us (7%)
  matrix products  28.5 us (4%)
  between operations  14.3 us (2%)
    unnamed x21, local copies, waits for them, and re-layouts  92.2 us
    all_to_all x1, waiting for transfers between devices, per_device(): lax.all_to_all(lax.all_to_all(x_send, 'dp', split_axis=2, concat_axis=0,...  87.7 us
    reduce_scatter x1, waiting for transfers between devices, per_device(): lax.psum_scatter(jnp.dot(piece, w_pair, preferred_element_type=jnp.float3...  54 us
    gather x2, local copies, waits for them, and re-layouts, per_device(): jnp.take(scaled, scaled_index, axis=0) * valid  51.4 us
    all_to_all x1, waiting for transfers between devices, per_device(): lax.all_to_all(lax.all_to_all(dy_send, 'dp', split_axis=2, concat_axis=0,...  45 us
    mul x1, other arithmetic, per_device(): jnp.take(scaled, scaled_index, axis=0) * valid  43.2 us
    gather x2, local copies, waits for them, and re-layouts, per_device(): jnp.take(tokens, token_of, axis=0) * valid  40.8 us
    all_to_all x2, local copies, waits for them, and re-layouts, per_device(): lax.all_to_all(dy_send, 'dp', split_axis=2, concat_axis=0, tiled=True)  38.1 us
  transfers between devices with their start and end apart: 11, of which 7 were waited for; matrix products, arithmetic and copies ran while one was open for 46% of the time, Pallas kernels for 0%

commit v1 on v0

v1 whole, which is shorter than its diff:
```python
import jax
import jax.numpy as jnp
from jax import lax
from jax.experimental import pallas as pl
from jax.experimental.pallas import tpu as pltpu
from jax.sharding import Mesh, PartitionSpec as P

F32 = jnp.float32
BF16 = jnp.bfloat16
VMEM_LIMIT = 48 * 1024 * 1024


def iota(shape, dim):
    return lax.broadcasted_iota(jnp.int32, shape, dim)


def one_if(mask):
    return jnp.where(mask, 1.0, 0.0).astype(BF16)


def pack_rows(routes_t, weights_t, source, owners, blocks, scale):
    rows, width = source.shape
    part = width // blocks
    tiles = part // 128
    main = owners * 8

    def kernel(routes_ref, weights_ref, source_ref, out_ref, pick_ref, factor_ref):
        @pl.when(pl.program_id(0) == 0)
        def _():
            row = iota((2 * main, rows), 0)
            expert = lax.shift_right_logical(jnp.where(row < main, row, row - main), 3)
            first = routes_ref[0:1, :] == expert
            second = routes_ref[1:2, :] == expert
            named = first | second
            before = one_if(iota((rows, rows), 0) < iota((rows, rows), 1))
            rank = jnp.dot(one_if(named), before, preferred_element_type=F32)
            wanted = jnp.where(row < main, jnp.bitwise_and(row, 7), 8).astype(F32)
            picked = named & (rank == wanted)
            pick_ref[...] = one_if(picked)
            value = jnp.where(first, weights_ref[0:1, :], 0.0) + jnp.where(
                second, weights_ref[1:2, :], 0.0
            )
            factor_ref[...] = jnp.sum(jnp.where(picked, value, 0.0), axis=1, keepdims=True)

        val = jnp.dot(pick_ref[...], source_ref[...], preferred_element_type=F32)
        if scale:
            val = val * factor_ref[...]
        sub = jnp.bitwise_and(iota((main, 128), 0), 7)
        ninth = jnp.zeros((main, 128), F32)
        for j in range(tiles):
            cols = slice(128 * j, 128 * (j + 1))
            out_ref[0, :, 8 * j : 8 * (j + 1), :] = (
                val[:main, cols].reshape(owners, 8, 128).astype(BF16)
            )
            ninth = jnp.where(sub == j, val[main:, cols], ninth)
        out_ref[0, :, 8 * tiles :, :] = ninth.reshape(owners, 8, 128).astype(BF16)

    return pl.pallas_call(
        kernel,
        grid=(blocks,),
        in_specs=[
            pl.BlockSpec((2, rows), lambda i: (0, 0)),
            pl.BlockSpec((2, rows), lambda i: (0, 0)),
            pl.BlockSpec((rows, part), lambda i: (0, i)),
        ],
        out_specs=pl.BlockSpec((1, owners, 9 * tiles, 128), lambda i: (i, 0, 0, 0)),
        out_shape=jax.ShapeDtypeStruct((blocks, owners, 9 * tiles, 128), BF16),
        scratch_shapes=[pltpu.VMEM((2 * main, rows), BF16), pltpu.VMEM((2 * main, 1), F32)],
        compiler_params=pltpu.CompilerParams(vmem_limit_bytes=VMEM_LIMIT),
        cost_estimate=pl.CostEstimate(
            flops=4 * main * rows * width, bytes_accessed=2 * width * (rows + 9 * owners), transcendentals=0
        ),
        name="pack_rows",
    )(routes_t, weights_t, source)


def pack_weights(gate, up, down, owners):
    depth, total = gate.shape
    pair = 2 * total // owners
    wide = 512

    def kernel(gate_ref, up_ref, down_ref, out_ref):
        for n, ref in enumerate((gate_ref, up_ref, down_ref)):
            out_ref[0, :, n * wide : (n + 1) * wide] = ref[:, :wide]
            out_ref[1, :, n * wide : (n + 1) * wide] = ref[:, pair - wide :]

    spec = pl.BlockSpec((depth, pair), lambda i: (0, i))
    return pl.pallas_call(
        kernel,
        grid=(owners // 2,),
        in_specs=[spec, spec, spec],
        out_specs=pl.BlockSpec((2, depth, 3 * wide), lambda i: (i, 0, 0)),
        out_shape=jax.ShapeDtypeStruct((owners, depth, 3 * wide), BF16),
        cost_estimate=pl.CostEstimate(
            flops=0, bytes_accessed=2 * depth * (3 * total + owners * 3 * wide), transcendentals=0
        ),
        name="pack_weights",
    )(gate, up, down)


def unpack_and_multiply(received, weight, group):
    senders, height, _ = received.shape
    tiles = height // 9
    depth, columns = weight.shape
    main = group * 8
    rows = group * 9
    steps = senders // group

    def kernel(received_ref, weight_ref, rows_ref, product_ref):
        for j in range(tiles):
            rows_ref[:main, 128 * j : 128 * (j + 1)] = (
                received_ref[:, 8 * j : 8 * (j + 1), :].astype(F32).reshape(main, 128).astype(BF16)
            )
        last = received_ref[:, 8 * tiles :, :].astype(F32).reshape(main, 128).astype(BF16)
        row, col = iota((main, main), 0), iota((main, main), 1)
        turn = one_if(
            (row % group == lax.shift_right_logical(col, 3)) & (row // group == jnp.bitwise_and(col, 7))
        )
        ninth = jnp.dot(turn, last, preferred_element_type=F32).astype(BF16)
        for j in range(tiles):
            rows_ref[main:, 128 * j : 128 * (j + 1)] = ninth[group * j : group * (j + 1)]
        product_ref[...] = jnp.dot(rows_ref[...], weight_ref[...], preferred_element_type=F32)

    return pl.pallas_call(
        kernel,
        grid=(steps,),
        in_specs=[
            pl.BlockSpec((group, height, 128), lambda i: (i, 0, 0)),
            pl.BlockSpec((depth, columns), lambda i: (0, 0)),
        ],
        out_specs=[
            pl.BlockSpec((rows, depth), lambda i: (i, 0)),
            pl.BlockSpec((rows, columns), lambda i: (i, 0)),
        ],
        out_shape=[
            jax.ShapeDtypeStruct((steps * rows, depth), BF16),
            jax.ShapeDtypeStruct((steps * rows, columns), F32),
        ],
        compiler_params=pltpu.CompilerParams(vmem_limit_bytes=VMEM_LIMIT),
        cost_estimate=pl.CostEstimate(
            flops=2 * steps * rows * depth * columns,
            bytes_accessed=steps * rows * (4 * depth + 4 * columns) + 2 * depth * columns,
            transcendentals=0,
        ),
        name="unpack_and_multiply",
    )(received, weight)


def follow(value, earlier):
    def kernel(value_ref, earlier_ref, out_ref):
        del value_ref, earlier_ref, out_ref

    anywhere = pl.BlockSpec(memory_space=pl.ANY)
    return pl.pallas_call(
        kernel,
        in_specs=[anywhere, anywhere],
        out_specs=anywhere,
        out_shape=jax.ShapeDtypeStruct(value.shape, value.dtype),
        input_output_aliases={0: 0},
        name="follow",
    )(value, earlier)


def contract_rows(left, right):
    return lax.dot_general(left, right, (((0,), (0,)), ((), ())), preferred_element_type=F32)


def per_device(tokens, cotangent, routes, combine_weights, gate_dense, up_dense, down_dense):
    blocks, owners = lax.axis_size("dp"), lax.axis_size(("z", "y"))
    hidden = gate_dense.shape[1] // owners
    everyone = ("dp", "z", "y")
    routes_t, weights_t = routes.T, combine_weights.T

    w_send = pack_weights(gate_dense, up_dense, down_dense, owners)
    w_all = lax.all_to_all(w_send, ("z", "y"), split_axis=0, concat_axis=0, tiled=True)
    w_all = w_all.reshape(-1, w_all.shape[2])
    odd = lax.axis_index(("z", "y")) % 2 == 1
    wide = w_all.shape[1] // 3
    w_gate, w_up, w_down = (
        jnp.where(odd, w_all[:, (n + 1) * wide - hidden : (n + 1) * wide], w_all[:, n * wide : n * wide + hidden])
        for n in range(3)
    )
    w_pair = jnp.concatenate([w_gate, w_up], axis=1)

    def packed(source, scale):
        send = pack_rows(routes_t, weights_t, source, owners, blocks, scale)
        return send.reshape((-1,) + send.shape[2:])

    def exchange(send):
        return lax.all_to_all(send, everyone, split_axis=0, concat_axis=0, tiled=True)

    x_received = exchange(packed(tokens, False))
    x_rows, pair = unpack_and_multiply(x_received, w_pair, owners)
    pair = lax.psum_scatter(pair, "dp", scatter_dimension=0, tiled=True)
    gate_vals, up_vals = pair[:, :hidden], pair[:, hidden:]
    sigma = jax.nn.sigmoid(gate_vals)
    active = gate_vals * sigma
    slope = sigma * (1.0 + gate_vals * (1.0 - sigma))
    hidden_all = lax.all_gather((active * up_vals).astype(BF16), "dp", axis=0, tiled=True)

    dy_rows, back = unpack_and_multiply(
        exchange(follow(packed(cotangent, True), x_received)), w_down, owners
    )
    back = lax.psum_scatter(back, "dp", scatter_dimension=0, tiled=True)
    d_pair = jnp.concatenate(
        [(back * up_vals * slope).astype(BF16), (back * active).astype(BF16)], axis=1
    )
    grad_down = contract_rows(hidden_all, dy_rows).T
    grad_pair = contract_rows(lax.all_gather(d_pair, "dp", axis=0, tiled=True), x_rows)
    return (grad_pair[:hidden].T, grad_pair[hidden:].T, grad_down)


def solution(mesh):
    fine = Mesh(mesh.devices.reshape(mesh.devices.shape[0], -1, 4), ("dp", "z", "y"))
    split = P(("dp", "z", "y"), None)
    return jax.shard_map(
        per_device,
        mesh=fine,
        in_specs=(split,) * 7,
        out_specs=(P("dp", ("z", "y")),) * 3,
        check_vma=False,
    )
```

time: 747 us -> 488 us (0.65)
  local copies, waits for them, and re-layouts: 287 us -> 5.91 us
  blocking collectives: 0 us -> 117 us
  other arithmetic: 50.8 us -> 8.1 us
  Pallas kernels: 0 us -> 41 us
  starting transfers between devices: 61.7 us -> 25.4 us
  waiting for transfers between devices: 297 us -> 262 us
  matrix products: 28.5 us -> 14.2 us
    all_to_all x0 -> x1, blocking collectives: none -> 117 us  [exchange(): lax.all_to_all(send, everyone, split_axis=0, concat_axis=0, tiled=True)]
    all_to_all x12 -> x0, local copies, waits for them, and re-layouts: 97.7 us -> none  [the longest x2 38.1 us: per_device(): lax.all_to_all(dy_send, 'dp', split_axis=2, concat_axis=0, tiled=True)]
    gather x4 -> x0, local copies, waits for them, and re-layouts: 92.2 us -> none  [the longest x2 51.4 us: per_device(): jnp.take(scaled, scaled_index, axis=0) * valid]
    unnamed x21 -> x10, local copies, waits for them, and re-layouts: 92.2 us -> 3.64 us
    mul x2 -> x0, other arithmetic: 43.2 us -> none  [the longest x1 43.2 us: per_device(): jnp.take(scaled, scaled_index, axis=0) * valid]
    pallas_call x0 -> x6, Pallas kernels: none -> 41 us  [the longest x2 19.6 us: unpack_and_multiply(): pl.pallas_call(kernel, grid=(steps,), in_specs=[pl.BlockSpec((group, heig...]
    all_to_all x7 -> x2, starting transfers between devices: 61.1 us -> 25 us  [the longest x1 12.7 us: exchange(): lax.all_to_all(send, everyone, split_axis=0, concat_axis=0, tiled=True)]
    reduce_scatter x2, waiting for transfers between devices: 54 us -> 32.4 us  [the longest x1 32.4 us: per_device(): back = lax.psum_scatter(back, 'dp', scatter_dimension=0, tiled=True)]
  transfers between devices with their start and end apart: 11 -> 6, of which waited for: 7 -> 5; matrix products, arithmetic and copies ran while one was open for 46% -> 3% of each run, Pallas kernels for 0% -> 4%
where the time goes in v1:
time: 488 us; the launch traced here: 487 us
  waiting for transfers between devices  262 us (54%)
  blocking collectives  117 us (24%)
  Pallas kernels  41 us (8%)
  starting transfers between devices  25.4 us (5%)
  matrix products  14.2 us (3%)
  between operations  13.9 us (3%)
  other arithmetic  8.1 us (2%)
  local copies, waits for them, and re-layouts  5.91 us (1%)
    all_to_all x1, blocking collectives, exchange(): lax.all_to_all(send, everyone, split_axis=0, concat_axis=0, tiled=True)  117 us
    all_to_all x1, waiting for transfers between devices, exchange(): lax.all_to_all(send, everyone, split_axis=0, concat_axis=0, tiled=True)  104 us
    all_to_all x1, waiting for transfers between devices, per_device(): lax.all_to_all(w_send, ('z', 'y'), split_axis=0, concat_axis=0, tiled=True)  64.4 us
    reduce_scatter x1, waiting for transfers between devices, per_device(): back = lax.psum_scatter(back, 'dp', scatter_dimension=0, tiled=True)  32.4 us
    all_gather x1, waiting for transfers between devices, per_device(): lax.all_gather(d_pair, 'dp', axis=0, tiled=True)  30.7 us
    all_gather x1, waiting for transfers between devices, per_device(): lax.all_gather((active * up_vals).astype(BF16), 'dp', axis=0, tiled=True)  29.6 us
    pallas_call x2, Pallas kernels, unpack_and_multiply(): pl.pallas_call(kernel, grid=(steps,), in_specs=[pl.BlockSpec((group, heig...  19.6 us
    dot_general x2, matrix products, contract_rows(): lax.dot_general(left, right, (((0,), (0,)), ((), ())), preferred_element_...  14.2 us
  transfers between devices with their start and end apart: 6, of which 5 were waited for; matrix products, arithmetic and copies ran while one was open for 3% of the time, Pallas kernels for 4%

profile of v1, /device:TPU:1, one launch (start us, length us, event | category | flops | bytes accessed | tf_op | source)
XLA Modules:
  0.0 486.9 jit_solution(14987590224343810465)
XLA Ops:
  7.2 9.6 %pack_weights.1 = bf16[32,32,1536]{2,1,0:T(8,128)(2,1)} custom-call(bf16[32,14336]{1,0:T(8,128)(2,1)} %gate_ref.1, bf16[32,14336]{1,0:T(8,128)(2,1)} %up_ref.1, bf16[32,14336]{1,0:T(8,128)(2,1)} %down_ref.1), custom_call_target="tpu_custom_call" | custom-call | bytes 5898240 | tf_op jit(solution)/shard_map/pack_weights/pallas_call | solution.py:88
  16.7 12.3 %all-to-all-start.2 = ((bf16[32,32,1536]{2,1,0:T(8,128)(2,1)}), bf16[32,32,1536]{2,1,0:T(8,128)(2,1)}, u32[]{:S(2)}, u32[]{:S(2)}) async-start(bf16[32,32,1536]{2,1,0:T(8,128)(2,1)} %pack_weights.1), calls=%async_computation.2 | async-start | bytes 6291456 | tf_op jit(solution)/shard_map/all_to_all | solution.py:175
  29.1 5.9 %pack_rows.3 = bf16[8,32,72,128]{3,2,1,0:T(8,128)(2,1)} custom-call(s32[2,128]{1,0:T(2,128)S(1)} %bitcast.13, f32[2,128]{1,0:T(2,128)S(1)} %bitcast.15, bf16[128,8192]{1,0:T(8,128)(2,1)S(1)} %copy-done), custom_call_target="tpu_custom_call" | custom-call | flops 1073741824 | bytes 6815744 | tf_op jit(solution)/shard_map/pack_rows/pallas_call | solution.py:58
  35.0 64.4 %all-to-all-done.2 = bf16[32,32,1536]{2,1,0:T(8,128)(2,1)} async-done(((bf16[32,32,1536]{2,1,0:T(8,128)(2,1)}), bf16[32,32,1536]{2,1,0:T(8,128)(2,1)}, u32[]{:S(2)}, u32[]{:S(2)}) %all-to-all-start.2) | async-done | bytes 3145760 | tf_op jit(solution)/shard_map/all_to_all | solution.py:175
  99.4 12.7 %all-to-all-start = ((bf16[256,72,128]{2,1,0:T(8,128)(2,1)}), bf16[256,72,128]{2,1,0:T(8,128)(2,1)}, u32[]{:S(2)}, u32[]{:S(2)}) async-start(bf16[256,72,128]{2,1,0:T(8,128)(2,1)} %bitcast.18), calls=%async_computation | async-start | bytes 9437184 | tf_op jit(solution)/shard_map/all_to_all | solution.py:190
  112.2 4.0 slice_select_fusion.1
  116.2 0.6 pad_maximum_fusion.weight_ref
  116.8 104.5 %all-to-all-done.earlier_ref.received_ref = bf16[256,72,128]{2,1,0:T(8,128)(2,1)} async-done(((bf16[256,72,128]{2,1,0:T(8,128)(2,1)}), bf16[256,72,128]{2,1,0:T(8,128)(2,1)}, u32[]{:S(2)}, u32[]{:S(2)}) %all-to-all-start) | async-done | bytes 4718624 | tf_op jit(solution)/shard_map/all_to_all | solution.py:190
  221.3 10.9 %unpack_and_multiply.3 = (bf16[2304,1024]{1,0:T(8,128)(2,1)}, f32[2304,896]{1,0:T(8,128)}) custom-call(bf16[256,72,128]{2,1,0:T(8,128)(2,1)} %all-to-all-done.earlier_ref.received_ref, bf16[1024,896]{1,0:T(8,128)(2,1)S(1)} %pad_maximum_fusion.weight_ref), custom_call_target="tpu_custom_call" | custom-call | flops 4227858432 | bytes 19529728 | tf_op jit(solution)/shard_map/unpack_and_multiply/pallas_call | solution.py:124
  232.3 1.5 copy-done.1
  233.8 6.0 %pack_rows.2 = bf16[8,32,72,128]{3,2,1,0:T(8,128)(2,1)} custom-call(s32[2,128]{1,0:T(2,128)S(1)} %bitcast.14, f32[2,128]{1,0:T(2,128)S(1)} %bitcast.16, bf16[128,8192]{1,0:T(8,128)(2,1)S(1)} %copy-done.1), custom_call_target="tpu_custom_call" | custom-call | flops 1073741824 | bytes 6815744 | tf_op jit(solution)/shard_map/pack_rows/pallas_call | solution.py:58
  239.8 116.7 %all_to_all.15.received_ref = bf16[256,72,128]{2,1,0:T(8,128)(2,1)} all-to-all(bf16[256,72,128]{2,1,0:T(8,128)(2,1)} %follow.1), channel_id=1, replica_groups=mesh['dp'=8,'z'=8,'y'=4] {'dp','z','y'}, dimensions={0} | all-to-all | bytes 9437184 | tf_op jit(solution)/shard_map/all_to_all | solution.py:190
  356.4 8.7 %unpack_and_multiply.2 = (bf16[2304,1024]{1,0:T(8,128)(2,1)S(1)}, f32[2304,448]{1,0:T(8,128)}) custom-call(bf16[256,72,128]{2,1,0:T(8,128)(2,1)} %all_to_all.15.received_ref, bf16[1024,448]{1,0:T(8,128)(2,1)S(1)} %get-tuple-element.15.weight_ref), custom_call_target="tpu_custom_call" | custom-call | flops 2113929216 | bytes 14483456 | tf_op jit(solution)/shard_map/unpack_and_multiply/pallas_call | solution.py:124
  365.1 2.1 copy-done.4
  367.3 0.0 all-gather.5.cloned.1.call-start
  367.3 32.4 %reduce-scatter.3.cloned.1.call-done = f32[288,448]{1,0:T(8,128)} async-done(((f32[2304,448]{1,0:T(8,128)}), f32[288,448]{1,0:T(8,128)}) %reduce-scatter.3.cloned.1.call-update) | async-done | bytes 516112 | tf_op jit(solution)/shard_map/reduce_scatter | solution.py:204
  399.8 2.5 multiply_convert_fusion.2
  402.3 0.2 all-gather.3.cloned.1.call-start
  402.5 0.9 pad_maximum_fusion.1
  403.5 29.6 %all-gather.5.cloned.1.call-done = bf16[2304,448]{1,0:T(8,128)(2,1)} async-done(((bf16[288,448]{1,0:T(8,128)(2,1)}), bf16[2304,448]{1,0:T(8,128)(2,1)}) %all-gather.5.cloned.1.call-update) | async-done | bytes 2064400 | tf_op jit(solution)/shard_map/all_gather | solution.py:199
  433.1 6.7 %fusion.2 = f32[1024,448]{0,1:T(8,128)} fusion(bf16[2304,1024]{1,0:T(8,128)(2,1)} %copy-done.4, bf16[2304,448]{1,0:T(8,128)(2,1)} %all-gather.5.cloned.1.call-done), kind=kOutput, calls=%fused_computation.13 | convolution fusion | flops 2113929216 | bytes 8617984 | tf_op jit(solution)/shard_map/dot_general | solution.py:165
  439.8 30.7 %all-gather.3.cloned.1.call-done = bf16[2304,896]{1,0:T(8,128)(2,1)} async-done(((bf16[288,896]{1,0:T(8,128)(2,1)}), bf16[2304,896]{1,0:T(8,128)(2,1)}) %all-gather.3.cloned.1.call-update) | async-done | bytes 4128784 | tf_op jit(solution)/shard_map/all_gather | solution.py:209
  470.5 7.6 %fusion.1 = f32[896,1024]{1,0:T(8,128)S(1)} fusion(bf16[2304,896]{1,0:T(8,128)(2,1)} %all-gather.3.cloned.1.call-done, bf16[2304,1024]{1,0:T(8,128)(2,1)} %get-tuple-element.9), kind=kOutput, calls=%fused_computation.12 | convolution fusion | flops 4227858432 | bytes 12517376 | tf_op jit(solution)/shard_map/dot_general | solution.py:165
  478.1 2.3 slice_bitcast_fusion
  (16 shorter events, 0.2 us)
Async XLA Ops:
  16.7 12.3 %copy-start = (bf16[128,8192]{1,0:T(8,128)(2,1)S(1)}, bf16[128,8192]{1,0:T(8,128)(2,1)}, u32[]{:S(2)}) copy-start(bf16[128,8192]{1,0:T(8,128)(2,1)} %source_ref.3) | copy-start | bytes 6291460
  16.7 12.3 %copy-start.2 = (s32[128,2]{0,1:T(2,128)S(1)}, s32[128,2]{0,1:T(2,128)}, u32[]{:S(2)}) copy-start(s32[128,2]{0,1:T(2,128)} %param.9) | copy-start | bytes 3076
  16.7 12.3 %copy-start.3 = (f32[128,2]{0,1:T(2,128)S(1)}, f32[128,2]{0,1:T(2,128)}, u32[]{:S(2)}) copy-start(f32[128,2]{0,1:T(2,128)} %param.10) | copy-start | bytes 3076
  16.7 82.6 %all-to-all-start.2 = ((bf16[32,32,1536]{2,1,0:T(8,128)(2,1)}), bf16[32,32,1536]{2,1,0:T(8,128)(2,1)}, u32[]{:S(2)}, u32[]{:S(2)}) async-start(bf16[32,32,1536]{2,1,0:T(8,128)(2,1)} %pack_weights.1), calls=%async_computation.2 | async-start | bytes 6291456 | tf_op jit(solution)/shard_map/all_to_all | solution.py:175
  99.4 121.9 %all-to-all-start = ((bf16[256,72,128]{2,1,0:T(8,128)(2,1)}), bf16[256,72,128]{2,1,0:T(8,128)(2,1)}, u32[]{:S(2)}, u32[]{:S(2)}) async-start(bf16[256,72,128]{2,1,0:T(8,128)(2,1)} %bitcast.18), calls=%async_computation | async-start | bytes 9437184 | tf_op jit(solution)/shard_map/all_to_all | solution.py:190
  112.1 255.2 %reduce-scatter.5.cloned.1.call-start = ((), (), s32[]{:S(2)}) async-start(), calls=%async_computation.6 | async-start | bytes 9289728 | tf_op jit(solution)/shard_map/reduce_scatter | solution.py:194
  232.2 1.6 copy-start.1
  232.2 167.5 %reduce-scatter.3.cloned.1.call-start = ((), (), s32[]{:S(2)}) async-start(), calls=%async_computation.5 | async-start | bytes 5308416 | tf_op jit(solution)/shard_map/reduce_scatter | solution.py:204
  365.1 2.1 copy-start.4
  367.3 65.9 %all-gather.5.cloned.1.call-start = ((), (), s32[]{:S(2)}) async-start(), calls=%async_computation.8 | async-start | bytes 2654208 | tf_op jit(solution)/shard_map/all_gather | solution.py:199
  402.3 68.2 %all-gather.3.cloned.1.call-start = ((), (), s32[]{:S(2)}) async-start(), calls=%async_computation.7 | async-start | bytes 4644864 | tf_op jit(solution)/shard_map/all_gather | solution.py:209
Sparse Core Ops, SparseCore 0:
  232.4 81.7 reduce-scatter.4
  367.4 32.3 reduce-scatter.2
  402.4 30.6 all-gather.4
  435.5 34.9 all-gather.2

commit v2 on v1

v2 whole, which is shorter than its diff:
```python
import jax
import jax.numpy as jnp
from jax import lax
from jax.experimental import pallas as pl
from jax.experimental.pallas import tpu as pltpu
from jax.sharding import PartitionSpec as P

F32 = jnp.float32
BF16 = jnp.bfloat16
VMEM_LIMIT = 48 * 1024 * 1024
ANYWHERE = pl.BlockSpec(memory_space=pl.ANY)


def iota(shape, dim):
    return lax.broadcasted_iota(jnp.int32, shape, dim)


def one_if(mask):
    return jnp.where(mask, 1.0, 0.0).astype(BF16)


def pack_rows(routes_t, weights_t, source, owners, blocks, scale):
    rows, width = source.shape
    part = width // blocks
    tiles = part // 128
    main = owners * 8

    def kernel(routes_ref, weights_ref, source_ref, out_ref, pick_ref, factor_ref):
        @pl.when(pl.program_id(0) == 0)
        def _():
            row = iota((2 * main, rows), 0)
            expert = lax.shift_right_logical(jnp.where(row < main, row, row - main), 3)
            first = routes_ref[0:1, :] == expert
            second = routes_ref[1:2, :] == expert
            named = first | second
            before = one_if(iota((rows, rows), 0) < iota((rows, rows), 1))
            rank = jnp.dot(one_if(named), before, preferred_element_type=F32)
            wanted = jnp.where(row < main, jnp.bitwise_and(row, 7), 8).astype(F32)
            picked = named & (rank == wanted)
            pick_ref[...] = one_if(picked)
            value = jnp.where(first, weights_ref[0:1, :], 0.0) + jnp.where(
                second, weights_ref[1:2, :], 0.0
            )
            factor_ref[...] = jnp.sum(jnp.where(picked, value, 0.0), axis=1, keepdims=True)

        val = jnp.dot(pick_ref[...], source_ref[...], preferred_element_type=F32)
        if scale:
            val = val * factor_ref[...]
        sub = jnp.bitwise_and(iota((main, 128), 0), 7)
        ninth = jnp.zeros((main, 128), F32)
        for j in range(tiles):
            cols = slice(128 * j, 128 * (j + 1))
            out_ref[0, :, 8 * j : 8 * (j + 1), :] = (
                val[:main, cols].reshape(owners, 8, 128).astype(BF16)
            )
            ninth = jnp.where(sub == j, val[main:, cols], ninth)
        out_ref[0, :, 8 * tiles :, :] = ninth.reshape(owners, 8, 128).astype(BF16)

    return pl.pallas_call(
        kernel,
        grid=(blocks,),
        in_specs=[
            pl.BlockSpec((2, rows), lambda i: (0, 0)),
            pl.BlockSpec((2, rows), lambda i: (0, 0)),
            pl.BlockSpec((rows, part), lambda i: (0, i)),
        ],
        out_specs=pl.BlockSpec((1, owners, 9 * tiles, 128), lambda i: (i, 0, 0, 0)),
        out_shape=jax.ShapeDtypeStruct((blocks, owners, 9 * tiles, 128), BF16),
        scratch_shapes=[pltpu.VMEM((2 * main, rows), BF16), pltpu.VMEM((2 * main, 1), F32)],
        compiler_params=pltpu.CompilerParams(vmem_limit_bytes=VMEM_LIMIT),
        cost_estimate=pl.CostEstimate(
            flops=4 * main * rows * width, bytes_accessed=2 * width * (rows + 9 * owners), transcendentals=0
        ),
        name="pack_rows",
    )(routes_t, weights_t, source)


def pack_weights(gate, up, down, owners):
    depth, total = gate.shape
    wide = total // owners
    many = 4
    full = -(-3 * wide // 128) * 128

    def kernel(gate_ref, up_ref, down_ref, out_ref):
        for e in range(many):
            for n, ref in enumerate((gate_ref, up_ref, down_ref)):
                out_ref[e, :, n * wide : (n + 1) * wide] = ref[:, e * wide : (e + 1) * wide]
            out_ref[e, :, 3 * wide :] = jnp.zeros((depth, full - 3 * wide), BF16)

    spec = pl.BlockSpec((depth, many * wide), lambda i: (0, i))
    return pl.pallas_call(
        kernel,
        grid=(owners // many,),
        in_specs=[spec, spec, spec],
        out_specs=pl.BlockSpec((many, depth, full), lambda i: (i, 0, 0)),
        out_shape=jax.ShapeDtypeStruct((owners, depth, full), BF16),
        compiler_params=pltpu.CompilerParams(vmem_limit_bytes=VMEM_LIMIT),
        cost_estimate=pl.CostEstimate(
            flops=0, bytes_accessed=2 * depth * (3 * total + owners * full), transcendentals=0
        ),
        name="pack_weights",
    )(gate, up, down)


def unpack_and_multiply(place, received, weight, chips, first, parts, split):
    senders, height, _ = received.shape
    tiles = height // 9
    depth, columns = weight.shape
    group = senders // (2 * chips)
    main = group * 8
    half = group * 9 // 2

    def kernel(place_ref, received_ref, weight_ref, rows_ref, *refs):
        product_refs, work_ref = refs[:-1], refs[-1]
        core = place_ref[1]
        row, col = iota((main, main), 0), iota((main, main), 1)
        turn = one_if(
            (row % group == lax.shift_right_logical(col, 3)) & (row // group == jnp.bitwise_and(col, 7))
        )
        for j in range(tiles):
            work_ref[:main, 128 * j : 128 * (j + 1)] = (
                received_ref[:, 8 * j : 8 * (j + 1), :].astype(F32).reshape(main, 128).astype(BF16)
            )
        last = received_ref[:, 8 * tiles :, :].astype(F32).reshape(main, 128).astype(BF16)
        ninth = jnp.dot(turn, last, preferred_element_type=F32).astype(BF16)
        for j in range(tiles):
            work_ref[main:, 128 * j : 128 * (j + 1)] = ninth[group * j : group * (j + 1)]
        product = jnp.dot(work_ref[...], weight_ref[...], preferred_element_type=F32)
        low, high = product[:half], product[half:]
        if split:
            product_refs[0][0] = jnp.where(core == 0, low, high)
            product_refs[1][0] = jnp.where(core == 0, high, low)
            rows_ref[0, 0, 0] = work_ref[:half]
            rows_ref[0, 0, 1] = work_ref[half:]
        else:
            product_refs[0][0, 0, 0] = low
            product_refs[0][0, 1, 0] = high
            rows_ref[0, 0, core] = work_ref[:half]
            rows_ref[0, 0, 1 - core] = work_ref[half:]

    def slot(i, place_ref):
        return (place_ref[0] + chips - i % chips) % chips

    if split:
        rows_map = lambda i, s: (i // chips, i % chips, 0, 0, 0)
        product_specs = [pl.BlockSpec((1, half, columns), lambda i, s: (slot(i, s), 0, 0))] * 2
        product_shapes = [jax.ShapeDtypeStruct((chips, half, columns), F32)] * 2
    else:
        rows_map = lambda i, s: (i // chips, slot(i, s), 0, 0, 0)
        product_specs = [
            pl.BlockSpec((1, 2, 1, half, columns), lambda i, s: (i % chips, 0, i // chips, 0, 0))
        ]
        product_shapes = [jax.ShapeDtypeStruct((chips, 2, parts, half, columns), F32)]
    return pl.pallas_call(
        kernel,
        grid_spec=pltpu.PrefetchScalarGridSpec(
            num_scalar_prefetch=1,
            grid=(parts * chips,),
            in_specs=[
                pl.BlockSpec((group, height, 128), lambda i, s: (first * chips + i, 0, 0)),
                pl.BlockSpec((depth, columns), lambda i, s: (0, 0)),
            ],
            out_specs=[pl.BlockSpec((1, 1, 2, half, depth), rows_map)] + product_specs,
            scratch_shapes=[pltpu.VMEM((2 * half, depth), BF16)],
        ),
        out_shape=[jax.ShapeDtypeStruct((parts, chips, 2, half, depth), BF16)] + product_shapes,
        compiler_params=pltpu.CompilerParams(vmem_limit_bytes=VMEM_LIMIT),
        cost_estimate=pl.CostEstimate(
            flops=4 * parts * chips * half * depth * columns,
            bytes_accessed=parts * chips * half * (8 * depth + 8 * columns) + 2 * depth * columns,
            transcendentals=0,
        ),
        name="unpack_and_multiply",
    )(place, received, weight)


def add_steps(one, two, kind):
    steps, rows, columns = one.shape

    def kernel(one_ref, two_ref, *out_refs):
        for n in range(steps):
            out_refs[n][...] = (one_ref[n] + two_ref[n]).astype(out_refs[n].dtype)

    whole = pl.BlockSpec(memory_space=pltpu.VMEM)
    return pl.pallas_call(
        kernel,
        in_specs=[whole] * 2,
        out_specs=[whole] * steps,
        out_shape=[
            jax.ShapeDtypeStruct((rows, columns), kind if n else F32) for n in range(steps)
        ],
        compiler_params=pltpu.CompilerParams(vmem_limit_bytes=VMEM_LIMIT),
        cost_estimate=pl.CostEstimate(
            flops=one.size, bytes_accessed=12 * one.size, transcendentals=0
        ),
        name="add_steps",
    )(one, two)


def follow(values, earlier):
    count = len(values)

    def kernel(*refs):
        del refs

    return pl.pallas_call(
        kernel,
        in_specs=[ANYWHERE] * (count + len(earlier)),
        out_specs=[ANYWHERE] * count,
        out_shape=[jax.ShapeDtypeStruct(v.shape, v.dtype) for v in values],
        input_output_aliases={n: n for n in range(count)},
        name="follow",
    )(*values, *earlier)


def contract_rows(left, right):
    return lax.dot_general(left, right, (((0,), (0,)), ((), ())), preferred_element_type=F32)


def flat(value):
    return value.reshape(-1, value.shape[-1])


def per_device(tokens, cotangent, routes, combine_weights, gate_dense, up_dense, down_dense):
    blocks, owners = lax.axis_size("dp"), lax.axis_size("expert")
    chips = blocks // 2
    hidden = gate_dense.shape[1] // owners
    routes_t, weights_t = routes.T, combine_weights.T
    dp = lax.axis_index("dp")
    place = jnp.stack([dp // 2, dp % 2]).astype(jnp.int32)

    def along_x(step, value):
        if step % chips == 0:
            return value
        pairs = [(2 * i + c, 2 * ((i + step) % chips) + c) for i in range(chips) for c in range(2)]
        return lax.ppermute(value, "dp", pairs)

    def other_core(value):
        return lax.ppermute(value, "dp", [(i, i ^ 1) for i in range(blocks)])

    def packed(source, scale):
        return pack_rows(routes_t, weights_t, source, owners, blocks, scale)

    def exchange(send):
        send = send.reshape((-1,) + send.shape[-2:])
        return lax.all_to_all(send, ("dp", "expert"), split_axis=0, concat_axis=0, tiled=True)

    def reduce_rows(keep, send):
        sums = add_steps(keep, other_core(send), BF16)
        total = sums[0]
        for step in range(1, chips):
            total = total + along_x(-step, sums[step]).astype(F32)
        return total

    def gather_rows(value):
        pieces = []
        for step in range(chips):
            piece = along_x(step, value)
            pieces += [piece, other_core(piece)]
        return jnp.concatenate(pieces, axis=0)

    w_send = pack_weights(gate_dense, up_dense, down_dense, owners)
    w_all = flat(lax.all_to_all(w_send, "expert", split_axis=0, concat_axis=0, tiled=True))
    w_pair, w_down = w_all[:, : 2 * hidden], w_all[:, 2 * hidden : 3 * hidden]

    dy_send = packed(cotangent, True)
    (x_send,) = follow([packed(tokens, False)], [dy_send])
    x_received = exchange(x_send)
    dy_received = exchange(dy_send)

    x_rows, pair = unpack_and_multiply(place, x_received, w_pair, chips, 0, 2, False)
    pair = lax.psum_scatter(flat(pair), "dp", scatter_dimension=0, tiled=True)
    gate_vals, up_vals = pair[:, :hidden], pair[:, hidden:]
    sigma = jax.nn.sigmoid(gate_vals)
    active = gate_vals * sigma
    slope = up_vals * (sigma * (1.0 + gate_vals * (1.0 - sigma)))
    hidden_mine = (active * up_vals).astype(BF16)
    hidden_all = lax.all_gather(hidden_mine, "dp", axis=0, tiled=True)
    hidden_all = hidden_all.reshape(blocks, 2, -1, hidden)

    half = pair.shape[0] // 2
    grads = None
    for n in range(2):
        if n == 1:
            (dy_received,) = follow([dy_received], [hidden_mine])
        dy_rows, keep, send = unpack_and_multiply(place, dy_received, w_down, chips, n, 1, True)
        back = reduce_rows(keep, send)
        mine = slice(n * half, (n + 1) * half)
        d_pair = jnp.concatenate(
            [(back * slope[mine]).astype(BF16), (back * active[mine]).astype(BF16)], axis=1
        )
        grad_down = contract_rows(flat(hidden_all[:, n]), flat(dy_rows))
        grad_pair = contract_rows(gather_rows(d_pair), flat(x_rows[n]))
        grads = (grad_pair, grad_down) if grads is None else (grads[0] + grad_pair, grads[1] + grad_down)
    return (grads[0][:hidden].T, grads[0][hidden:].T, grads[1].T)


def solution(mesh):
    split = P(("dp", "expert"), None)
    return jax.shard_map(
        per_device,
        mesh=mesh,
        in_specs=(split,) * 7,
        out_specs=(P("dp", "expert"),) * 3,
        check_vma=False,
    )
```

time: 488 us -> 436 us (0.89)
  blocking collectives: 117 us -> 0 us
  waiting for transfers between devices: 262 us -> 308 us
  starting transfers between devices: 25.4 us -> 45.3 us
  local copies, waits for them, and re-layouts: 5.91 us -> 17.5 us
  matrix products: 14.2 us -> 9.29 us
    all_to_all x1 -> x0, blocking collectives: 117 us -> none  [exchange(): lax.all_to_all(send, everyone, split_axis=0, concat_axis=0, tiled=True)]
    all_to_all x2 -> x3, waiting for transfers between devices: 169 us -> 269 us  [the longest x2 215 us: exchange(): lax.all_to_all(send, ('dp', 'expert'), split_axis=0, concat_axis=0, tiled...]
    all_gather x2 -> x1, waiting for transfers between devices: 60.3 us -> 0.01 us  [per_device(): hidden_all = lax.all_gather(hidden_mine, 'dp', axis=0, tiled=True)]
    ppermute x0 -> x22, waiting for transfers between devices: none -> 39.5 us  [the longest x12 37.7 us: along_x(): return lax.ppermute(value, 'dp', pairs)]
    reduce_scatter x2 -> x1, waiting for transfers between devices: 32.4 us -> 0.01 us  [per_device(): pair = lax.psum_scatter(flat(pair), 'dp', scatter_dimension=0, tiled=True)]
    ppermute x0 -> x22, starting transfers between devices: none -> 13.9 us  [the longest x12 9.04 us: along_x(): return lax.ppermute(value, 'dp', pairs)]
    slice x0 -> x4, local copies, waits for them, and re-layouts: none -> 7.78 us  [the longest x2 2.94 us: per_device(): w_pair, w_down = (w_all[:, :2 * hidden], w_all[:, 2 * hidden:3 * hidden])]
    all_to_all x2 -> x3, starting transfers between devices: 25 us -> 31.4 us  [the longest x2 19.1 us: exchange(): lax.all_to_all(send, ('dp', 'expert'), split_axis=0, concat_axis=0, tiled...]
  transfers between devices with their start and end apart: 6 -> 27, of which waited for: 5 -> 14; matrix products, arithmetic and copies ran while one was open for 3% -> 4% of each run, Pallas kernels for 4% -> 5%
where the time goes in v2:
time: 436 us; the launch traced here: 435 us
  waiting for transfers between devices  308 us (71%)
  starting transfers between devices  45.3 us (10%)
  Pallas kernels  37.7 us (9%)
  local copies, waits for them, and re-layouts  17.5 us (4%)
  between operations  14.4 us (3%)
  matrix products  9.29 us (2%)
    all_to_all x2, waiting for transfers between devices, exchange(): lax.all_to_all(send, ('dp', 'expert'), split_axis=0, concat_axis=0, tiled...  215 us
    all_to_all x1, waiting for transfers between devices, per_device(): lax.all_to_all(w_send, 'expert', split_axis=0, concat_axis=0, tiled=True)  53.3 us
    ppermute x12, waiting for transfers between devices, along_x(): return lax.ppermute(value, 'dp', pairs)  37.7 us
    pallas_call x3, Pallas kernels, unpack_and_multiply(): pl.pallas_call(kernel, grid_spec=pltpu.PrefetchScalarGridSpec(num_scalar_...  21.9 us
    all_to_all x2, starting transfers between devices, exchange(): lax.all_to_all(send, ('dp', 'expert'), split_axis=0, concat_axis=0, tiled...  19.1 us
    all_to_all x1, starting transfers between devices, per_device(): lax.all_to_all(w_send, 'expert', split_axis=0, concat_axis=0, tiled=True)  12.3 us
    pallas_call x2, Pallas kernels, pack_rows(): pl.pallas_call(kernel, grid=(blocks,), in_specs=[pl.BlockSpec((2, rows),...  11.9 us
    dot_general x4, matrix products, contract_rows(): lax.dot_general(left, right, (((0,), (0,)), ((), ())), preferred_element_...  9.29 us
  transfers between devices with their start and end apart: 27, of which 14 were waited for; matrix products, arithmetic and copies ran while one was open for 4% of the time, Pallas kernels for 5%

profile of v2, /device:TPU:1, one launch (start us, length us, event | category | flops | bytes accessed | tf_op | source)
XLA Modules:
  0.0 435.5 jit_solution(17605219075616234182)
XLA Ops:
  10.7 3.7 pack_weights.1
  14.4 12.3 %all-to-all-start.1 = ((bf16[32,32,1408]{2,1,0:T(8,128)(2,1)}), bf16[32,32,1408]{2,1,0:T(8,128)(2,1)}, u32[]{:S(2)}, u32[]{:S(2)}) async-start(bf16[32,32,1408]{2,1,0:T(8,128)(2,1)} %pack_weights.1), calls=%async_computation.1 | async-start | bytes 5767168 | tf_op jit(solution)/shard_map/all_to_all | solution.py:263
  26.7 6.0 %pack_rows.2.refs_1_ = bf16[8,32,72,128]{3,2,1,0:T(8,128)(2,1)} custom-call(s32[2,128]{1,0:T(2,128)S(1)} %bitcast.27, f32[2,128]{1,0:T(2,128)S(1)} %bitcast.29, bf16[128,8192]{1,0:T(8,128)(2,1)S(1)} %copy-done), custom_call_target="tpu_custom_call" | custom-call | flops 1073741824 | bytes 6815744 | tf_op jit(solution)/shard_map/pack_rows/pallas_call | solution.py:59
  32.7 5.9 %pack_rows.3.refs_0_ = bf16[8,32,72,128]{3,2,1,0:T(8,128)(2,1)} custom-call(s32[2,128]{1,0:T(2,128)S(1)} %bitcast.28, f32[2,128]{1,0:T(2,128)S(1)} %bitcast.30, bf16[128,8192]{1,0:T(8,128)(2,1)S(1)} %copy-done.1), custom_call_target="tpu_custom_call" | custom-call | flops 1073741824 | bytes 6815744 | tf_op jit(solution)/shard_map/pack_rows/pallas_call | solution.py:59
  38.6 53.3 %all-to-all-done.1 = bf16[32,32,1408]{2,1,0:T(8,128)(2,1)} async-done(((bf16[32,32,1408]{2,1,0:T(8,128)(2,1)}), bf16[32,32,1408]{2,1,0:T(8,128)(2,1)}, u32[]{:S(2)}, u32[]{:S(2)}) %all-to-all-start.1) | async-done | bytes 2883616 | tf_op jit(solution)/shard_map/all_to_all | solution.py:263
  91.9 12.3 %all-to-all-start.2 = ((bf16[256,72,128]{2,1,0:T(8,128)(2,1)}), bf16[256,72,128]{2,1,0:T(8,128)(2,1)}, u32[]{:S(2)}, u32[]{:S(2)}) async-start(bf16[256,72,128]{2,1,0:T(8,128)(2,1)} %bitcast.34), calls=%async_computation.2 | async-start | bytes 9437184 | tf_op jit(solution)/shard_map/all_to_all | solution.py:246
  106.0 107.4 %all-to-all-done.2.received_ref = bf16[256,72,128]{2,1,0:T(8,128)(2,1)} async-done(((bf16[256,72,128]{2,1,0:T(8,128)(2,1)}), bf16[256,72,128]{2,1,0:T(8,128)(2,1)}, u32[]{:S(2)}, u32[]{:S(2)}) %all-to-all-start.2) | async-done | bytes 4718624 | tf_op jit(solution)/shard_map/all_to_all | solution.py:246
  213.3 11.9 %unpack_and_multiply.4 = (bf16[2,4,2,144,1024]{4,3,2,1,0:T(8,128)(2,1)}, f32[4,2,2,144,896]{4,3,2,1,0:T(8,128)}) custom-call(s32[2]{0:T(128)S(1)} %pad_add_fusion.place_ref, bf16[256,72,128]{2,1,0:T(8,128)(2,1)} %all-to-all-done.2.received_ref, bf16[1024,896]{1,0:T(8,128)(2,1)S(1)} %slice.57.weight_ref), custom_call_target="tpu_custom_call" | custom-call | flops 4227858432 | bytes 19529728 | tf_op jit(solution)/shard_map/unpack_and_multiply/pallas_call | solution.py:154
  225.3 6.8 %all-to-all-start = ((bf16[256,72,128]{2,1,0:T(8,128)(2,1)}), bf16[256,72,128]{2,1,0:T(8,128)(2,1)}, u32[]{:S(2)}, u32[]{:S(2)}) async-start(bf16[256,72,128]{2,1,0:T(8,128)(2,1)} %bitcast.33), calls=%async_computation | async-start | bytes 9437184 | tf_op jit(solution)/shard_map/all_to_all | solution.py:246
  233.4 108.0 %all-to-all-done.received_ref.refs_0_ = bf16[256,72,128]{2,1,0:T(8,128)(2,1)} async-done(((bf16[256,72,128]{2,1,0:T(8,128)(2,1)}), bf16[256,72,128]{2,1,0:T(8,128)(2,1)}, u32[]{:S(2)}, u32[]{:S(2)}) %all-to-all-start) | async-done | bytes 4718624 | tf_op jit(solution)/shard_map/all_to_all | solution.py:246
  341.4 5.4 %unpack_and_multiply.3 = (bf16[1,4,2,144,1024]{4,3,2,1,0:T(8,128)(2,1)S(1)}, f32[4,144,448]{2,1,0:T(8,128)S(1)}, f32[4,144,448]{2,1,0:T(8,128)}) custom-call(s32[2]{0:T(128)S(1)} %pad_add_fusion.place_ref, bf16[256,72,128]{2,1,0:T(8,128)(2,1)} %all-to-all-done.received_ref.refs_0_, bf16[1024,448]{1,0:T(8,128)(2,1)S(1)} %slice.56.weight_ref), custom_call_target="tpu_custom_call" | custom-call | flops 1056964608 | bytes 7700480 | tf_op jit(solution)/shard_map/unpack_and_multiply/pallas_call | solution.py:154
  348.4 2.7 multiply_multiply_fusion
  351.1 4.6 %unpack_and_multiply.5 = (bf16[1,4,2,144,1024]{4,3,2,1,0:T(8,128)(2,1)S(1)}, f32[4,144,448]{2,1,0:T(8,128)S(1)}, f32[4,144,448]{2,1,0:T(8,128)S(1)}) custom-call(s32[2]{0:T(128)S(1)} %pad_add_fusion.place_ref, bf16[256,72,128]{2,1,0:T(8,128)(2,1)} %follow.3.received_ref, bf16[1024,448]{1,0:T(8,128)(2,1)S(1)} %slice.56.weight_ref), custom_call_target="tpu_custom_call" | custom-call | flops 1056964608 | bytes 7700480 | tf_op jit(solution)/shard_map/unpack_and_multiply/pallas_call | solution.py:154
  360.1 2.2 collective-permute-start.12
  364.5 5.1 %collective-permute-done.3 = bf16[144,448]{1,0:T(8,128)(2,1)S(1)} collective-permute-done((bf16[144,448]{1,0:T(8,128)(2,1)S(1)}, bf16[144,448]{1,0:T(8,128)(2,1)S(1)}, u32[]{:S(2)}, u32[]{:S(2)}) %collective-permute-start.3) | collective-permute-done | bytes 129056 | tf_op jit(solution)/shard_map/ppermute | solution.py:236
  370.8 4.2 collective-permute-done.14
  378.4 2.9 fusion.5
  383.3 9.6 %collective-permute-done.5 = bf16[144,896]{1,0:T(8,128)(2,1)S(1)} collective-permute-done((bf16[144,896]{1,0:T(8,128)(2,1)S(1)}, bf16[144,896]{1,0:T(8,128)(2,1)S(1)}, u32[]{:S(2)}, u32[]{:S(2)}) %collective-permute-start.5) | collective-permute-done | bytes 258080 | tf_op jit(solution)/shard_map/ppermute | solution.py:236
  393.0 5.9 %collective-permute-done.7 = bf16[144,896]{1,0:T(8,128)(2,1)S(1)} collective-permute-done((bf16[144,896]{1,0:T(8,128)(2,1)S(1)}, bf16[144,896]{1,0:T(8,128)(2,1)S(1)}, u32[]{:S(2)}, u32[]{:S(2)}) %collective-permute-start.7) | collective-permute-done | bytes 258080 | tf_op jit(solution)/shard_map/ppermute | solution.py:236
  400.3 10.9 %collective-permute-done.16 = bf16[144,896]{1,0:T(8,128)(2,1)S(1)} collective-permute-done((bf16[144,896]{1,0:T(8,128)(2,1)S(1)}, bf16[144,896]{1,0:T(8,128)(2,1)S(1)}, u32[]{:S(2)}, u32[]{:S(2)}) %collective-permute-start.16) | collective-permute-done | bytes 258080 | tf_op jit(solution)/shard_map/ppermute | solution.py:236
  414.4 2.6 fusion.7
  417.1 2.6 convolution_add_fusion
  419.7 2.3 slice_bitcast_fusion
  426.0 2.6 convolution_add_fusion.1
  (96 shorter events, 30.1 us)
Async XLA Ops:
  14.4 77.4 %all-to-all-start.1 = ((bf16[32,32,1408]{2,1,0:T(8,128)(2,1)}), bf16[32,32,1408]{2,1,0:T(8,128)(2,1)}, u32[]{:S(2)}, u32[]{:S(2)}) async-start(bf16[32,32,1408]{2,1,0:T(8,128)(2,1)} %pack_weights.1), calls=%async_computation.1 | async-start | bytes 5767168 | tf_op jit(solution)/shard_map/all_to_all | solution.py:263
  91.9 121.5 %all-to-all-start.2 = ((bf16[256,72,128]{2,1,0:T(8,128)(2,1)}), bf16[256,72,128]{2,1,0:T(8,128)(2,1)}, u32[]{:S(2)}, u32[]{:S(2)}) async-start(bf16[256,72,128]{2,1,0:T(8,128)(2,1)} %bitcast.34), calls=%async_computation.2 | async-start | bytes 9437184 | tf_op jit(solution)/shard_map/all_to_all | solution.py:246
  104.2 244.3 %reduce-scatter.2.cloned.1.call-start = ((), (), s32[]{:S(2)}) async-start(), calls=%async_computation.4 | async-start | bytes 9289728 | tf_op jit(solution)/shard_map/reduce_scatter | solution.py:272
  225.3 116.1 %all-to-all-start = ((bf16[256,72,128]{2,1,0:T(8,128)(2,1)}), bf16[256,72,128]{2,1,0:T(8,128)(2,1)}, u32[]{:S(2)}, u32[]{:S(2)}) async-start(bf16[256,72,128]{2,1,0:T(8,128)(2,1)} %bitcast.33), calls=%async_computation | async-start | bytes 9437184 | tf_op jit(solution)/shard_map/all_to_all | solution.py:246
  232.1 189.9 %all-gather.2.cloned.1.call-start = ((), (), s32[]{:S(2)}) async-start(), calls=%async_computation.5 | async-start | bytes 2654208 | tf_op jit(solution)/shard_map/all_gather | solution.py:278
  348.2 9.2 %collective-permute-start = (f32[4,144,448]{2,1,0:T(8,128)}, f32[4,144,448]{2,1,0:T(8,128)S(1)}, u32[]{:S(2)}, u32[]{:S(2)}) collective-permute-start(f32[4,144,448]{2,1,0:T(8,128)} %get-tuple-element.20), channel_id=1, source_target_pairs={{0,32},{32,0},{64,96},{96,64},{128,160},{160,128},{192,224},{224,1... | collective-permute-start | bytes 3096584 | tf_op jit(solution)/shard_map/ppermute | solution.py:239
  357.1 2.8 collective-permute-start.11
  357.5 5.4 %collective-permute-start.1 = (bf16[144,448]{1,0:T(8,128)(2,1)S(1)}, bf16[144,448]{1,0:T(8,128)(2,1)S(1)}, u32[]{:S(2)}, u32[]{:S(2)}) collective-permute-start(bf16[144,448]{1,0:T(8,128)(2,1)S(1)} %get-tuple-element.22), channel_id=1, source_target_pairs={{0,192},{32,224},{64,0},{96,32},{128,64},{160,96},{192,128},{224,1... | collective-permute-start | bytes 387080 | tf_op jit(solution)/shard_map/ppermute | solution.py:236
  358.3 6.2 %collective-permute-start.2 = (bf16[144,448]{1,0:T(8,128)(2,1)S(1)}, bf16[144,448]{1,0:T(8,128)(2,1)S(1)}, u32[]{:S(2)}, u32[]{:S(2)}) collective-permute-start(bf16[144,448]{1,0:T(8,128)(2,1)S(1)} %get-tuple-element.23), channel_id=1, source_target_pairs={{0,128},{32,160},{64,192},{96,224},{128,0},{160,32},{192,64},{224,... | collective-permute-start | bytes 387080 | tf_op jit(solution)/shard_map/ppermute | solution.py:236
  359.4 10.2 %collective-permute-start.3 = (bf16[144,448]{1,0:T(8,128)(2,1)S(1)}, bf16[144,448]{1,0:T(8,128)(2,1)S(1)}, u32[]{:S(2)}, u32[]{:S(2)}) collective-permute-start(bf16[144,448]{1,0:T(8,128)(2,1)S(1)} %get-tuple-element.24), channel_id=1, source_target_pairs={{0,64},{32,96},{64,128},{96,160},{128,192},{160,224},{192,0},{224,... | collective-permute-start | bytes 387080 | tf_op jit(solution)/shard_map/ppermute | solution.py:236
  360.1 9.6 %collective-permute-start.12 = (bf16[144,448]{1,0:T(8,128)(2,1)S(1)}, bf16[144,448]{1,0:T(8,128)(2,1)S(1)}, u32[]{:S(2)}, u32[]{:S(2)}) collective-permute-start(bf16[144,448]{1,0:T(8,128)(2,1)S(1)} %get-tuple-element.30), channel_id=1, source_target_pairs={{0,192},{32,224},{64,0},{96,32},{128,64},{160,96},{192,128},{224,1... | collective-permute-start | bytes 387080 | tf_op jit(solution)/shard_map/ppermute | solution.py:236
  362.3 8.5 %collective-permute-start.13 = (bf16[144,448]{1,0:T(8,128)(2,1)S(1)}, bf16[144,448]{1,0:T(8,128)(2,1)S(1)}, u32[]{:S(2)}, u32[]{:S(2)}) collective-permute-start(bf16[144,448]{1,0:T(8,128)(2,1)S(1)} %get-tuple-element.31), channel_id=1, source_target_pairs={{0,128},{32,160},{64,192},{96,224},{128,0},{160,32},{192,64},{224,... | collective-permute-start | bytes 387080 | tf_op jit(solution)/shard_map/ppermute | solution.py:236
  363.0 12.0 %collective-permute-start.14 = (bf16[144,448]{1,0:T(8,128)(2,1)S(1)}, bf16[144,448]{1,0:T(8,128)(2,1)S(1)}, u32[]{:S(2)}, u32[]{:S(2)}) collective-permute-start(bf16[144,448]{1,0:T(8,128)(2,1)S(1)} %get-tuple-element.32), channel_id=1, source_target_pairs={{0,64},{32,96},{64,128},{96,160},{128,192},{160,224},{192,0},{224,... | collective-permute-start | bytes 387080 | tf_op jit(solution)/shard_map/ppermute | solution.py:236
  375.4 7.7 %collective-permute-start.4 = (bf16[144,896]{1,0:T(8,128)(2,1)S(1)}, bf16[144,896]{1,0:T(8,128)(2,1)S(1)}, u32[]{:S(2)}, u32[]{:S(2)}) collective-permute-start(bf16[144,896]{1,0:T(8,128)(2,1)S(1)} %get-tuple-element.36), channel_id=1, source_target_pairs={{0,32},{32,0},{64,96},{96,64},{128,160},{160,128},{192,224},{224,1... | collective-permute-start | bytes 774152 | tf_op jit(solution)/shard_map/ppermute | solution.py:239
  376.1 16.9 %collective-permute-start.5 = (bf16[144,896]{1,0:T(8,128)(2,1)S(1)}, bf16[144,896]{1,0:T(8,128)(2,1)S(1)}, u32[]{:S(2)}, u32[]{:S(2)}) collective-permute-start(bf16[144,896]{1,0:T(8,128)(2,1)S(1)} %get-tuple-element.36), channel_id=1, source_target_pairs={{0,64},{32,96},{64,128},{96,160},{128,192},{160,224},{192,0},{224,... | collective-permute-start | bytes 774152 | tf_op jit(solution)/shard_map/ppermute | solution.py:236
  376.1 22.7 %collective-permute-start.7 = (bf16[144,896]{1,0:T(8,128)(2,1)S(1)}, bf16[144,896]{1,0:T(8,128)(2,1)S(1)}, u32[]{:S(2)}, u32[]{:S(2)}) collective-permute-start(bf16[144,896]{1,0:T(8,128)(2,1)S(1)} %get-tuple-element.36), channel_id=1, source_target_pairs={{0,128},{32,160},{64,192},{96,224},{128,0},{160,32},{192,64},{224,... | collective-permute-start | bytes 774152 | tf_op jit(solution)/shard_map/ppermute | solution.py:236
  377.7 21.2 %collective-permute-start.15 = (bf16[144,896]{1,0:T(8,128)(2,1)S(1)}, bf16[144,896]{1,0:T(8,128)(2,1)S(1)}, u32[]{:S(2)}, u32[]{:S(2)}) collective-permute-start(bf16[144,896]{1,0:T(8,128)(2,1)S(1)} %get-tuple-element.38), channel_id=1, source_target_pairs={{0,32},{32,0},{64,96},{96,64},{128,160},{160,128},{192,224},{224,1... | collective-permute-start | bytes 774152 | tf_op jit(solution)/shard_map/ppermute | solution.py:239
  381.3 30.4 %collective-permute-start.9 = (bf16[144,896]{1,0:T(8,128)(2,1)S(1)}, bf16[144,896]{1,0:T(8,128)(2,1)S(1)}, u32[]{:S(2)}, u32[]{:S(2)}) collective-permute-start(bf16[144,896]{1,0:T(8,128)(2,1)S(1)} %get-tuple-element.36), channel_id=1, source_target_pairs={{0,192},{32,224},{64,0},{96,32},{128,64},{160,96},{192,128},{224,1... | collective-permute-start | bytes 774152 | tf_op jit(solution)/shard_map/ppermute | solution.py:236
  383.1 28.1 %collective-permute-start.16 = (bf16[144,896]{1,0:T(8,128)(2,1)S(1)}, bf16[144,896]{1,0:T(8,128)(2,1)S(1)}, u32[]{:S(2)}, u32[]{:S(2)}) collective-permute-start(bf16[144,896]{1,0:T(8,128)(2,1)S(1)} %get-tuple-element.38), channel_id=1, source_target_pairs={{0,64},{32,96},{64,128},{96,160},{128,192},{160,224},{192,0},{224,... | collective-permute-start | bytes 774152 | tf_op jit(solution)/shard_map/ppermute | solution.py:236
  393.0 18.9 %collective-permute-start.18 = (bf16[144,896]{1,0:T(8,128)(2,1)S(1)}, bf16[144,896]{1,0:T(8,128)(2,1)S(1)}, u32[]{:S(2)}, u32[]{:S(2)}) collective-permute-start(bf16[144,896]{1,0:T(8,128)(2,1)S(1)} %get-tuple-element.38), channel_id=1, source_target_pairs={{0,128},{32,160},{64,192},{96,224},{128,0},{160,32},{192,64},{224,... | collective-permute-start | bytes 774152 | tf_op jit(solution)/shard_map/ppermute | solution.py:236
  398.8 13.5 %collective-permute-start.20 = (bf16[144,896]{1,0:T(8,128)(2,1)S(1)}, bf16[144,896]{1,0:T(8,128)(2,1)S(1)}, u32[]{:S(2)}, u32[]{:S(2)}) collective-permute-start(bf16[144,896]{1,0:T(8,128)(2,1)S(1)} %get-tuple-element.38), channel_id=1, source_target_pairs={{0,192},{32,224},{64,0},{96,32},{128,64},{160,96},{192,128},{224,1... | collective-permute-start | bytes 774152 | tf_op jit(solution)/shard_map/ppermute | solution.py:236
  398.8 13.6 %collective-permute-start.6 = (bf16[144,896]{1,0:T(8,128)(2,1)S(1)}, bf16[144,896]{1,0:T(8,128)(2,1)S(1)}, u32[]{:S(2)}, u32[]{:S(2)}) collective-permute-start(bf16[144,896]{1,0:T(8,128)(2,1)S(1)} %collective-permute-done.5), channel_id=1, source_target_pairs={{0,32},{32,0},{64,96},{96,64},{128,160},{160,128},{192,224},{224,1... | collective-permute-start | bytes 774152 | tf_op jit(solution)/shard_map/ppermute | solution.py:239
  411.8 2.3 collective-permute-start.10
  412.4 2.0 collective-permute-start.21
  (16 other events, 93.3 us)
Sparse Core Ops, SparseCore 0:
  225.4 86.5 reduce-scatter.1
  363.9 41.9 all-gather.1

commit v3 on v2

--- a/solution.py
+++ b/solution.py
@@ -7,7 +7,7 @@
 
 F32 = jnp.float32
 BF16 = jnp.bfloat16
-VMEM_LIMIT = 48 * 1024 * 1024
+VMEM_LIMIT = 20 * 1024 * 1024
 ANYWHERE = pl.BlockSpec(memory_space=pl.ANY)
 
 
@@ -67,7 +67,7 @@
         out_specs=pl.BlockSpec((1, owners, 9 * tiles, 128), lambda i: (i, 0, 0, 0)),
         out_shape=jax.ShapeDtypeStruct((blocks, owners, 9 * tiles, 128), BF16),
         scratch_shapes=[pltpu.VMEM((2 * main, rows), BF16), pltpu.VMEM((2 * main, 1), F32)],
-        compiler_params=pltpu.CompilerParams(vmem_limit_bytes=VMEM_LIMIT),
+        compiler_params=pltpu.CompilerParams(vmem_limit_bytes=3 * VMEM_LIMIT),
         cost_estimate=pl.CostEstimate(
             flops=4 * main * rows * width, bytes_accessed=2 * width * (rows + 9 * owners), transcendentals=0
         ),
@@ -94,7 +94,7 @@
         in_specs=[spec, spec, spec],
         out_specs=pl.BlockSpec((many, depth, full), lambda i: (i, 0, 0)),
         out_shape=jax.ShapeDtypeStruct((owners, depth, full), BF16),
-        compiler_params=pltpu.CompilerParams(vmem_limit_bytes=VMEM_LIMIT),
+        compiler_params=pltpu.CompilerParams(vmem_limit_bytes=3 * VMEM_LIMIT),
         cost_estimate=pl.CostEstimate(
             flops=0, bytes_accessed=2 * depth * (3 * total + owners * full), transcendentals=0
         ),
@@ -102,7 +102,7 @@
     )(gate, up, down)
 
 
-def unpack_and_multiply(place, received, weight, chips, first, parts, split):
+def unpack_and_multiply(place, received, weight, chips, first, parts):
     senders, height, _ = received.shape
     tiles = height // 9
     depth, columns = weight.shape
@@ -110,8 +110,7 @@
     main = group * 8
     half = group * 9 // 2
 
-    def kernel(place_ref, received_ref, weight_ref, rows_ref, *refs):
-        product_refs, work_ref = refs[:-1], refs[-1]
+    def kernel(place_ref, received_ref, weight_ref, rows_ref, keep_ref, send_ref, work_ref):
         core = place_ref[1]
         row, col = iota((main, main), 0), iota((main, main), 1)
         turn = one_if(
@@ -127,30 +126,16 @@
             work_ref[main:, 128 * j : 128 * (j + 1)] = ninth[group * j : group * (j + 1)]
         product = jnp.dot(work_ref[...], weight_ref[...], preferred_element_type=F32)
         low, high = product[:half], product[half:]
-        if split:
-            product_refs[0][0] = jnp.where(core == 0, low, high)
-            product_refs[1][0] = jnp.where(core == 0, high, low)
-            rows_ref[0, 0, 0] = work_ref[:half]
-            rows_ref[0, 0, 1] = work_ref[half:]
-        else:
-            product_refs[0][0, 0, 0] = low
-            product_refs[0][0, 1, 0] = high
-            rows_ref[0, 0, core] = work_ref[:half]
-            rows_ref[0, 0, 1 - core] = work_ref[half:]
+        keep_ref[0, 0] = jnp.where(core == 0, low, high)
+        send_ref[0, 0] = jnp.where(core == 0, high, low)
+        rows_ref[0, 0, core] = work_ref[:half]
+        rows_ref[0, 0, 1 - core] = work_ref[half:]
 
     def slot(i, place_ref):
         return (place_ref[0] + chips - i % chips) % chips
 
-    if split:
-        rows_map = lambda i, s: (i // chips, i % chips, 0, 0, 0)
-        product_specs = [pl.BlockSpec((1, half, columns), lambda i, s: (slot(i, s), 0, 0))] * 2
-        product_shapes = [jax.ShapeDtypeStruct((chips, half, columns), F32)] * 2
-    else:
-        rows_map = lambda i, s: (i // chips, slot(i, s), 0, 0, 0)
-        product_specs = [
-            pl.BlockSpec((1, 2, 1, half, columns), lambda i, s: (i % chips, 0, i // chips, 0, 0))
-        ]
-        product_shapes = [jax.ShapeDtypeStruct((chips, 2, parts, half, columns), F32)]
+    product_spec = pl.BlockSpec((1, 1, half, columns), lambda i, s: (slot(i, s), i // chips, 0, 0))
+    product_shape = jax.ShapeDtypeStruct((chips, parts, half, columns), F32)
     return pl.pallas_call(
         kernel,
         grid_spec=pltpu.PrefetchScalarGridSpec(
@@ -160,10 +145,18 @@
                 pl.BlockSpec((group, height, 128), lambda i, s: (first * chips + i, 0, 0)),
                 pl.BlockSpec((depth, columns), lambda i, s: (0, 0)),
             ],
-            out_specs=[pl.BlockSpec((1, 1, 2, half, depth), rows_map)] + product_specs,
+            out_specs=[
+                pl.BlockSpec((1, 1, 2, half, depth), lambda i, s: (i // chips, slot(i, s), 0, 0, 0)),
+                product_spec,
+                product_spec,
+            ],
             scratch_shapes=[pltpu.VMEM((2 * half, depth), BF16)],
         ),
-        out_shape=[jax.ShapeDtypeStruct((parts, chips, 2, half, depth), BF16)] + product_shapes,
+        out_shape=[
+            jax.ShapeDtypeStruct((parts, chips, 2, half, depth), BF16),
+            product_shape,
+            product_shape,
+        ],
         compiler_params=pltpu.CompilerParams(vmem_limit_bytes=VMEM_LIMIT),
         cost_estimate=pl.CostEstimate(
             flops=4 * parts * chips * half * depth * columns,
@@ -197,6 +190,34 @@
     )(one, two)
 
 
+def slopes(total, active, slope, part):
+    own, others = total[0], total[1:]
+    rows, columns = own.shape
+
+    def kernel(own_ref, *refs):
+        active_ref, slope_ref, out_ref = refs[len(others) :]
+        back = own_ref[...]
+        for ref in refs[: len(others)]:
+            back = back + ref[...].astype(F32)
+        out_ref[:, :columns] = (back * slope_ref[...]).astype(BF16)
+        out_ref[:, columns:] = (back * active_ref[...]).astype(BF16)
+
+    whole = pl.BlockSpec((rows, columns), lambda i: (0, 0))
+    mine = pl.BlockSpec((rows, columns), lambda i: (part, 0))
+    return pl.pallas_call(
+        kernel,
+        grid=(1,),
+        in_specs=[whole] * len(total) + [mine] * 2,
+        out_specs=pl.BlockSpec((rows, 2 * columns), lambda i: (0, 0)),
+        out_shape=jax.ShapeDtypeStruct((rows, 2 * columns), BF16),
+        compiler_params=pltpu.CompilerParams(vmem_limit_bytes=VMEM_LIMIT),
+        cost_estimate=pl.CostEstimate(
+            flops=6 * own.size, bytes_accessed=24 * own.size, transcendentals=0
+        ),
+        name="slopes",
+    )(own, *others, active, slope)
+
+
 def follow(values, earlier):
     count = len(values)
 
@@ -213,8 +234,52 @@
     )(*values, *earlier)
 
 
-def contract_rows(left, right):
-    return lax.dot_general(left, right, (((0,), (0,)), ((), ())), preferred_element_type=F32)
+def contract_rows(pieces, rows):
+    parts, chips, cores, half, depth = rows.shape
+    columns = pieces[0].shape[1]
+    outs = 1 + columns // 896
+    hidden = columns // outs
+    count = len(pieces)
+    height = parts * count * half
+    wide = 256
+
+    def kernel(*refs):
+        piece_refs, rows_ref = refs[:count], refs[count]
+        out_refs, done_ref = refs[count + 1 : -3], refs[-3]
+        left_ref, turned_ref = refs[-2:]
+        done_ref[...] = jnp.zeros_like(done_ref)
+
+        @pl.when(pl.program_id(0) == 0)
+        def _():
+            for p in range(parts):
+                for n in range(count):
+                    to = (p * count + n) * half
+                    left_ref[to : to + half] = piece_refs[n][p * half : (p + 1) * half]
+            turned_ref[...] = left_ref[...].T
+
+        right = rows_ref[...].reshape(height, wide)
+        product = jnp.dot(turned_ref[...], right, preferred_element_type=F32)
+        for n in range(outs):
+            out_refs[n][...] = product[n * hidden : (n + 1) * hidden]
+
+    return pl.pallas_call(
+        kernel,
+        grid=(depth // wide,),
+        in_specs=[pl.BlockSpec(piece.shape, lambda i: (0, 0)) for piece in pieces]
+        + [pl.BlockSpec(rows.shape[:4] + (wide,), lambda i: (0, 0, 0, 0, i))],
+        out_specs=[pl.BlockSpec((hidden, wide), lambda i: (0, i))] * outs
+        + [pl.BlockSpec((8, 128), lambda i: (0, 0))],
+        out_shape=[jax.ShapeDtypeStruct((hidden, depth), F32)] * outs
+        + [jax.ShapeDtypeStruct((8, 128), F32)],
+        scratch_shapes=[pltpu.VMEM((height, columns), BF16), pltpu.VMEM((columns, height), BF16)],
+        compiler_params=pltpu.CompilerParams(vmem_limit_bytes=3 * VMEM_LIMIT),
+        cost_estimate=pl.CostEstimate(
+            flops=2 * height * depth * columns,
+            bytes_accessed=2 * height * (depth + columns) + 4 * columns * depth,
+            transcendentals=0,
+        ),
+        name="contract_rows",
+    )(*pieces, rows)
 
 
 def flat(value):
@@ -246,18 +311,18 @@
         return lax.all_to_all(send, ("dp", "expert"), split_axis=0, concat_axis=0, tiled=True)
 
     def reduce_rows(keep, send):
+        keep, send = (value.reshape(chips, -1, value.shape[-1]) for value in (keep, send))
         sums = add_steps(keep, other_core(send), BF16)
-        total = sums[0]
-        for step in range(1, chips):
-            total = total + along_x(-step, sums[step]).astype(F32)
-        return total
-
-    def gather_rows(value):
+        return [sums[0]] + [along_x(-step, sums[step]) for step in range(1, chips)]
+
+    def gather_rows(value, after=()):
         pieces = []
         for step in range(chips):
             piece = along_x(step, value)
+            if after and step == chips - 1:
+                (piece,) = follow([piece], after)
             pieces += [piece, other_core(piece)]
-        return jnp.concatenate(pieces, axis=0)
+        return pieces
 
     w_send = pack_weights(gate_dense, up_dense, down_dense, owners)
     w_all = flat(lax.all_to_all(w_send, "expert", split_axis=0, concat_axis=0, tiled=True))
@@ -268,31 +333,20 @@
     x_received = exchange(x_send)
     dy_received = exchange(dy_send)
 
-    x_rows, pair = unpack_and_multiply(place, x_received, w_pair, chips, 0, 2, False)
-    pair = lax.psum_scatter(flat(pair), "dp", scatter_dimension=0, tiled=True)
+    x_rows, keep, send = unpack_and_multiply(place, x_received, w_pair, chips, 0, 2)
+    pair = sum(total.astype(F32) for total in reduce_rows(keep, send))
     gate_vals, up_vals = pair[:, :hidden], pair[:, hidden:]
     sigma = jax.nn.sigmoid(gate_vals)
     active = gate_vals * sigma
     slope = up_vals * (sigma * (1.0 + gate_vals * (1.0 - sigma)))
-    hidden_mine = (active * up_vals).astype(BF16)
-    hidden_all = lax.all_gather(hidden_mine, "dp", axis=0, tiled=True)
-    hidden_all = hidden_all.reshape(blocks, 2, -1, hidden)
-
-    half = pair.shape[0] // 2
-    grads = None
-    for n in range(2):
-        if n == 1:
-            (dy_received,) = follow([dy_received], [hidden_mine])
-        dy_rows, keep, send = unpack_and_multiply(place, dy_received, w_down, chips, n, 1, True)
-        back = reduce_rows(keep, send)
-        mine = slice(n * half, (n + 1) * half)
-        d_pair = jnp.concatenate(
-            [(back * slope[mine]).astype(BF16), (back * active[mine]).astype(BF16)], axis=1
-        )
-        grad_down = contract_rows(flat(hidden_all[:, n]), flat(dy_rows))
-        grad_pair = contract_rows(gather_rows(d_pair), flat(x_rows[n]))
-        grads = (grad_pair, grad_down) if grads is None else (grads[0] + grad_pair, grads[1] + grad_down)
-    return (grads[0][:hidden].T, grads[0][hidden:].T, grads[1].T)
+    hidden_all = gather_rows((active * up_vals).astype(BF16))
+    (dy_received,) = follow([dy_received], hidden_all)
+
+    dy_rows, keep, send = unpack_and_multiply(place, dy_received, w_down, chips, 0, 2)
+    d_pair = slopes(reduce_rows(keep, send), active, slope, 0)
+    grad_down, down_done = contract_rows(hidden_all, dy_rows)
+    grad_gate, grad_up, _ = contract_rows(gather_rows(d_pair, [down_done]), x_rows)
+    return (grad_gate.T, grad_up.T, grad_down.T)
 
 
 def solution(mesh):

time: 436 us -> 393 us (0.901)
  waiting for transfers between devices: 308 us -> 163 us
  blocking collectives: 0 us -> 121 us
  Pallas kernels: 37.7 us -> 56.2 us
  between operations: 14.4 us -> 0.9 us
  local copies, waits for them, and re-layouts: 17.5 us -> 7.55 us
  matrix products: 9.29 us -> 0 us
    all_to_all x2 -> x1, waiting for transfers between devices: 215 us -> 13.3 us  [exchange(): lax.all_to_all(send, ('dp', 'expert'), split_axis=0, concat_axis=0, tiled...]
    all_to_all x0 -> x1, blocking collectives: none -> 121 us  [exchange(): lax.all_to_all(send, ('dp', 'expert'), split_axis=0, concat_axis=0, tiled...]
    ppermute x12, waiting for transfers between devices: 37.7 us -> 88.3 us  [along_x(): return lax.ppermute(value, 'dp', pairs)]
    pallas_call x0 -> x3, Pallas kernels: none -> 17.1 us  [the longest x2 16.8 us: contract_rows(): pl.pallas_call(kernel, grid=(depth // wide,), in_specs=[pl.BlockSpec(piec...]
    all_to_all x2 -> x1, starting transfers between devices: 19.1 us -> 6.79 us  [exchange(): lax.all_to_all(send, ('dp', 'expert'), split_axis=0, concat_axis=0, tiled...]
    ppermute x10, waiting for transfers between devices: 1.81 us -> 12.5 us  [other_core(): return lax.ppermute(value, 'dp', [(i, i ^ 1) for i in range(blocks)])]
    ppermute x10, starting transfers between devices: 4.85 us -> 15.2 us  [other_core(): return lax.ppermute(value, 'dp', [(i, i ^ 1) for i in range(blocks)])]
    dot_general x4 -> x0, matrix products: 9.29 us -> none  [contract_rows(): lax.dot_general(left, right, (((0,), (0,)), ((), ())), preferred_element_...]
  transfers between devices with their start and end apart: 27 -> 24, of which waited for: 14 -> 15; matrix products, arithmetic and copies ran while one was open for 4% -> 1% of each run, Pallas kernels for 5% -> 8%
where the time goes in v3:
time: 393 us; the launch traced here: 392 us
  waiting for transfers between devices  163 us (41%)
  blocking collectives  121 us (31%)
  Pallas kernels  56.2 us (14%)
  starting transfers between devices  41.6 us (11%)
  local copies, waits for them, and re-layouts  7.55 us (2%)
    all_to_all x1, blocking collectives, exchange(): lax.all_to_all(send, ('dp', 'expert'), split_axis=0, concat_axis=0, tiled...  121 us
    ppermute x12, waiting for transfers between devices, along_x(): return lax.ppermute(value, 'dp', pairs)  88.3 us
    all_to_all x1, waiting for transfers between devices, per_device(): lax.all_to_all(w_send, 'expert', split_axis=0, concat_axis=0, tiled=True)  49.2 us
    pallas_call x2, Pallas kernels, contract_rows(): pl.pallas_call(kernel, grid=(depth // wide,), in_specs=[pl.BlockSpec(piec...  16.8 us
    pallas_call x2, Pallas kernels, pack_rows(): pl.pallas_call(kernel, grid=(blocks,), in_specs=[pl.BlockSpec((2, rows),...  16 us
    pallas_call x2, Pallas kernels, unpack_and_multiply(): pl.pallas_call(kernel, grid_spec=pltpu.PrefetchScalarGridSpec(num_scalar_...  15.8 us
    ppermute x10, starting transfers between devices, other_core(): return lax.ppermute(value, 'dp', [(i, i ^ 1) for i in range(blocks)])  15.2 us
    all_to_all x1, waiting for transfers between devices, exchange(): lax.all_to_all(send, ('dp', 'expert'), split_axis=0, concat_axis=0, tiled...  13.3 us
  transfers between devices with their start and end apart: 24, of which 15 were waited for; matrix products, arithmetic and copies ran while one was open for 1% of the time, Pallas kernels for 8%

profile of v3, /device:TPU:1, one launch (start us, length us, event | category | flops | bytes accessed | tf_op | source)
XLA Modules:
  0.0 391.7 jit_solution(10397368505766753929)
XLA Ops:
  0.6 6.5 %pack_weights.1 = bf16[32,32,1408]{2,1,0:T(8,128)(2,1)} custom-call(bf16[32,14336]{1,0:T(8,128)(2,1)} %gate_ref.1, bf16[32,14336]{1,0:T(8,128)(2,1)} %up_ref.1, bf16[32,14336]{1,0:T(8,128)(2,1)} %down_ref.1), custom_call_target="tpu_custom_call" | custom-call | bytes 5636096 | tf_op jit(solution)/shard_map/pack_weights/pallas_call | solution.py:91
  7.1 12.0 %all-to-all-start.2 = ((bf16[32,32,1408]{2,1,0:T(8,128)(2,1)}), bf16[32,32,1408]{2,1,0:T(8,128)(2,1)S(1)}, u32[]{:S(2)}, u32[]{:S(2)}) async-start(bf16[32,32,1408]{2,1,0:T(8,128)(2,1)} %pack_weights.1), calls=%async_computation.2 | async-start | bytes 5767168 | tf_op jit(solution)/shard_map/all_to_all | solution.py:328
  19.2 8.0 %pack_rows.2.refs_1_ = bf16[8,32,72,128]{3,2,1,0:T(8,128)(2,1)} custom-call(s32[2,128]{1,0:T(2,128)} %bitcast.22, f32[2,128]{1,0:T(2,128)} %bitcast.24, bf16[128,8192]{1,0:T(8,128)(2,1)} %source_ref.2), custom_call_target="tpu_custom_call" | custom-call | flops 1073741824 | bytes 6815744 | tf_op jit(solution)/shard_map/pack_rows/pallas_call | solution.py:59
  27.2 8.0 %pack_rows.3.refs_0_ = bf16[8,32,72,128]{3,2,1,0:T(8,128)(2,1)} custom-call(s32[2,128]{1,0:T(2,128)} %bitcast.23, f32[2,128]{1,0:T(2,128)} %bitcast.25, bf16[128,8192]{1,0:T(8,128)(2,1)} %source_ref.3), custom_call_target="tpu_custom_call" | custom-call | flops 1073741824 | bytes 6815744 | tf_op jit(solution)/shard_map/pack_rows/pallas_call | solution.py:59
  35.2 49.2 %all-to-all-done.2 = bf16[32,32,1408]{2,1,0:T(8,128)(2,1)S(1)} async-done(((bf16[32,32,1408]{2,1,0:T(8,128)(2,1)}), bf16[32,32,1408]{2,1,0:T(8,128)(2,1)S(1)}, u32[]{:S(2)}, u32[]{:S(2)}) %all-to-all-start.2) | async-done | bytes 2883616 | tf_op jit(solution)/shard_map/all_to_all | solution.py:328
  84.3 121.5 %all_to_all.15.received_ref = bf16[256,72,128]{2,1,0:T(8,128)(2,1)} all-to-all(bf16[256,72,128]{2,1,0:T(8,128)(2,1)} %bitcast.19), channel_id=1, replica_groups=mesh['dp'=8,'expert'=32] {'dp','expert'}, dimensions={0} | all-to-all | bytes 9437184 | tf_op jit(solution)/shard_map/all_to_all | solution.py:311
  205.8 6.8 %all-to-all-start = ((bf16[256,72,128]{2,1,0:T(8,128)(2,1)}), bf16[256,72,128]{2,1,0:T(8,128)(2,1)}, u32[]{:S(2)}, u32[]{:S(2)}) async-start(bf16[256,72,128]{2,1,0:T(8,128)(2,1)} %bitcast.18), calls=%async_computation | async-start | bytes 9437184 | tf_op jit(solution)/shard_map/all_to_all | solution.py:311
  215.2 7.8 %unpack_and_multiply.2 = (bf16[2,4,2,144,1024]{4,3,2,1,0:T(8,128)(2,1)S(1)}, f32[4,2,144,896]{3,2,1,0:T(8,128)S(1)}, f32[4,2,144,896]{3,2,1,0:T(8,128)S(1)}) custom-call(s32[2]{0:T(128)S(1)} %pad_add_fusion.place_ref, bf16[256,72,128]{2,1,0:T(8,128)(2,1)S(1)} %copy-done, bf16[1024,896]{1,0:T(8,128)(2,1)S(1)} %slice.16.weight_ref), custom_call_target="tpu_custom_call" | custom-call | flops 4227858432 | bytes 19529728 | tf_op jit(solution)/shard_map/unpack_and_multiply/pallas_call | solution.py:139
  225.1 2.3 collective-permute-start
  227.5 6.7 %collective-permute-done.two_ref = f32[4,288,896]{2,1,0:T(8,128)S(1)} collective-permute-done((f32[4,288,896]{2,1,0:T(8,128)S(1)}, f32[4,288,896]{2,1,0:T(8,128)S(1)}, u32[]{:S(2)}, u32[]{:S(2)}) %collective-permute-start) | collective-permute-done | bytes 4128800 | tf_op jit(solution)/shard_map/ppermute | solution.py:304
  236.7 20.5 %collective-permute-done.1 = bf16[288,896]{1,0:T(8,128)(2,1)S(1)} collective-permute-done((bf16[288,896]{1,0:T(8,128)(2,1)S(1)}, bf16[288,896]{1,0:T(8,128)(2,1)S(1)}, u32[]{:S(2)}, u32[]{:S(2)}) %collective-permute-start.1) | collective-permute-done | bytes 516128 | tf_op jit(solution)/shard_map/ppermute | solution.py:301
  258.4 20.5 %collective-permute-done.3 = bf16[288,896]{1,0:T(8,128)(2,1)S(1)} collective-permute-done((bf16[288,896]{1,0:T(8,128)(2,1)S(1)}, bf16[288,896]{1,0:T(8,128)(2,1)S(1)}, u32[]{:S(2)}, u32[]{:S(2)}) %collective-permute-start.3) | collective-permute-done | bytes 516128 | tf_op jit(solution)/shard_map/ppermute | solution.py:301
  282.1 10.1 %collective-permute-done.9.refs_7_.refs_6_ = bf16[288,448]{1,0:T(8,128)(2,1)S(1)} collective-permute-done((bf16[288,448]{1,0:T(8,128)(2,1)S(1)}, bf16[288,448]{1,0:T(8,128)(2,1)S(1)}, u32[]{:S(2)}, u32[]{:S(2)}) %collective-permute-start.9) | collective-permute-done | bytes 258080 | tf_op jit(solution)/shard_map/ppermute | solution.py:301
  292.2 3.0 collective-permute-start.10
  295.1 2.5 collective-permute-start.8
  297.6 9.3 %collective-permute-done.5.refs_3_.refs_2_ = bf16[288,448]{1,0:T(8,128)(2,1)S(1)} collective-permute-done((bf16[288,448]{1,0:T(8,128)(2,1)S(1)}, bf16[288,448]{1,0:T(8,128)(2,1)S(1)}, u32[]{:S(2)}, u32[]{:S(2)}) %collective-permute-start.5) | collective-permute-done | bytes 258080 | tf_op jit(solution)/shard_map/ppermute | solution.py:301
  308.6 13.3 %all-to-all-done.refs_0_ = bf16[256,72,128]{2,1,0:T(8,128)(2,1)} async-done(((bf16[256,72,128]{2,1,0:T(8,128)(2,1)}), bf16[256,72,128]{2,1,0:T(8,128)(2,1)}, u32[]{:S(2)}, u32[]{:S(2)}) %all-to-all-start) | async-done | bytes 4718624 | tf_op jit(solution)/shard_map/all_to_all | solution.py:311
  322.0 8.0 %unpack_and_multiply.3 = (bf16[2,4,2,144,1024]{4,3,2,1,0:T(8,128)(2,1)S(1)}, f32[4,2,144,448]{3,2,1,0:T(8,128)S(1)}, f32[4,2,144,448]{3,2,1,0:T(8,128)S(1)}) custom-call(s32[2]{0:T(128)S(1)} %pad_add_fusion.place_ref, bf16[256,72,128]{2,1,0:T(8,128)(2,1)} %follow.4.received_ref, bf16[1024,448]{1,0:T(8,128)(2,1)S(1)} %slice.19.weight_ref), custom_call_target="tpu_custom_call" | custom-call | flops 2113929216 | bytes 14483456 | tf_op jit(solution)/shard_map/unpack_and_multiply/pallas_call | solution.py:139
  330.4 4.3 %collective-permute-done.11.two_ref = f32[4,288,448]{2,1,0:T(8,128)S(1)} collective-permute-done((f32[4,288,448]{2,1,0:T(8,128)S(1)}, f32[4,288,448]{2,1,0:T(8,128)S(1)}, u32[]{:S(2)}, u32[]{:S(2)}) %collective-permute-start.11) | collective-permute-done | bytes 2064416 | tf_op jit(solution)/shard_map/ppermute | solution.py:304
  336.9 6.4 %collective-permute-done.12.refs_0_ = bf16[288,448]{1,0:T(8,128)(2,1)S(1)} collective-permute-done((bf16[288,448]{1,0:T(8,128)(2,1)S(1)}, bf16[288,448]{1,0:T(8,128)(2,1)S(1)}, u32[]{:S(2)}, u32[]{:S(2)}) %collective-permute-start.12) | collective-permute-done | bytes 258080 | tf_op jit(solution)/shard_map/ppermute | solution.py:301
  345.1 7.3 %collective-permute-done.14.refs_2_ = bf16[288,448]{1,0:T(8,128)(2,1)S(1)} collective-permute-done((bf16[288,448]{1,0:T(8,128)(2,1)S(1)}, bf16[288,448]{1,0:T(8,128)(2,1)S(1)}, u32[]{:S(2)}, u32[]{:S(2)}) %collective-permute-start.14) | collective-permute-done | bytes 258080 | tf_op jit(solution)/shard_map/ppermute | solution.py:301
  354.9 7.1 %contract_rows.2 = (f32[448,1024]{1,0:T(8,128)}, f32[8,128]{1,0:T(8,128)}) custom-call(bf16[288,448]{1,0:T(8,128)(2,1)} %copy-done.5, bf16[288,448]{1,0:T(8,128)(2,1)} %collective-permute-done.4.refs_2_.refs_1_, bf16[288,448]{1,0:T(8,128)(2,1)} %copy-done.9, bf16[288,448]{1,0:T(8,128)(2,1)} %collective-permute-done.6.refs_4_.refs_3_, ...), custom_call_target="tpu_custom_call" | custom-call | flops 2113929216 | bytes 8617984 | tf_op jit(solution)/shard_map/contract_rows/pallas_call | solution.py:265
  370.1 9.0 %collective-permute-done.16.refs_2_ = bf16[288,896]{1,0:T(8,128)(2,1)S(1)} collective-permute-done((bf16[288,896]{1,0:T(8,128)(2,1)S(1)}, bf16[288,896]{1,0:T(8,128)(2,1)S(1)}, u32[]{:S(2)}, u32[]{:S(2)}) %collective-permute-start.16) | collective-permute-done | bytes 516128 | tf_op jit(solution)/shard_map/ppermute | solution.py:301
  382.0 9.7 %contract_rows.3 = (f32[448,1024]{1,0:T(8,128)}, f32[448,1024]{1,0:T(8,128)}, f32[8,128]{1,0:T(8,128)}) custom-call(bf16[288,896]{1,0:T(8,128)(2,1)} %copy-done.1, bf16[288,896]{1,0:T(8,128)(2,1)} %copy-done.12, bf16[288,896]{1,0:T(8,128)(2,1)} %copy-done.11, bf16[288,896]{1,0:T(8,128)(2,1)} %copy-done.15, bf16[288,896]{1,0:T(8,128)(2,1)} %copy-done.10, ...), custom_call_target="tpu_custom_call" | custom-call | flops 4227858432 | bytes 12517376 | tf_op jit(solution)/shard_map/contract_rows/pallas_call | solution.py:265
  (75 shorter events, 31.1 us)
Async XLA Ops:
  7.1 77.2 %all-to-all-start.2 = ((bf16[32,32,1408]{2,1,0:T(8,128)(2,1)}), bf16[32,32,1408]{2,1,0:T(8,128)(2,1)S(1)}, u32[]{:S(2)}, u32[]{:S(2)}) async-start(bf16[32,32,1408]{2,1,0:T(8,128)(2,1)} %pack_weights.1), calls=%async_computation.2 | async-start | bytes 5767168 | tf_op jit(solution)/shard_map/all_to_all | solution.py:328
  205.8 116.1 %all-to-all-start = ((bf16[256,72,128]{2,1,0:T(8,128)(2,1)}), bf16[256,72,128]{2,1,0:T(8,128)(2,1)}, u32[]{:S(2)}, u32[]{:S(2)}) async-start(bf16[256,72,128]{2,1,0:T(8,128)(2,1)} %bitcast.18), calls=%async_computation | async-start | bytes 9437184 | tf_op jit(solution)/shard_map/all_to_all | solution.py:311
  225.1 9.0 %collective-permute-start = (f32[4,288,896]{2,1,0:T(8,128)S(1)}, f32[4,288,896]{2,1,0:T(8,128)S(1)}, u32[]{:S(2)}, u32[]{:S(2)}) collective-permute-start(f32[4,288,896]{2,1,0:T(8,128)S(1)} %bitcast.16), channel_id=1, source_target_pairs={{0,32},{32,0},{64,96},{96,64},{128,160},{160,128},{192,224},{224,1... | collective-permute-start | bytes 12386312 | tf_op jit(solution)/shard_map/ppermute | solution.py:304
  234.8 22.4 %collective-permute-start.1 = (bf16[288,896]{1,0:T(8,128)(2,1)S(1)}, bf16[288,896]{1,0:T(8,128)(2,1)S(1)}, u32[]{:S(2)}, u32[]{:S(2)}) collective-permute-start(bf16[288,896]{1,0:T(8,128)(2,1)S(1)} %get-tuple-element.24), channel_id=1, source_target_pairs={{0,192},{32,224},{64,0},{96,32},{128,64},{160,96},{192,128},{224,1... | collective-permute-start | bytes 1548296 | tf_op jit(solution)/shard_map/ppermute | solution.py:301
  235.6 22.8 %collective-permute-start.2 = (bf16[288,896]{1,0:T(8,128)(2,1)S(1)}, bf16[288,896]{1,0:T(8,128)(2,1)S(1)}, u32[]{:S(2)}, u32[]{:S(2)}) collective-permute-start(bf16[288,896]{1,0:T(8,128)(2,1)S(1)} %get-tuple-element.25), channel_id=1, source_target_pairs={{0,128},{32,160},{64,192},{96,224},{128,0},{160,32},{192,64},{224,... | collective-permute-start | bytes 1548296 | tf_op jit(solution)/shard_map/ppermute | solution.py:301
  236.1 42.7 %collective-permute-start.3 = (bf16[288,896]{1,0:T(8,128)(2,1)S(1)}, bf16[288,896]{1,0:T(8,128)(2,1)S(1)}, u32[]{:S(2)}, u32[]{:S(2)}) collective-permute-start(bf16[288,896]{1,0:T(8,128)(2,1)S(1)} %get-tuple-element.26), channel_id=1, source_target_pairs={{0,64},{32,96},{64,128},{96,160},{128,192},{160,224},{192,0},{224,... | collective-permute-start | bytes 1548296 | tf_op jit(solution)/shard_map/ppermute | solution.py:301
  279.5 12.7 %collective-permute-start.9 = (bf16[288,448]{1,0:T(8,128)(2,1)S(1)}, bf16[288,448]{1,0:T(8,128)(2,1)S(1)}, u32[]{:S(2)}, u32[]{:S(2)}) collective-permute-start(bf16[288,448]{1,0:T(8,128)(2,1)S(1)} %get-tuple-element.40.refs_1_.refs_0_), channel_id=1, source_target_pairs={{0,192},{32,224},{64,0},{96,32},{128,64},{160,96},{192,128},{224,1... | collective-permute-start | bytes 774152 | tf_op jit(solution)/shard_map/ppermute | solution.py:301
  279.5 15.6 %collective-permute-start.7 = (bf16[288,448]{1,0:T(8,128)(2,1)S(1)}, bf16[288,448]{1,0:T(8,128)(2,1)S(1)}, u32[]{:S(2)}, u32[]{:S(2)}) collective-permute-start(bf16[288,448]{1,0:T(8,128)(2,1)S(1)} %get-tuple-element.40.refs_1_.refs_0_), channel_id=1, source_target_pairs={{0,128},{32,160},{64,192},{96,224},{128,0},{160,32},{192,64},{224,... | collective-permute-start | bytes 774152 | tf_op jit(solution)/shard_map/ppermute | solution.py:301
  280.2 26.7 %collective-permute-start.5 = (bf16[288,448]{1,0:T(8,128)(2,1)S(1)}, bf16[288,448]{1,0:T(8,128)(2,1)S(1)}, u32[]{:S(2)}, u32[]{:S(2)}) collective-permute-start(bf16[288,448]{1,0:T(8,128)(2,1)S(1)} %get-tuple-element.40.refs_1_.refs_0_), channel_id=1, source_target_pairs={{0,64},{32,96},{64,128},{96,160},{128,192},{160,224},{192,0},{224,... | collective-permute-start | bytes 774152 | tf_op jit(solution)/shard_map/ppermute | solution.py:301
  281.0 40.9 %collective-permute-start.4 = (bf16[288,448]{1,0:T(8,128)(2,1)S(1)}, bf16[288,448]{1,0:T(8,128)(2,1)}, u32[]{:S(2)}, u32[]{:S(2)}) collective-permute-start(bf16[288,448]{1,0:T(8,128)(2,1)S(1)} %get-tuple-element.40.refs_1_.refs_0_), channel_id=1, source_target_pairs={{0,32},{32,0},{64,96},{96,64},{128,160},{160,128},{192,224},{224,1... | collective-permute-start | bytes 774152 | tf_op jit(solution)/shard_map/ppermute | solution.py:304
  292.2 29.8 %collective-permute-start.10 = (bf16[288,448]{1,0:T(8,128)(2,1)S(1)}, bf16[288,448]{1,0:T(8,128)(2,1)}, u32[]{:S(2)}, u32[]{:S(2)}) collective-permute-start(bf16[288,448]{1,0:T(8,128)(2,1)S(1)} %collective-permute-done.9.refs_7_.refs_6_), channel_id=1, source_target_pairs={{0,32},{32,0},{64,96},{96,64},{128,160},{160,128},{192,224},{224,1... | collective-permute-start | bytes 774152 | tf_op jit(solution)/shard_map/ppermute | solution.py:304
  295.1 26.8 %collective-permute-start.8 = (bf16[288,448]{1,0:T(8,128)(2,1)S(1)}, bf16[288,448]{1,0:T(8,128)(2,1)}, u32[]{:S(2)}, u32[]{:S(2)}) collective-permute-start(bf16[288,448]{1,0:T(8,128)(2,1)S(1)} %collective-permute-done.7.refs_5_.refs_4_), channel_id=1, source_target_pairs={{0,32},{32,0},{64,96},{96,64},{128,160},{160,128},{192,224},{224,1... | collective-permute-start | bytes 774152 | tf_op jit(solution)/shard_map/ppermute | solution.py:304
  306.9 15.0 %collective-permute-start.6 = (bf16[288,448]{1,0:T(8,128)(2,1)S(1)}, bf16[288,448]{1,0:T(8,128)(2,1)}, u32[]{:S(2)}, u32[]{:S(2)}) collective-permute-start(bf16[288,448]{1,0:T(8,128)(2,1)S(1)} %collective-permute-done.5.refs_3_.refs_2_), channel_id=1, source_target_pairs={{0,32},{32,0},{64,96},{96,64},{128,160},{160,128},{192,224},{224,1... | collective-permute-start | bytes 774152 | tf_op jit(solution)/shard_map/ppermute | solution.py:304
  330.0 4.6 %collective-permute-start.11 = (f32[4,288,448]{2,1,0:T(8,128)S(1)}, f32[4,288,448]{2,1,0:T(8,128)S(1)}, u32[]{:S(2)}, u32[]{:S(2)}) collective-permute-start(f32[4,288,448]{2,1,0:T(8,128)S(1)} %bitcast.17), channel_id=1, source_target_pairs={{0,32},{32,0},{64,96},{96,64},{128,160},{160,128},{192,224},{224,1... | collective-permute-start | bytes 6193160 | tf_op jit(solution)/shard_map/ppermute | solution.py:304
  334.9 8.4 %collective-permute-start.12 = (bf16[288,448]{1,0:T(8,128)(2,1)S(1)}, bf16[288,448]{1,0:T(8,128)(2,1)S(1)}, u32[]{:S(2)}, u32[]{:S(2)}) collective-permute-start(bf16[288,448]{1,0:T(8,128)(2,1)S(1)} %get-tuple-element.30), channel_id=1, source_target_pairs={{0,192},{32,224},{64,0},{96,32},{128,64},{160,96},{192,128},{224,1... | collective-permute-start | bytes 774152 | tf_op jit(solution)/shard_map/ppermute | solution.py:301
  335.7 9.4 %collective-permute-start.13 = (bf16[288,448]{1,0:T(8,128)(2,1)S(1)}, bf16[288,448]{1,0:T(8,128)(2,1)S(1)}, u32[]{:S(2)}, u32[]{:S(2)}) collective-permute-start(bf16[288,448]{1,0:T(8,128)(2,1)S(1)} %get-tuple-element.31), channel_id=1, source_target_pairs={{0,128},{32,160},{64,192},{96,224},{128,0},{160,32},{192,64},{224,... | collective-permute-start | bytes 774152 | tf_op jit(solution)/shard_map/ppermute | solution.py:301
  336.9 15.5 %collective-permute-start.14 = (bf16[288,448]{1,0:T(8,128)(2,1)S(1)}, bf16[288,448]{1,0:T(8,128)(2,1)S(1)}, u32[]{:S(2)}, u32[]{:S(2)}) collective-permute-start(bf16[288,448]{1,0:T(8,128)(2,1)S(1)} %get-tuple-element.32), channel_id=1, source_target_pairs={{0,64},{32,96},{64,128},{96,160},{128,192},{160,224},{192,0},{224,... | collective-permute-start | bytes 774152 | tf_op jit(solution)/shard_map/ppermute | solution.py:301
  352.7 12.9 %collective-permute-start.20 = (bf16[288,896]{1,0:T(8,128)(2,1)S(1)}, bf16[288,896]{1,0:T(8,128)(2,1)S(1)}, u32[]{:S(2)}, u32[]{:S(2)}) collective-permute-start(bf16[288,896]{1,0:T(8,128)(2,1)S(1)} %slopes.1.refs_0_), channel_id=1, source_target_pairs={{0,192},{32,224},{64,0},{96,32},{128,64},{160,96},{192,128},{224,1... | collective-permute-start | bytes 1548296 | tf_op jit(solution)/shard_map/ppermute | solution.py:301
  352.8 15.9 %collective-permute-start.18 = (bf16[288,896]{1,0:T(8,128)(2,1)S(1)}, bf16[288,896]{1,0:T(8,128)(2,1)S(1)}, u32[]{:S(2)}, u32[]{:S(2)}) collective-permute-start(bf16[288,896]{1,0:T(8,128)(2,1)S(1)} %slopes.1.refs_0_), channel_id=1, source_target_pairs={{0,128},{32,160},{64,192},{96,224},{128,0},{160,32},{192,64},{224,... | collective-permute-start | bytes 1548296 | tf_op jit(solution)/shard_map/ppermute | solution.py:301
  354.1 25.0 %collective-permute-start.16 = (bf16[288,896]{1,0:T(8,128)(2,1)S(1)}, bf16[288,896]{1,0:T(8,128)(2,1)S(1)}, u32[]{:S(2)}, u32[]{:S(2)}) collective-permute-start(bf16[288,896]{1,0:T(8,128)(2,1)S(1)} %slopes.1.refs_0_), channel_id=1, source_target_pairs={{0,64},{32,96},{64,128},{96,160},{128,192},{160,224},{192,0},{224,... | collective-permute-start | bytes 1548296 | tf_op jit(solution)/shard_map/ppermute | solution.py:301
  362.0 17.7 %collective-permute-start.15 = (bf16[288,896]{1,0:T(8,128)(2,1)S(1)}, bf16[288,896]{1,0:T(8,128)(2,1)S(1)}, u32[]{:S(2)}, u32[]{:S(2)}) collective-permute-start(bf16[288,896]{1,0:T(8,128)(2,1)S(1)} %slopes.1.refs_0_), channel_id=1, source_target_pairs={{0,32},{32,0},{64,96},{96,64},{128,160},{160,128},{192,224},{224,1... | collective-permute-start | bytes 1548296 | tf_op jit(solution)/shard_map/ppermute | solution.py:304
  366.5 13.2 %collective-permute-start.21 = (bf16[288,896]{1,0:T(8,128)(2,1)}, bf16[288,896]{1,0:T(8,128)(2,1)S(1)}, u32[]{:S(2)}, u32[]{:S(2)}) collective-permute-start(bf16[288,896]{1,0:T(8,128)(2,1)} %follow.5.refs_6_), channel_id=1, source_target_pairs={{0,32},{32,0},{64,96},{96,64},{128,160},{160,128},{192,224},{224,1... | collective-permute-start | bytes 1548296 | tf_op jit(solution)/shard_map/ppermute | solution.py:304
  368.7 10.9 %collective-permute-start.19 = (bf16[288,896]{1,0:T(8,128)(2,1)S(1)}, bf16[288,896]{1,0:T(8,128)(2,1)S(1)}, u32[]{:S(2)}, u32[]{:S(2)}) collective-permute-start(bf16[288,896]{1,0:T(8,128)(2,1)S(1)} %collective-permute-done.18.refs_4_), channel_id=1, source_target_pairs={{0,32},{32,0},{64,96},{96,64},{128,160},{160,128},{192,224},{224,1... | collective-permute-start | bytes 1548296 | tf_op jit(solution)/shard_map/ppermute | solution.py:304
  379.1 2.0 collective-permute-start.17
  (16 other events, 304.3 us)

commit v4 on v3

--- a/solution.py
+++ b/solution.py
@@ -234,41 +234,44 @@
     )(*values, *earlier)
 
 
-def contract_rows(pieces, rows):
-    parts, chips, cores, half, depth = rows.shape
+def contract_rows(pieces, plan, rows, slots, sums=()):
+    parts, _, cores, half, depth = rows.shape
     columns = pieces[0].shape[1]
     outs = 1 + columns // 896
     hidden = columns // outs
-    count = len(pieces)
-    height = parts * count * half
+    count, many = len(pieces), len(slots)
+    height = len(plan) * half
     wide = 256
 
     def kernel(*refs):
-        piece_refs, rows_ref = refs[:count], refs[count]
-        out_refs, done_ref = refs[count + 1 : -3], refs[-3]
-        left_ref, turned_ref = refs[-2:]
+        piece_refs, rows_refs = refs[:count], refs[count : count + many]
+        sum_refs, out_refs = refs[count + many : -3 - outs], refs[-3 - outs : -3]
+        done_ref, left_ref, turned_ref = refs[-3:]
         done_ref[...] = jnp.zeros_like(done_ref)
 
         @pl.when(pl.program_id(0) == 0)
         def _():
-            for p in range(parts):
-                for n in range(count):
-                    to = (p * count + n) * half
-                    left_ref[to : to + half] = piece_refs[n][p * half : (p + 1) * half]
+            for n, (piece, first) in enumerate(plan):
+                left_ref[n * half : (n + 1) * half] = piece_refs[piece][first : first + half]
             turned_ref[...] = left_ref[...].T
 
-        right = rows_ref[...].reshape(height, wide)
+        right = jnp.concatenate([ref[...].reshape(height // many, wide) for ref in rows_refs], axis=0)
         product = jnp.dot(turned_ref[...], right, preferred_element_type=F32)
         for n in range(outs):
-            out_refs[n][...] = product[n * hidden : (n + 1) * hidden]
-
+            share = product[n * hidden : (n + 1) * hidden]
+            out_refs[n][...] = share + sum_refs[n][...] if sums else share
+
+    def rows_spec(slot):
+        return pl.BlockSpec((parts, 1, cores, half, wide), lambda i: (0, slot, 0, 0, i))
+
+    tile = pl.BlockSpec((hidden, wide), lambda i: (0, i))
     return pl.pallas_call(
         kernel,
         grid=(depth // wide,),
         in_specs=[pl.BlockSpec(piece.shape, lambda i: (0, 0)) for piece in pieces]
-        + [pl.BlockSpec(rows.shape[:4] + (wide,), lambda i: (0, 0, 0, 0, i))],
-        out_specs=[pl.BlockSpec((hidden, wide), lambda i: (0, i))] * outs
-        + [pl.BlockSpec((8, 128), lambda i: (0, 0))],
+        + [rows_spec(slot) for slot in slots]
+        + [tile] * len(sums),
+        out_specs=[tile] * outs + [pl.BlockSpec((8, 128), lambda i: (0, 0))],
         out_shape=[jax.ShapeDtypeStruct((hidden, depth), F32)] * outs
         + [jax.ShapeDtypeStruct((8, 128), F32)],
         scratch_shapes=[pltpu.VMEM((height, columns), BF16), pltpu.VMEM((columns, height), BF16)],
@@ -279,7 +282,7 @@
             transcendentals=0,
         ),
         name="contract_rows",
-    )(*pieces, rows)
+    )(*pieces, *[rows] * many, *sums)
 
 
 def flat(value):
@@ -315,14 +318,15 @@
         sums = add_steps(keep, other_core(send), BF16)
         return [sums[0]] + [along_x(-step, sums[step]) for step in range(1, chips)]
 
-    def gather_rows(value, after=()):
+    def gather_rows(value):
         pieces = []
         for step in range(chips):
             piece = along_x(step, value)
-            if after and step == chips - 1:
-                (piece,) = follow([piece], after)
             pieces += [piece, other_core(piece)]
         return pieces
+
+    def blocks_of(count):
+        return [(2 * n + q, p * half) for n in range(count) for p in range(2) for q in range(2)]
 
     w_send = pack_weights(gate_dense, up_dense, down_dense, owners)
     w_all = flat(lax.all_to_all(w_send, "expert", split_axis=0, concat_axis=0, tiled=True))
@@ -344,8 +348,18 @@
 
     dy_rows, keep, send = unpack_and_multiply(place, dy_received, w_down, chips, 0, 2)
     d_pair = slopes(reduce_rows(keep, send), active, slope, 0)
-    grad_down, down_done = contract_rows(hidden_all, dy_rows)
-    grad_gate, grad_up, _ = contract_rows(gather_rows(d_pair, [down_done]), x_rows)
+    half = x_rows.shape[3]
+    left, right = along_x(1, d_pair), along_x(-1, d_pair)
+    grad_down, down_done = contract_rows(hidden_all, blocks_of(chips), dy_rows, range(chips))
+    left, right = follow([left, right], [down_done])
+    far = [along_x(1, left[:half]), along_x(-1, right[half:])]
+    near = []
+    for piece in (d_pair, left, right):
+        near += [piece, other_core(piece)]
+    *grad_pair, near_done = contract_rows(near, blocks_of(3), x_rows, (0, 1, 3))
+    far_left, far_right = follow(far, [near_done])
+    far = [far_left, other_core(far_left), far_right, other_core(far_right)]
+    grad_gate, grad_up, _ = contract_rows(far, [(n, 0) for n in range(4)], x_rows, (2,), grad_pair)
     return (grad_gate.T, grad_up.T, grad_down.T)
 
 

time: 393 us -> 396 us (level)
  waiting for transfers between devices: 163 us -> 156 us
  local copies, waits for them, and re-layouts: 7.55 us -> 13.4 us
  Pallas kernels: 56.2 us -> 61.1 us
    ppermute x12 -> x13, waiting for transfers between devices: 88.3 us -> 80.7 us  [along_x(): return lax.ppermute(value, 'dp', pairs)]
    pallas_call x2 -> x3, Pallas kernels: 16.8 us -> 21.6 us  [contract_rows(): pl.pallas_call(kernel, grid=(depth // wide,), in_specs=[pl.BlockSpec(piec...]
    unnamed x32 -> x36, local copies, waits for them, and re-layouts: 6.11 us -> 10 us
    ppermute x10 -> x11, starting transfers between devices: 15.2 us -> 13.8 us  [other_core(): return lax.ppermute(value, 'dp', [(i, i ^ 1) for i in range(blocks)])]
    ppermute x12 -> x13, starting transfers between devices: 7.59 us -> 8.53 us  [along_x(): return lax.ppermute(value, 'dp', pairs)]
    ppermute x10 -> x11, waiting for transfers between devices: 12.5 us -> 12.7 us  [other_core(): return lax.ppermute(value, 'dp', [(i, i ^ 1) for i in range(blocks)])]
  transfers between devices with their start and end apart: 24 -> 26, of which waited for: 15 -> 16; matrix products, arithmetic and copies ran while one was open for 1% -> 1% of each run, Pallas kernels for 8% -> 10%
where the time goes in v4:
time: 396 us; the launch traced here: 395 us
  waiting for transfers between devices  156 us (39%)
  blocking collectives  121 us (31%)
  Pallas kernels  61.1 us (15%)
  starting transfers between devices  41.2 us (10%)
  local copies, waits for them, and re-layouts  13.4 us (3%)
    all_to_all x1, blocking collectives, exchange(): lax.all_to_all(send, ('dp', 'expert'), split_axis=0, concat_axis=0, tiled...  121 us
    ppermute x13, waiting for transfers between devices, along_x(): return lax.ppermute(value, 'dp', pairs)  80.7 us
    all_to_all x1, waiting for transfers between devices, per_device(): lax.all_to_all(w_send, 'expert', split_axis=0, concat_axis=0, tiled=True)  49.1 us
    pallas_call x3, Pallas kernels, contract_rows(): pl.pallas_call(kernel, grid=(depth // wide,), in_specs=[pl.BlockSpec(piec...  21.6 us
    pallas_call x2, Pallas kernels, pack_rows(): pl.pallas_call(kernel, grid=(blocks,), in_specs=[pl.BlockSpec((2, rows),...  16 us
    pallas_call x2, Pallas kernels, unpack_and_multiply(): pl.pallas_call(kernel, grid_spec=pltpu.PrefetchScalarGridSpec(num_scalar_...  15.8 us
    ppermute x11, starting transfers between devices, other_core(): return lax.ppermute(value, 'dp', [(i, i ^ 1) for i in range(blocks)])  13.8 us
    all_to_all x1, waiting for transfers between devices, exchange(): lax.all_to_all(send, ('dp', 'expert'), split_axis=0, concat_axis=0, tiled...  13.3 us
  transfers between devices with their start and end apart: 26, of which 16 were waited for; matrix products, arithmetic and copies ran while one was open for 1% of the time, Pallas kernels for 10%

profile of v4, /device:TPU:1, one launch (start us, length us, event | category | flops | bytes accessed | tf_op | source)
XLA Modules:
  0.0 394.6 jit_solution(17541701790542763547)
XLA Ops:
  0.6 6.5 %pack_weights.1 = bf16[32,32,1408]{2,1,0:T(8,128)(2,1)} custom-call(bf16[32,14336]{1,0:T(8,128)(2,1)} %gate_ref.1, bf16[32,14336]{1,0:T(8,128)(2,1)} %up_ref.1, bf16[32,14336]{1,0:T(8,128)(2,1)} %down_ref.1), custom_call_target="tpu_custom_call" | custom-call | bytes 5636096 | tf_op jit(solution)/shard_map/pack_weights/pallas_call | solution.py:91
  7.1 12.0 %all-to-all-start.2 = ((bf16[32,32,1408]{2,1,0:T(8,128)(2,1)}), bf16[32,32,1408]{2,1,0:T(8,128)(2,1)S(1)}, u32[]{:S(2)}, u32[]{:S(2)}) async-start(bf16[32,32,1408]{2,1,0:T(8,128)(2,1)} %pack_weights.1), calls=%async_computation.2 | async-start | bytes 5767168 | tf_op jit(solution)/shard_map/all_to_all | solution.py:332
  19.2 8.0 %pack_rows.2.refs_1_ = bf16[8,32,72,128]{3,2,1,0:T(8,128)(2,1)} custom-call(s32[2,128]{1,0:T(2,128)} %bitcast.22, f32[2,128]{1,0:T(2,128)} %bitcast.24, bf16[128,8192]{1,0:T(8,128)(2,1)} %source_ref.2), custom_call_target="tpu_custom_call" | custom-call | flops 1073741824 | bytes 6815744 | tf_op jit(solution)/shard_map/pack_rows/pallas_call | solution.py:59
  27.2 8.0 %pack_rows.3.refs_0_ = bf16[8,32,72,128]{3,2,1,0:T(8,128)(2,1)} custom-call(s32[2,128]{1,0:T(2,128)} %bitcast.23, f32[2,128]{1,0:T(2,128)} %bitcast.25, bf16[128,8192]{1,0:T(8,128)(2,1)} %source_ref.3), custom_call_target="tpu_custom_call" | custom-call | flops 1073741824 | bytes 6815744 | tf_op jit(solution)/shard_map/pack_rows/pallas_call | solution.py:59
  35.2 49.1 %all-to-all-done.2 = bf16[32,32,1408]{2,1,0:T(8,128)(2,1)S(1)} async-done(((bf16[32,32,1408]{2,1,0:T(8,128)(2,1)}), bf16[32,32,1408]{2,1,0:T(8,128)(2,1)S(1)}, u32[]{:S(2)}, u32[]{:S(2)}) %all-to-all-start.2) | async-done | bytes 2883616 | tf_op jit(solution)/shard_map/all_to_all | solution.py:332
  84.3 121.5 %all_to_all.15.received_ref = bf16[256,72,128]{2,1,0:T(8,128)(2,1)} all-to-all(bf16[256,72,128]{2,1,0:T(8,128)(2,1)} %bitcast.19), channel_id=1, replica_groups=mesh['dp'=8,'expert'=32] {'dp','expert'}, dimensions={0} | all-to-all | bytes 9437184 | tf_op jit(solution)/shard_map/all_to_all | solution.py:314
  205.8 6.8 %all-to-all-start = ((bf16[256,72,128]{2,1,0:T(8,128)(2,1)}), bf16[256,72,128]{2,1,0:T(8,128)(2,1)}, u32[]{:S(2)}, u32[]{:S(2)}) async-start(bf16[256,72,128]{2,1,0:T(8,128)(2,1)} %bitcast.18), calls=%async_computation | async-start | bytes 9437184 | tf_op jit(solution)/shard_map/all_to_all | solution.py:314
  215.2 7.8 %unpack_and_multiply.2 = (bf16[2,4,2,144,1024]{4,3,2,1,0:T(8,128)(2,1)S(1)}, f32[4,2,144,896]{3,2,1,0:T(8,128)S(1)}, f32[4,2,144,896]{3,2,1,0:T(8,128)S(1)}) custom-call(s32[2]{0:T(128)S(1)} %pad_add_fusion.place_ref, bf16[256,72,128]{2,1,0:T(8,128)(2,1)S(1)} %copy-done.2, bf16[1024,896]{1,0:T(8,128)(2,1)S(1)} %slice.24.weight_ref), custom_call_target="tpu_custom_call" | custom-call | flops 4227858432 | bytes 19529728 | tf_op jit(solution)/shard_map/unpack_and_multiply/pallas_call | solution.py:139
  227.5 6.7 %collective-permute-done.two_ref = f32[4,288,896]{2,1,0:T(8,128)S(1)} collective-permute-done((f32[4,288,896]{2,1,0:T(8,128)S(1)}, f32[4,288,896]{2,1,0:T(8,128)S(1)}, u32[]{:S(2)}, u32[]{:S(2)}) %collective-permute-start) | collective-permute-done | bytes 4128800 | tf_op jit(solution)/shard_map/ppermute | solution.py:307
  236.7 20.5 %collective-permute-done.1 = bf16[288,896]{1,0:T(8,128)(2,1)S(1)} collective-permute-done((bf16[288,896]{1,0:T(8,128)(2,1)S(1)}, bf16[288,896]{1,0:T(8,128)(2,1)S(1)}, u32[]{:S(2)}, u32[]{:S(2)}) %collective-permute-start.1) | collective-permute-done | bytes 516128 | tf_op jit(solution)/shard_map/ppermute | solution.py:304
  258.3 20.5 %collective-permute-done.3 = bf16[288,896]{1,0:T(8,128)(2,1)S(1)} collective-permute-done((bf16[288,896]{1,0:T(8,128)(2,1)S(1)}, bf16[288,896]{1,0:T(8,128)(2,1)S(1)}, u32[]{:S(2)}, u32[]{:S(2)}) %collective-permute-start.3) | collective-permute-done | bytes 516128 | tf_op jit(solution)/shard_map/ppermute | solution.py:304
  282.1 10.0 %collective-permute-done.9.refs_7_.refs_6_ = bf16[288,448]{1,0:T(8,128)(2,1)S(1)} collective-permute-done((bf16[288,448]{1,0:T(8,128)(2,1)S(1)}, bf16[288,448]{1,0:T(8,128)(2,1)S(1)}, u32[]{:S(2)}, u32[]{:S(2)}) %collective-permute-start.9) | collective-permute-done | bytes 258080 | tf_op jit(solution)/shard_map/ppermute | solution.py:304
  292.2 3.0 collective-permute-start.10
  295.1 2.6 collective-permute-start.8
  297.7 9.2 %collective-permute-done.5.refs_3_.refs_2_ = bf16[288,448]{1,0:T(8,128)(2,1)S(1)} collective-permute-done((bf16[288,448]{1,0:T(8,128)(2,1)S(1)}, bf16[288,448]{1,0:T(8,128)(2,1)S(1)}, u32[]{:S(2)}, u32[]{:S(2)}) %collective-permute-start.5) | collective-permute-done | bytes 258080 | tf_op jit(solution)/shard_map/ppermute | solution.py:304
  308.6 13.3 %all-to-all-done.refs_0_ = bf16[256,72,128]{2,1,0:T(8,128)(2,1)} async-done(((bf16[256,72,128]{2,1,0:T(8,128)(2,1)}), bf16[256,72,128]{2,1,0:T(8,128)(2,1)}, u32[]{:S(2)}, u32[]{:S(2)}) %all-to-all-start) | async-done | bytes 4718624 | tf_op jit(solution)/shard_map/all_to_all | solution.py:314
  322.0 8.0 %unpack_and_multiply.3 = (bf16[2,4,2,144,1024]{4,3,2,1,0:T(8,128)(2,1)S(1)}, f32[4,2,144,448]{3,2,1,0:T(8,128)S(1)}, f32[4,2,144,448]{3,2,1,0:T(8,128)S(1)}) custom-call(s32[2]{0:T(128)S(1)} %pad_add_fusion.place_ref, bf16[256,72,128]{2,1,0:T(8,128)(2,1)} %follow.5.received_ref, bf16[1024,448]{1,0:T(8,128)(2,1)S(1)} %slice.27.weight_ref), custom_call_target="tpu_custom_call" | custom-call | flops 2113929216 | bytes 14483456 | tf_op jit(solution)/shard_map/unpack_and_multiply/pallas_call | solution.py:139
  332.4 4.3 %collective-permute-done.11.two_ref = f32[4,288,448]{2,1,0:T(8,128)S(1)} collective-permute-done((f32[4,288,448]{2,1,0:T(8,128)S(1)}, f32[4,288,448]{2,1,0:T(8,128)S(1)}, u32[]{:S(2)}, u32[]{:S(2)}) %collective-permute-start.11) | collective-permute-done | bytes 2064416 | tf_op jit(solution)/shard_map/ppermute | solution.py:307
  339.0 6.4 %collective-permute-done.12.refs_0_ = bf16[288,448]{1,0:T(8,128)(2,1)S(1)} collective-permute-done((bf16[288,448]{1,0:T(8,128)(2,1)S(1)}, bf16[288,448]{1,0:T(8,128)(2,1)S(1)}, u32[]{:S(2)}, u32[]{:S(2)}) %collective-permute-start.12) | collective-permute-done | bytes 258080 | tf_op jit(solution)/shard_map/ppermute | solution.py:304
  347.2 7.3 %collective-permute-done.14.refs_2_ = bf16[288,448]{1,0:T(8,128)(2,1)S(1)} collective-permute-done((bf16[288,448]{1,0:T(8,128)(2,1)S(1)}, bf16[288,448]{1,0:T(8,128)(2,1)S(1)}, u32[]{:S(2)}, u32[]{:S(2)}) %collective-permute-start.14) | collective-permute-done | bytes 258080 | tf_op jit(solution)/shard_map/ppermute | solution.py:304
  356.4 7.1 %contract_rows.3 = (f32[448,1024]{1,0:T(8,128)}, f32[8,128]{1,0:T(8,128)}) custom-call(bf16[288,448]{1,0:T(8,128)(2,1)} %copy-done.7, bf16[288,448]{1,0:T(8,128)(2,1)} %collective-permute-done.4.refs_2_.refs_1_, bf16[288,448]{1,0:T(8,128)(2,1)} %copy-done.10, bf16[288,448]{1,0:T(8,128)(2,1)} %collective-permute-done.6.refs_4_.refs_3_, ...), custom_call_target="tpu_custom_call" | custom-call | flops 2113929216 | bytes 8617984 | tf_op jit(solution)/shard_map/contract_rows/pallas_call | solution.py:268
  364.6 3.1 collective-permute-done.16.refs_1_
  375.8 8.4 %contract_rows.4 = (f32[448,1024]{1,0:T(8,128)}, f32[448,1024]{1,0:T(8,128)}, f32[8,128]{1,0:T(8,128)}) custom-call(bf16[288,896]{1,0:T(8,128)(2,1)} %copy-done.3, bf16[288,896]{1,0:T(8,128)(2,1)} %copy-done.13, bf16[288,896]{1,0:T(8,128)(2,1)} %get-tuple-element.42.refs_2_, bf16[288,896]{1,0:T(8,128)(2,1)} %copy-done.14, ...), custom_call_target="tpu_custom_call" | custom-call | flops 3170893824 | bytes 10305536 | tf_op jit(solution)/shard_map/contract_rows/pallas_call | solution.py:268
  388.5 6.1 %contract_rows.5 = (f32[448,1024]{1,0:T(8,128)}, f32[448,1024]{1,0:T(8,128)}, f32[8,128]{1,0:T(8,128)}) custom-call(bf16[144,896]{1,0:T(8,128)(2,1)} %get-tuple-element.46.refs_0_, bf16[144,896]{1,0:T(8,128)(2,1)} %copy-done.16, bf16[144,896]{1,0:T(8,128)(2,1)} %get-tuple-element.47.refs_2_, bf16[144,896]{1,0:T(8,128)(2,1)} %copy-done.17, ...), custom_call_target="tpu_custom_call" | custom-call | flops 1056964608 | bytes 5881856 | tf_op jit(solution)/shard_map/contract_rows/pallas_call | solution.py:268
  (87 shorter events, 37.4 us)
Async XLA Ops:
  7.1 77.2 %all-to-all-start.2 = ((bf16[32,32,1408]{2,1,0:T(8,128)(2,1)}), bf16[32,32,1408]{2,1,0:T(8,128)(2,1)S(1)}, u32[]{:S(2)}, u32[]{:S(2)}) async-start(bf16[32,32,1408]{2,1,0:T(8,128)(2,1)} %pack_weights.1), calls=%async_computation.2 | async-start | bytes 5767168 | tf_op jit(solution)/shard_map/all_to_all | solution.py:332
  205.8 116.1 %all-to-all-start = ((bf16[256,72,128]{2,1,0:T(8,128)(2,1)}), bf16[256,72,128]{2,1,0:T(8,128)(2,1)}, u32[]{:S(2)}, u32[]{:S(2)}) async-start(bf16[256,72,128]{2,1,0:T(8,128)(2,1)} %bitcast.18), calls=%async_computation | async-start | bytes 9437184 | tf_op jit(solution)/shard_map/all_to_all | solution.py:314
  225.1 9.0 %collective-permute-start = (f32[4,288,896]{2,1,0:T(8,128)S(1)}, f32[4,288,896]{2,1,0:T(8,128)S(1)}, u32[]{:S(2)}, u32[]{:S(2)}) collective-permute-start(f32[4,288,896]{2,1,0:T(8,128)S(1)} %bitcast.16), channel_id=1, source_target_pairs={{0,32},{32,0},{64,96},{96,64},{128,160},{160,128},{192,224},{224,1... | collective-permute-start | bytes 12386312 | tf_op jit(solution)/shard_map/ppermute | solution.py:307
  234.8 22.4 %collective-permute-start.1 = (bf16[288,896]{1,0:T(8,128)(2,1)S(1)}, bf16[288,896]{1,0:T(8,128)(2,1)S(1)}, u32[]{:S(2)}, u32[]{:S(2)}) collective-permute-start(bf16[288,896]{1,0:T(8,128)(2,1)S(1)} %get-tuple-element.31), channel_id=1, source_target_pairs={{0,192},{32,224},{64,0},{96,32},{128,64},{160,96},{192,128},{224,1... | collective-permute-start | bytes 1548296 | tf_op jit(solution)/shard_map/ppermute | solution.py:304
  235.6 22.8 %collective-permute-start.2 = (bf16[288,896]{1,0:T(8,128)(2,1)S(1)}, bf16[288,896]{1,0:T(8,128)(2,1)S(1)}, u32[]{:S(2)}, u32[]{:S(2)}) collective-permute-start(bf16[288,896]{1,0:T(8,128)(2,1)S(1)} %get-tuple-element.32), channel_id=1, source_target_pairs={{0,128},{32,160},{64,192},{96,224},{128,0},{160,32},{192,64},{224,... | collective-permute-start | bytes 1548296 | tf_op jit(solution)/shard_map/ppermute | solution.py:304
  236.1 42.7 %collective-permute-start.3 = (bf16[288,896]{1,0:T(8,128)(2,1)S(1)}, bf16[288,896]{1,0:T(8,128)(2,1)S(1)}, u32[]{:S(2)}, u32[]{:S(2)}) collective-permute-start(bf16[288,896]{1,0:T(8,128)(2,1)S(1)} %get-tuple-element.33), channel_id=1, source_target_pairs={{0,64},{32,96},{64,128},{96,160},{128,192},{160,224},{192,0},{224,... | collective-permute-start | bytes 1548296 | tf_op jit(solution)/shard_map/ppermute | solution.py:304
  279.4 12.7 %collective-permute-start.9 = (bf16[288,448]{1,0:T(8,128)(2,1)S(1)}, bf16[288,448]{1,0:T(8,128)(2,1)S(1)}, u32[]{:S(2)}, u32[]{:S(2)}) collective-permute-start(bf16[288,448]{1,0:T(8,128)(2,1)S(1)} %get-tuple-element.54.refs_1_.refs_0_), channel_id=1, source_target_pairs={{0,192},{32,224},{64,0},{96,32},{128,64},{160,96},{192,128},{224,1... | collective-permute-start | bytes 774152 | tf_op jit(solution)/shard_map/ppermute | solution.py:304
  279.5 15.6 %collective-permute-start.7 = (bf16[288,448]{1,0:T(8,128)(2,1)S(1)}, bf16[288,448]{1,0:T(8,128)(2,1)S(1)}, u32[]{:S(2)}, u32[]{:S(2)}) collective-permute-start(bf16[288,448]{1,0:T(8,128)(2,1)S(1)} %get-tuple-element.54.refs_1_.refs_0_), channel_id=1, source_target_pairs={{0,128},{32,160},{64,192},{96,224},{128,0},{160,32},{192,64},{224,... | collective-permute-start | bytes 774152 | tf_op jit(solution)/shard_map/ppermute | solution.py:304
  280.2 26.7 %collective-permute-start.5 = (bf16[288,448]{1,0:T(8,128)(2,1)S(1)}, bf16[288,448]{1,0:T(8,128)(2,1)S(1)}, u32[]{:S(2)}, u32[]{:S(2)}) collective-permute-start(bf16[288,448]{1,0:T(8,128)(2,1)S(1)} %get-tuple-element.54.refs_1_.refs_0_), channel_id=1, source_target_pairs={{0,64},{32,96},{64,128},{96,160},{128,192},{160,224},{192,0},{224,... | collective-permute-start | bytes 774152 | tf_op jit(solution)/shard_map/ppermute | solution.py:304
  281.0 40.9 %collective-permute-start.4 = (bf16[288,448]{1,0:T(8,128)(2,1)S(1)}, bf16[288,448]{1,0:T(8,128)(2,1)}, u32[]{:S(2)}, u32[]{:S(2)}) collective-permute-start(bf16[288,448]{1,0:T(8,128)(2,1)S(1)} %get-tuple-element.54.refs_1_.refs_0_), channel_id=1, source_target_pairs={{0,32},{32,0},{64,96},{96,64},{128,160},{160,128},{192,224},{224,1... | collective-permute-start | bytes 774152 | tf_op jit(solution)/shard_map/ppermute | solution.py:307
  292.2 29.8 %collective-permute-start.10 = (bf16[288,448]{1,0:T(8,128)(2,1)S(1)}, bf16[288,448]{1,0:T(8,128)(2,1)}, u32[]{:S(2)}, u32[]{:S(2)}) collective-permute-start(bf16[288,448]{1,0:T(8,128)(2,1)S(1)} %collective-permute-done.9.refs_7_.refs_6_), channel_id=1, source_target_pairs={{0,32},{32,0},{64,96},{96,64},{128,160},{160,128},{192,224},{224,1... | collective-permute-start | bytes 774152 | tf_op jit(solution)/shard_map/ppermute | solution.py:307
  295.1 26.8 %collective-permute-start.8 = (bf16[288,448]{1,0:T(8,128)(2,1)S(1)}, bf16[288,448]{1,0:T(8,128)(2,1)}, u32[]{:S(2)}, u32[]{:S(2)}) collective-permute-start(bf16[288,448]{1,0:T(8,128)(2,1)S(1)} %collective-permute-done.7.refs_5_.refs_4_), channel_id=1, source_target_pairs={{0,32},{32,0},{64,96},{96,64},{128,160},{160,128},{192,224},{224,1... | collective-permute-start | bytes 774152 | tf_op jit(solution)/shard_map/ppermute | solution.py:307
  306.9 15.0 %collective-permute-start.6 = (bf16[288,448]{1,0:T(8,128)(2,1)S(1)}, bf16[288,448]{1,0:T(8,128)(2,1)}, u32[]{:S(2)}, u32[]{:S(2)}) collective-permute-start(bf16[288,448]{1,0:T(8,128)(2,1)S(1)} %collective-permute-done.5.refs_3_.refs_2_), channel_id=1, source_target_pairs={{0,32},{32,0},{64,96},{96,64},{128,160},{160,128},{192,224},{224,1... | collective-permute-start | bytes 774152 | tf_op jit(solution)/shard_map/ppermute | solution.py:307
  332.2 4.5 %collective-permute-start.11 = (f32[4,288,448]{2,1,0:T(8,128)S(1)}, f32[4,288,448]{2,1,0:T(8,128)S(1)}, u32[]{:S(2)}, u32[]{:S(2)}) collective-permute-start(f32[4,288,448]{2,1,0:T(8,128)S(1)} %bitcast.17), channel_id=1, source_target_pairs={{0,32},{32,0},{64,96},{96,64},{128,160},{160,128},{192,224},{224,1... | collective-permute-start | bytes 6193160 | tf_op jit(solution)/shard_map/ppermute | solution.py:307
  336.9 8.5 %collective-permute-start.12 = (bf16[288,448]{1,0:T(8,128)(2,1)S(1)}, bf16[288,448]{1,0:T(8,128)(2,1)S(1)}, u32[]{:S(2)}, u32[]{:S(2)}) collective-permute-start(bf16[288,448]{1,0:T(8,128)(2,1)S(1)} %get-tuple-element.37), channel_id=1, source_target_pairs={{0,192},{32,224},{64,0},{96,32},{128,64},{160,96},{192,128},{224,1... | collective-permute-start | bytes 774152 | tf_op jit(solution)/shard_map/ppermute | solution.py:304
  337.8 9.4 %collective-permute-start.13 = (bf16[288,448]{1,0:T(8,128)(2,1)S(1)}, bf16[288,448]{1,0:T(8,128)(2,1)S(1)}, u32[]{:S(2)}, u32[]{:S(2)}) collective-permute-start(bf16[288,448]{1,0:T(8,128)(2,1)S(1)} %get-tuple-element.38), channel_id=1, source_target_pairs={{0,128},{32,160},{64,192},{96,224},{128,0},{160,32},{192,64},{224,... | collective-permute-start | bytes 774152 | tf_op jit(solution)/shard_map/ppermute | solution.py:304
  339.0 15.5 %collective-permute-start.14 = (bf16[288,448]{1,0:T(8,128)(2,1)S(1)}, bf16[288,448]{1,0:T(8,128)(2,1)S(1)}, u32[]{:S(2)}, u32[]{:S(2)}) collective-permute-start(bf16[288,448]{1,0:T(8,128)(2,1)S(1)} %get-tuple-element.39), channel_id=1, source_target_pairs={{0,64},{32,96},{64,128},{96,160},{128,192},{160,224},{192,0},{224,... | collective-permute-start | bytes 774152 | tf_op jit(solution)/shard_map/ppermute | solution.py:304
  354.8 12.9 %collective-permute-start.16 = (bf16[288,896]{1,0:T(8,128)(2,1)S(1)}, bf16[288,896]{1,0:T(8,128)(2,1)S(1)}, u32[]{:S(2)}, u32[]{:S(2)}) collective-permute-start(bf16[288,896]{1,0:T(8,128)(2,1)S(1)} %slopes.1.refs_0_), channel_id=1, source_target_pairs={{0,192},{32,224},{64,0},{96,32},{128,64},{160,96},{192,128},{224,1... | collective-permute-start | bytes 1548296 | tf_op jit(solution)/shard_map/ppermute | solution.py:304
  354.9 13.5 %collective-permute-start.15 = (bf16[288,896]{1,0:T(8,128)(2,1)S(1)}, bf16[288,896]{1,0:T(8,128)(2,1)S(1)}, u32[]{:S(2)}, u32[]{:S(2)}) collective-permute-start(bf16[288,896]{1,0:T(8,128)(2,1)S(1)} %slopes.1.refs_0_), channel_id=1, source_target_pairs={{0,64},{32,96},{64,128},{96,160},{128,192},{160,224},{192,0},{224,... | collective-permute-start | bytes 1548296 | tf_op jit(solution)/shard_map/ppermute | solution.py:304
  363.5 11.2 %collective-permute-start.19 = (bf16[288,896]{1,0:T(8,128)(2,1)S(1)}, bf16[288,896]{1,0:T(8,128)(2,1)S(1)}, u32[]{:S(2)}, u32[]{:S(2)}) collective-permute-start(bf16[288,896]{1,0:T(8,128)(2,1)S(1)} %slopes.1.refs_0_), channel_id=1, source_target_pairs={{0,32},{32,0},{64,96},{96,64},{128,160},{160,128},{192,224},{224,1... | collective-permute-start | bytes 1548296 | tf_op jit(solution)/shard_map/ppermute | solution.py:307
  369.2 5.4 %collective-permute-start.20 = (bf16[288,896]{1,0:T(8,128)(2,1)}, bf16[288,896]{1,0:T(8,128)(2,1)S(1)}, u32[]{:S(2)}, u32[]{:S(2)}) collective-permute-start(bf16[288,896]{1,0:T(8,128)(2,1)} %get-tuple-element.42.refs_2_), channel_id=1, source_target_pairs={{0,32},{32,0},{64,96},{96,64},{128,160},{160,128},{192,224},{224,1... | collective-permute-start | bytes 1548296 | tf_op jit(solution)/shard_map/ppermute | solution.py:307
  371.1 3.5 collective-permute-start.21
  373.1 11.1 %collective-permute-start.18 = (bf16[144,896]{1,0:T(8,128)(2,1)S(1)}, bf16[144,896]{1,0:T(8,128)(2,1)S(1)}, u32[]{:S(2)}, u32[]{:S(2)}) collective-permute-start(bf16[144,896]{1,0:T(8,128)(2,1)S(1)} %slice.23), channel_id=1, source_target_pairs={{0,192},{32,224},{64,0},{96,32},{128,64},{160,96},{192,128},{224,1... | collective-permute-start | bytes 774152 | tf_op jit(solution)/shard_map/ppermute | solution.py:304
  373.4 10.8 %collective-permute-start.17 = (bf16[144,896]{1,0:T(8,128)(2,1)S(1)}, bf16[144,896]{1,0:T(8,128)(2,1)S(1)}, u32[]{:S(2)}, u32[]{:S(2)}) collective-permute-start(bf16[144,896]{1,0:T(8,128)(2,1)S(1)} %slice.22), channel_id=1, source_target_pairs={{0,64},{32,96},{64,128},{96,160},{128,192},{160,224},{192,0},{224,... | collective-permute-start | bytes 774152 | tf_op jit(solution)/shard_map/ppermute | solution.py:304
  (20 other events, 269.4 us)

commit v5 on v3

--- a/solution.py
+++ b/solution.py
@@ -78,28 +78,61 @@
 def pack_weights(gate, up, down, owners):
     depth, total = gate.shape
     wide = total // owners
-    many = 4
-    full = -(-3 * wide // 128) * 128
+    full = 3 * wide
+    half = depth // 2
+    many = 8
 
     def kernel(gate_ref, up_ref, down_ref, out_ref):
         for e in range(many):
             for n, ref in enumerate((gate_ref, up_ref, down_ref)):
-                out_ref[e, :, n * wide : (n + 1) * wide] = ref[:, e * wide : (e + 1) * wide]
-            out_ref[e, :, 3 * wide :] = jnp.zeros((depth, full - 3 * wide), BF16)
+                for h in range(2):
+                    to = h * full + n * wide
+                    out_ref[e, :, to : to + wide] = ref[h * half : (h + 1) * half, e * wide : (e + 1) * wide]
 
     spec = pl.BlockSpec((depth, many * wide), lambda i: (0, i))
     return pl.pallas_call(
         kernel,
         grid=(owners // many,),
         in_specs=[spec, spec, spec],
-        out_specs=pl.BlockSpec((many, depth, full), lambda i: (i, 0, 0)),
-        out_shape=jax.ShapeDtypeStruct((owners, depth, full), BF16),
+        out_specs=pl.BlockSpec((many, half, 2 * full), lambda i: (i, 0, 0)),
+        out_shape=jax.ShapeDtypeStruct((owners, half, 2 * full), BF16),
         compiler_params=pltpu.CompilerParams(vmem_limit_bytes=3 * VMEM_LIMIT),
-        cost_estimate=pl.CostEstimate(
-            flops=0, bytes_accessed=2 * depth * (3 * total + owners * full), transcendentals=0
-        ),
+        cost_estimate=pl.CostEstimate(flops=0, bytes_accessed=12 * depth * total, transcendentals=0),
         name="pack_weights",
     )(gate, up, down)
+
+
+def unpack_weights(received):
+    senders, half, double = received.shape
+    full = double // 2
+    wide = full // 3
+    many = 8
+    rows = many * 2 * half
+
+    def kernel(received_ref, pair_ref, down_ref):
+        for e in range(many):
+            for h in range(2):
+                to = slice((2 * e + h) * half, (2 * e + h + 1) * half)
+                at = h * full
+                pair_ref[to, :] = received_ref[e, :, at : at + 2 * wide]
+                down_ref[to, :] = received_ref[e, :, at + 2 * wide : at + full]
+
+    return pl.pallas_call(
+        kernel,
+        grid=(senders // many,),
+        in_specs=[pl.BlockSpec((many, half, double), lambda i: (i, 0, 0))],
+        out_specs=[
+            pl.BlockSpec((rows, 2 * wide), lambda i: (i, 0)),
+            pl.BlockSpec((rows, wide), lambda i: (i, 0)),
+        ],
+        out_shape=[
+            jax.ShapeDtypeStruct((senders * 2 * half, 2 * wide), BF16),
+            jax.ShapeDtypeStruct((senders * 2 * half, wide), BF16),
+        ],
+        compiler_params=pltpu.CompilerParams(vmem_limit_bytes=VMEM_LIMIT),
+        cost_estimate=pl.CostEstimate(flops=0, bytes_accessed=4 * received.size, transcendentals=0),
+        name="unpack_weights",
+    )(received)
 
 
 def unpack_and_multiply(place, received, weight, chips, first, parts):
@@ -325,8 +358,8 @@
         return pieces
 
     w_send = pack_weights(gate_dense, up_dense, down_dense, owners)
-    w_all = flat(lax.all_to_all(w_send, "expert", split_axis=0, concat_axis=0, tiled=True))
-    w_pair, w_down = w_all[:, : 2 * hidden], w_all[:, 2 * hidden : 3 * hidden]
+    w_received = lax.all_to_all(w_send, "expert", split_axis=0, concat_axis=0, tiled=True)
+    w_pair, w_down = unpack_weights(w_received)
 
     dy_send = packed(cotangent, True)
     (x_send,) = follow([packed(tokens, False)], [dy_send])

time: 393 us -> 388 us (0.987)
  transfers between devices with their start and end apart: 24 -> 24, of which waited for: 15 -> 15; matrix products, arithmetic and copies ran while one was open for 1% -> 0% of each run, Pallas kernels for 8% -> 8%
where the time goes in v5:
time: 388 us; the launch traced here: 387 us
  waiting for transfers between devices  161 us (41%)
  blocking collectives  121 us (31%)
  Pallas kernels  54.8 us (14%)
  starting transfers between devices  40.5 us (10%)
  local copies, waits for them, and re-layouts  7.1 us (2%)
    all_to_all x1, blocking collectives, exchange(): lax.all_to_all(send, ('dp', 'expert'), split_axis=0, concat_axis=0, tiled...  121 us
    ppermute x12, waiting for transfers between devices, along_x(): return lax.ppermute(value, 'dp', pairs)  89.7 us
    all_to_all x1, waiting for transfers between devices, per_device(): lax.all_to_all(w_send, 'expert', split_axis=0, concat_axis=0, tiled=True)  46.4 us
    pallas_call x2, Pallas kernels, contract_rows(): pl.pallas_call(kernel, grid=(depth // wide,), in_specs=[pl.BlockSpec(piec...  16.8 us
    pallas_call x2, Pallas kernels, pack_rows(): pl.pallas_call(kernel, grid=(blocks,), in_specs=[pl.BlockSpec((2, rows),...  16 us
    pallas_call x2, Pallas kernels, unpack_and_multiply(): pl.pallas_call(kernel, grid_spec=pltpu.PrefetchScalarGridSpec(num_scalar_...  15.8 us
    ppermute x10, starting transfers between devices, other_core(): return lax.ppermute(value, 'dp', [(i, i ^ 1) for i in range(blocks)])  14 us
    all_to_all x1, waiting for transfers between devices, exchange(): lax.all_to_all(send, ('dp', 'expert'), split_axis=0, concat_axis=0, tiled...  12.8 us
  transfers between devices with their start and end apart: 24, of which 15 were waited for; matrix products, arithmetic and copies ran while one was open for 0% of the time, Pallas kernels for 8%

profile of v5, /device:TPU:1, one launch (start us, length us, event | category | flops | bytes accessed | tf_op | source)
XLA Modules:
  0.0 386.8 jit_solution(7917417352512809851)
XLA Ops:
  0.6 4.4 %pack_weights.1 = bf16[32,16,2688]{2,1,0:T(8,128)(2,1)} custom-call(bf16[32,14336]{1,0:T(8,128)(2,1)} %gate_ref.1, bf16[32,14336]{1,0:T(8,128)(2,1)} %up_ref.1, bf16[32,14336]{1,0:T(8,128)(2,1)} %down_ref.1), custom_call_target="tpu_custom_call" | custom-call | bytes 5505024 | tf_op jit(solution)/shard_map/pack_weights/pallas_call | solution.py:93
  5.0 12.0 %all-to-all-start.2 = ((bf16[32,16,2688]{2,1,0:T(8,128)(2,1)}), bf16[32,16,2688]{2,1,0:T(8,128)(2,1)S(1)}, u32[]{:S(2)}, u32[]{:S(2)}) async-start(bf16[32,16,2688]{2,1,0:T(8,128)(2,1)} %pack_weights.1), calls=%async_computation.2 | async-start | bytes 5505024 | tf_op jit(solution)/shard_map/all_to_all | solution.py:361
  17.0 8.0 %pack_rows.2.refs_1_ = bf16[8,32,72,128]{3,2,1,0:T(8,128)(2,1)} custom-call(s32[2,128]{1,0:T(2,128)} %bitcast.19, f32[2,128]{1,0:T(2,128)} %bitcast.21, bf16[128,8192]{1,0:T(8,128)(2,1)} %source_ref.2), custom_call_target="tpu_custom_call" | custom-call | flops 1073741824 | bytes 6815744 | tf_op jit(solution)/shard_map/pack_rows/pallas_call | solution.py:59
  25.1 8.0 %pack_rows.3.refs_0_ = bf16[8,32,72,128]{3,2,1,0:T(8,128)(2,1)} custom-call(s32[2,128]{1,0:T(2,128)} %bitcast.20, f32[2,128]{1,0:T(2,128)} %bitcast.22, bf16[128,8192]{1,0:T(8,128)(2,1)} %source_ref.3), custom_call_target="tpu_custom_call" | custom-call | flops 1073741824 | bytes 6815744 | tf_op jit(solution)/shard_map/pack_rows/pallas_call | solution.py:59
  33.1 46.4 %all-to-all-done.2.received_ref = bf16[32,16,2688]{2,1,0:T(8,128)(2,1)S(1)} async-done(((bf16[32,16,2688]{2,1,0:T(8,128)(2,1)}), bf16[32,16,2688]{2,1,0:T(8,128)(2,1)S(1)}, u32[]{:S(2)}, u32[]{:S(2)}) %all-to-all-start.2) | async-done | bytes 2752544 | tf_op jit(solution)/shard_map/all_to_all | solution.py:361
  79.5 121.4 %all_to_all.15.received_ref = bf16[256,72,128]{2,1,0:T(8,128)(2,1)} all-to-all(bf16[256,72,128]{2,1,0:T(8,128)(2,1)} %bitcast.18), channel_id=1, replica_groups=mesh['dp'=8,'expert'=32] {'dp','expert'}, dimensions={0} | all-to-all | bytes 9437184 | tf_op jit(solution)/shard_map/all_to_all | solution.py:344
  200.9 6.8 %all-to-all-start = ((bf16[256,72,128]{2,1,0:T(8,128)(2,1)}), bf16[256,72,128]{2,1,0:T(8,128)(2,1)}, u32[]{:S(2)}, u32[]{:S(2)}) async-start(bf16[256,72,128]{2,1,0:T(8,128)(2,1)} %bitcast.17), calls=%async_computation | async-start | bytes 9437184 | tf_op jit(solution)/shard_map/all_to_all | solution.py:344
  211.8 7.8 %unpack_and_multiply.2 = (bf16[2,4,2,144,1024]{4,3,2,1,0:T(8,128)(2,1)S(1)}, f32[4,2,144,896]{3,2,1,0:T(8,128)S(1)}, f32[4,2,144,896]{3,2,1,0:T(8,128)S(1)}) custom-call(s32[2]{0:T(128)S(1)} %pad_add_fusion.place_ref, bf16[256,72,128]{2,1,0:T(8,128)(2,1)S(1)} %copy-done, bf16[1024,896]{1,0:T(8,128)(2,1)S(1)} %get-tuple-element.23.weight_ref), custom_call_target="tpu_custom_call" | custom-call | flops 4227858432 | bytes 19529728 | tf_op jit(solution)/shard_map/unpack_and_multiply/pallas_call | solution.py:172
  221.7 2.3 collective-permute-start
  224.1 6.7 %collective-permute-done.two_ref = f32[4,288,896]{2,1,0:T(8,128)S(1)} collective-permute-done((f32[4,288,896]{2,1,0:T(8,128)S(1)}, f32[4,288,896]{2,1,0:T(8,128)S(1)}, u32[]{:S(2)}, u32[]{:S(2)}) %collective-permute-start) | collective-permute-done | bytes 4128800 | tf_op jit(solution)/shard_map/ppermute | solution.py:337
  233.3 19.1 %collective-permute-done.1 = bf16[288,896]{1,0:T(8,128)(2,1)S(1)} collective-permute-done((bf16[288,896]{1,0:T(8,128)(2,1)S(1)}, bf16[288,896]{1,0:T(8,128)(2,1)S(1)}, u32[]{:S(2)}, u32[]{:S(2)}) %collective-permute-start.1) | collective-permute-done | bytes 516128 | tf_op jit(solution)/shard_map/ppermute | solution.py:334
  252.4 2.5 collective-permute-done.2
  254.9 20.6 %collective-permute-done.3 = bf16[288,896]{1,0:T(8,128)(2,1)S(1)} collective-permute-done((bf16[288,896]{1,0:T(8,128)(2,1)S(1)}, bf16[288,896]{1,0:T(8,128)(2,1)S(1)}, u32[]{:S(2)}, u32[]{:S(2)}) %collective-permute-start.3) | collective-permute-done | bytes 516128 | tf_op jit(solution)/shard_map/ppermute | solution.py:334
  278.8 11.0 %collective-permute-done.9.refs_7_.refs_6_ = bf16[288,448]{1,0:T(8,128)(2,1)S(1)} collective-permute-done((bf16[288,448]{1,0:T(8,128)(2,1)S(1)}, bf16[288,448]{1,0:T(8,128)(2,1)S(1)}, u32[]{:S(2)}, u32[]{:S(2)}) %collective-permute-start.9) | collective-permute-done | bytes 258080 | tf_op jit(solution)/shard_map/ppermute | solution.py:334
  291.6 2.5 collective-permute-start.8
  294.1 9.8 %collective-permute-done.5.refs_3_.refs_2_ = bf16[288,448]{1,0:T(8,128)(2,1)S(1)} collective-permute-done((bf16[288,448]{1,0:T(8,128)(2,1)S(1)}, bf16[288,448]{1,0:T(8,128)(2,1)S(1)}, u32[]{:S(2)}, u32[]{:S(2)}) %collective-permute-start.5) | collective-permute-done | bytes 258080 | tf_op jit(solution)/shard_map/ppermute | solution.py:334
  304.2 12.8 %all-to-all-done.refs_0_ = bf16[256,72,128]{2,1,0:T(8,128)(2,1)} async-done(((bf16[256,72,128]{2,1,0:T(8,128)(2,1)}), bf16[256,72,128]{2,1,0:T(8,128)(2,1)}, u32[]{:S(2)}, u32[]{:S(2)}) %all-to-all-start) | async-done | bytes 4718624 | tf_op jit(solution)/shard_map/all_to_all | solution.py:344
  317.1 8.0 %unpack_and_multiply.3 = (bf16[2,4,2,144,1024]{4,3,2,1,0:T(8,128)(2,1)S(1)}, f32[4,2,144,448]{3,2,1,0:T(8,128)S(1)}, f32[4,2,144,448]{3,2,1,0:T(8,128)S(1)}) custom-call(s32[2]{0:T(128)S(1)} %pad_add_fusion.place_ref, bf16[256,72,128]{2,1,0:T(8,128)(2,1)} %follow.4.received_ref, bf16[1024,448]{1,0:T(8,128)(2,1)S(1)} %copy-done.3), custom_call_target="tpu_custom_call" | custom-call | flops 2113929216 | bytes 14483456 | tf_op jit(solution)/shard_map/unpack_and_multiply/pallas_call | solution.py:172
  325.4 4.3 %collective-permute-done.11.two_ref = f32[4,288,448]{2,1,0:T(8,128)S(1)} collective-permute-done((f32[4,288,448]{2,1,0:T(8,128)S(1)}, f32[4,288,448]{2,1,0:T(8,128)S(1)}, u32[]{:S(2)}, u32[]{:S(2)}) %collective-permute-start.11) | collective-permute-done | bytes 2064416 | tf_op jit(solution)/shard_map/ppermute | solution.py:337
  332.0 6.4 %collective-permute-done.12.refs_0_ = bf16[288,448]{1,0:T(8,128)(2,1)S(1)} collective-permute-done((bf16[288,448]{1,0:T(8,128)(2,1)S(1)}, bf16[288,448]{1,0:T(8,128)(2,1)S(1)}, u32[]{:S(2)}, u32[]{:S(2)}) %collective-permute-start.12) | collective-permute-done | bytes 258080 | tf_op jit(solution)/shard_map/ppermute | solution.py:334
  340.2 7.3 %collective-permute-done.14.refs_2_ = bf16[288,448]{1,0:T(8,128)(2,1)S(1)} collective-permute-done((bf16[288,448]{1,0:T(8,128)(2,1)S(1)}, bf16[288,448]{1,0:T(8,128)(2,1)S(1)}, u32[]{:S(2)}, u32[]{:S(2)}) %collective-permute-start.14) | collective-permute-done | bytes 258080 | tf_op jit(solution)/shard_map/ppermute | solution.py:334
  350.0 7.1 %contract_rows.2 = (f32[448,1024]{1,0:T(8,128)}, f32[8,128]{1,0:T(8,128)}) custom-call(bf16[288,448]{1,0:T(8,128)(2,1)} %copy-done.6, bf16[288,448]{1,0:T(8,128)(2,1)} %collective-permute-done.4.refs_2_.refs_1_, bf16[288,448]{1,0:T(8,128)(2,1)} %copy-done.10, bf16[288,448]{1,0:T(8,128)(2,1)} %collective-permute-done.6.refs_4_.refs_3_, ...), custom_call_target="tpu_custom_call" | custom-call | flops 2113929216 | bytes 8617984 | tf_op jit(solution)/shard_map/contract_rows/pallas_call | solution.py:298
  365.2 9.0 %collective-permute-done.16.refs_2_ = bf16[288,896]{1,0:T(8,128)(2,1)S(1)} collective-permute-done((bf16[288,896]{1,0:T(8,128)(2,1)S(1)}, bf16[288,896]{1,0:T(8,128)(2,1)S(1)}, u32[]{:S(2)}, u32[]{:S(2)}) %collective-permute-start.16) | collective-permute-done | bytes 516128 | tf_op jit(solution)/shard_map/ppermute | solution.py:334
  377.1 9.7 %contract_rows.3 = (f32[448,1024]{1,0:T(8,128)}, f32[448,1024]{1,0:T(8,128)}, f32[8,128]{1,0:T(8,128)}) custom-call(bf16[288,896]{1,0:T(8,128)(2,1)} %copy-done.1, bf16[288,896]{1,0:T(8,128)(2,1)} %copy-done.13, bf16[288,896]{1,0:T(8,128)(2,1)} %copy-done.12, bf16[288,896]{1,0:T(8,128)(2,1)} %copy-done.16, bf16[288,896]{1,0:T(8,128)(2,1)} %copy-done.11, ...), custom_call_target="tpu_custom_call" | custom-call | flops 4227858432 | bytes 12517376 | tf_op jit(solution)/shard_map/contract_rows/pallas_call | solution.py:298
  (76 shorter events, 32.0 us)
Async XLA Ops:
  5.0 74.5 %all-to-all-start.2 = ((bf16[32,16,2688]{2,1,0:T(8,128)(2,1)}), bf16[32,16,2688]{2,1,0:T(8,128)(2,1)S(1)}, u32[]{:S(2)}, u32[]{:S(2)}) async-start(bf16[32,16,2688]{2,1,0:T(8,128)(2,1)} %pack_weights.1), calls=%async_computation.2 | async-start | bytes 5505024 | tf_op jit(solution)/shard_map/all_to_all | solution.py:361
  200.9 116.1 %all-to-all-start = ((bf16[256,72,128]{2,1,0:T(8,128)(2,1)}), bf16[256,72,128]{2,1,0:T(8,128)(2,1)}, u32[]{:S(2)}, u32[]{:S(2)}) async-start(bf16[256,72,128]{2,1,0:T(8,128)(2,1)} %bitcast.17), calls=%async_computation | async-start | bytes 9437184 | tf_op jit(solution)/shard_map/all_to_all | solution.py:344
  221.7 9.0 %collective-permute-start = (f32[4,288,896]{2,1,0:T(8,128)S(1)}, f32[4,288,896]{2,1,0:T(8,128)S(1)}, u32[]{:S(2)}, u32[]{:S(2)}) collective-permute-start(f32[4,288,896]{2,1,0:T(8,128)S(1)} %bitcast.15), channel_id=1, source_target_pairs={{0,32},{32,0},{64,96},{96,64},{128,160},{160,128},{192,224},{224,1... | collective-permute-start | bytes 12386312 | tf_op jit(solution)/shard_map/ppermute | solution.py:337
  231.4 20.9 %collective-permute-start.1 = (bf16[288,896]{1,0:T(8,128)(2,1)S(1)}, bf16[288,896]{1,0:T(8,128)(2,1)S(1)}, u32[]{:S(2)}, u32[]{:S(2)}) collective-permute-start(bf16[288,896]{1,0:T(8,128)(2,1)S(1)} %get-tuple-element.27), channel_id=1, source_target_pairs={{0,192},{32,224},{64,0},{96,32},{128,64},{160,96},{192,128},{224,1... | collective-permute-start | bytes 1548296 | tf_op jit(solution)/shard_map/ppermute | solution.py:334
  232.2 22.7 %collective-permute-start.2 = (bf16[288,896]{1,0:T(8,128)(2,1)S(1)}, bf16[288,896]{1,0:T(8,128)(2,1)S(1)}, u32[]{:S(2)}, u32[]{:S(2)}) collective-permute-start(bf16[288,896]{1,0:T(8,128)(2,1)S(1)} %get-tuple-element.28), channel_id=1, source_target_pairs={{0,128},{32,160},{64,192},{96,224},{128,0},{160,32},{192,64},{224,... | collective-permute-start | bytes 1548296 | tf_op jit(solution)/shard_map/ppermute | solution.py:334
  232.7 42.7 %collective-permute-start.3 = (bf16[288,896]{1,0:T(8,128)(2,1)S(1)}, bf16[288,896]{1,0:T(8,128)(2,1)S(1)}, u32[]{:S(2)}, u32[]{:S(2)}) collective-permute-start(bf16[288,896]{1,0:T(8,128)(2,1)S(1)} %get-tuple-element.29), channel_id=1, source_target_pairs={{0,64},{32,96},{64,128},{96,160},{128,192},{160,224},{192,0},{224,... | collective-permute-start | bytes 1548296 | tf_op jit(solution)/shard_map/ppermute | solution.py:334
  276.1 13.7 %collective-permute-start.9 = (bf16[288,448]{1,0:T(8,128)(2,1)S(1)}, bf16[288,448]{1,0:T(8,128)(2,1)S(1)}, u32[]{:S(2)}, u32[]{:S(2)}) collective-permute-start(bf16[288,448]{1,0:T(8,128)(2,1)S(1)} %get-tuple-element.44.refs_1_.refs_0_), channel_id=1, source_target_pairs={{0,192},{32,224},{64,0},{96,32},{128,64},{160,96},{192,128},{224,1... | collective-permute-start | bytes 774152 | tf_op jit(solution)/shard_map/ppermute | solution.py:334
  276.1 15.4 %collective-permute-start.7 = (bf16[288,448]{1,0:T(8,128)(2,1)S(1)}, bf16[288,448]{1,0:T(8,128)(2,1)S(1)}, u32[]{:S(2)}, u32[]{:S(2)}) collective-permute-start(bf16[288,448]{1,0:T(8,128)(2,1)S(1)} %get-tuple-element.44.refs_1_.refs_0_), channel_id=1, source_target_pairs={{0,128},{32,160},{64,192},{96,224},{128,0},{160,32},{192,64},{224,... | collective-permute-start | bytes 774152 | tf_op jit(solution)/shard_map/ppermute | solution.py:334
  276.6 27.2 %collective-permute-start.5 = (bf16[288,448]{1,0:T(8,128)(2,1)S(1)}, bf16[288,448]{1,0:T(8,128)(2,1)S(1)}, u32[]{:S(2)}, u32[]{:S(2)}) collective-permute-start(bf16[288,448]{1,0:T(8,128)(2,1)S(1)} %get-tuple-element.44.refs_1_.refs_0_), channel_id=1, source_target_pairs={{0,64},{32,96},{64,128},{96,160},{128,192},{160,224},{192,0},{224,... | collective-permute-start | bytes 774152 | tf_op jit(solution)/shard_map/ppermute | solution.py:334
  277.6 39.4 %collective-permute-start.4 = (bf16[288,448]{1,0:T(8,128)(2,1)S(1)}, bf16[288,448]{1,0:T(8,128)(2,1)}, u32[]{:S(2)}, u32[]{:S(2)}) collective-permute-start(bf16[288,448]{1,0:T(8,128)(2,1)S(1)} %get-tuple-element.44.refs_1_.refs_0_), channel_id=1, source_target_pairs={{0,32},{32,0},{64,96},{96,64},{128,160},{160,128},{192,224},{224,1... | collective-permute-start | bytes 774152 | tf_op jit(solution)/shard_map/ppermute | solution.py:337
  289.7 27.3 %collective-permute-start.10 = (bf16[288,448]{1,0:T(8,128)(2,1)S(1)}, bf16[288,448]{1,0:T(8,128)(2,1)}, u32[]{:S(2)}, u32[]{:S(2)}) collective-permute-start(bf16[288,448]{1,0:T(8,128)(2,1)S(1)} %collective-permute-done.9.refs_7_.refs_6_), channel_id=1, source_target_pairs={{0,32},{32,0},{64,96},{96,64},{128,160},{160,128},{192,224},{224,1... | collective-permute-start | bytes 774152 | tf_op jit(solution)/shard_map/ppermute | solution.py:337
  291.6 25.4 %collective-permute-start.8 = (bf16[288,448]{1,0:T(8,128)(2,1)S(1)}, bf16[288,448]{1,0:T(8,128)(2,1)}, u32[]{:S(2)}, u32[]{:S(2)}) collective-permute-start(bf16[288,448]{1,0:T(8,128)(2,1)S(1)} %collective-permute-done.7.refs_5_.refs_4_), channel_id=1, source_target_pairs={{0,32},{32,0},{64,96},{96,64},{128,160},{160,128},{192,224},{224,1... | collective-permute-start | bytes 774152 | tf_op jit(solution)/shard_map/ppermute | solution.py:337
  303.9 13.2 %collective-permute-start.6 = (bf16[288,448]{1,0:T(8,128)(2,1)S(1)}, bf16[288,448]{1,0:T(8,128)(2,1)}, u32[]{:S(2)}, u32[]{:S(2)}) collective-permute-start(bf16[288,448]{1,0:T(8,128)(2,1)S(1)} %collective-permute-done.5.refs_3_.refs_2_), channel_id=1, source_target_pairs={{0,32},{32,0},{64,96},{96,64},{128,160},{160,128},{192,224},{224,1... | collective-permute-start | bytes 774152 | tf_op jit(solution)/shard_map/ppermute | solution.py:337
  325.1 4.6 %collective-permute-start.11 = (f32[4,288,448]{2,1,0:T(8,128)S(1)}, f32[4,288,448]{2,1,0:T(8,128)S(1)}, u32[]{:S(2)}, u32[]{:S(2)}) collective-permute-start(f32[4,288,448]{2,1,0:T(8,128)S(1)} %bitcast.16), channel_id=1, source_target_pairs={{0,32},{32,0},{64,96},{96,64},{128,160},{160,128},{192,224},{224,1... | collective-permute-start | bytes 6193160 | tf_op jit(solution)/shard_map/ppermute | solution.py:337
  330.0 8.4 %collective-permute-start.12 = (bf16[288,448]{1,0:T(8,128)(2,1)S(1)}, bf16[288,448]{1,0:T(8,128)(2,1)S(1)}, u32[]{:S(2)}, u32[]{:S(2)}) collective-permute-start(bf16[288,448]{1,0:T(8,128)(2,1)S(1)} %get-tuple-element.34), channel_id=1, source_target_pairs={{0,192},{32,224},{64,0},{96,32},{128,64},{160,96},{192,128},{224,1... | collective-permute-start | bytes 774152 | tf_op jit(solution)/shard_map/ppermute | solution.py:334
  330.8 9.4 %collective-permute-start.13 = (bf16[288,448]{1,0:T(8,128)(2,1)S(1)}, bf16[288,448]{1,0:T(8,128)(2,1)S(1)}, u32[]{:S(2)}, u32[]{:S(2)}) collective-permute-start(bf16[288,448]{1,0:T(8,128)(2,1)S(1)} %get-tuple-element.35), channel_id=1, source_target_pairs={{0,128},{32,160},{64,192},{96,224},{128,0},{160,32},{192,64},{224,... | collective-permute-start | bytes 774152 | tf_op jit(solution)/shard_map/ppermute | solution.py:334
  332.0 15.5 %collective-permute-start.14 = (bf16[288,448]{1,0:T(8,128)(2,1)S(1)}, bf16[288,448]{1,0:T(8,128)(2,1)S(1)}, u32[]{:S(2)}, u32[]{:S(2)}) collective-permute-start(bf16[288,448]{1,0:T(8,128)(2,1)S(1)} %get-tuple-element.36), channel_id=1, source_target_pairs={{0,64},{32,96},{64,128},{96,160},{128,192},{160,224},{192,0},{224,... | collective-permute-start | bytes 774152 | tf_op jit(solution)/shard_map/ppermute | solution.py:334
  347.8 12.9 %collective-permute-start.20 = (bf16[288,896]{1,0:T(8,128)(2,1)S(1)}, bf16[288,896]{1,0:T(8,128)(2,1)S(1)}, u32[]{:S(2)}, u32[]{:S(2)}) collective-permute-start(bf16[288,896]{1,0:T(8,128)(2,1)S(1)} %slopes.1.refs_0_), channel_id=1, source_target_pairs={{0,192},{32,224},{64,0},{96,32},{128,64},{160,96},{192,128},{224,1... | collective-permute-start | bytes 1548296 | tf_op jit(solution)/shard_map/ppermute | solution.py:334
  347.9 15.9 %collective-permute-start.18 = (bf16[288,896]{1,0:T(8,128)(2,1)S(1)}, bf16[288,896]{1,0:T(8,128)(2,1)S(1)}, u32[]{:S(2)}, u32[]{:S(2)}) collective-permute-start(bf16[288,896]{1,0:T(8,128)(2,1)S(1)} %slopes.1.refs_0_), channel_id=1, source_target_pairs={{0,128},{32,160},{64,192},{96,224},{128,0},{160,32},{192,64},{224,... | collective-permute-start | bytes 1548296 | tf_op jit(solution)/shard_map/ppermute | solution.py:334
  349.2 25.0 %collective-permute-start.16 = (bf16[288,896]{1,0:T(8,128)(2,1)S(1)}, bf16[288,896]{1,0:T(8,128)(2,1)S(1)}, u32[]{:S(2)}, u32[]{:S(2)}) collective-permute-start(bf16[288,896]{1,0:T(8,128)(2,1)S(1)} %slopes.1.refs_0_), channel_id=1, source_target_pairs={{0,64},{32,96},{64,128},{96,160},{128,192},{160,224},{192,0},{224,... | collective-permute-start | bytes 1548296 | tf_op jit(solution)/shard_map/ppermute | solution.py:334
  357.1 17.7 %collective-permute-start.15 = (bf16[288,896]{1,0:T(8,128)(2,1)S(1)}, bf16[288,896]{1,0:T(8,128)(2,1)S(1)}, u32[]{:S(2)}, u32[]{:S(2)}) collective-permute-start(bf16[288,896]{1,0:T(8,128)(2,1)S(1)} %slopes.1.refs_0_), channel_id=1, source_target_pairs={{0,32},{32,0},{64,96},{96,64},{128,160},{160,128},{192,224},{224,1... | collective-permute-start | bytes 1548296 | tf_op jit(solution)/shard_map/ppermute | solution.py:337
  361.6 13.2 %collective-permute-start.21 = (bf16[288,896]{1,0:T(8,128)(2,1)}, bf16[288,896]{1,0:T(8,128)(2,1)S(1)}, u32[]{:S(2)}, u32[]{:S(2)}) collective-permute-start(bf16[288,896]{1,0:T(8,128)(2,1)} %follow.5.refs_6_), channel_id=1, source_target_pairs={{0,32},{32,0},{64,96},{96,64},{128,160},{160,128},{192,224},{224,1... | collective-permute-start | bytes 1548296 | tf_op jit(solution)/shard_map/ppermute | solution.py:337
  363.8 10.9 %collective-permute-start.19 = (bf16[288,896]{1,0:T(8,128)(2,1)S(1)}, bf16[288,896]{1,0:T(8,128)(2,1)S(1)}, u32[]{:S(2)}, u32[]{:S(2)}) collective-permute-start(bf16[288,896]{1,0:T(8,128)(2,1)S(1)} %collective-permute-done.18.refs_4_), channel_id=1, source_target_pairs={{0,32},{32,0},{64,96},{96,64},{128,160},{160,128},{192,224},{224,1... | collective-permute-start | bytes 1548296 | tf_op jit(solution)/shard_map/ppermute | solution.py:337
  374.2 2.0 collective-permute-start.17
  (17 other events, 210.7 us)

commit v6 on v5

--- a/solution.py
+++ b/solution.py
@@ -202,10 +202,17 @@
 
 def add_steps(one, two, kind):
     steps, rows, columns = one.shape
+    folded = columns % 128 > 0
+    sent = (rows // 2, 2 * columns) if folded else (rows, columns)
 
     def kernel(one_ref, two_ref, *out_refs):
         for n in range(steps):
-            out_refs[n][...] = (one_ref[n] + two_ref[n]).astype(out_refs[n].dtype)
+            total = (one_ref[n] + two_ref[n]).astype(out_refs[n].dtype)
+            if n and folded:
+                out_refs[n][:, :columns] = total[: rows // 2]
+                out_refs[n][:, columns:] = total[rows // 2 :]
+            else:
+                out_refs[n][...] = total
 
     whole = pl.BlockSpec(memory_space=pltpu.VMEM)
     return pl.pallas_call(
@@ -213,7 +220,8 @@
         in_specs=[whole] * 2,
         out_specs=[whole] * steps,
         out_shape=[
-            jax.ShapeDtypeStruct((rows, columns), kind if n else F32) for n in range(steps)
+            jax.ShapeDtypeStruct(sent, kind) if n else jax.ShapeDtypeStruct((rows, columns), F32)
+            for n in range(steps)
         ],
         compiler_params=pltpu.CompilerParams(vmem_limit_bytes=VMEM_LIMIT),
         cost_estimate=pl.CostEstimate(
@@ -223,25 +231,26 @@
     )(one, two)
 
 
-def slopes(total, active, slope, part):
+def slopes(total, active, slope):
     own, others = total[0], total[1:]
     rows, columns = own.shape
+    half = rows // 2
 
     def kernel(own_ref, *refs):
         active_ref, slope_ref, out_ref = refs[len(others) :]
-        back = own_ref[...]
-        for ref in refs[: len(others)]:
-            back = back + ref[...].astype(F32)
-        out_ref[:, :columns] = (back * slope_ref[...]).astype(BF16)
-        out_ref[:, columns:] = (back * active_ref[...]).astype(BF16)
-
-    whole = pl.BlockSpec((rows, columns), lambda i: (0, 0))
-    mine = pl.BlockSpec((rows, columns), lambda i: (part, 0))
-    return pl.pallas_call(
-        kernel,
-        grid=(1,),
-        in_specs=[whole] * len(total) + [mine] * 2,
-        out_specs=pl.BlockSpec((rows, 2 * columns), lambda i: (0, 0)),
+        for h in range(2):
+            mine = slice(h * half, (h + 1) * half)
+            back = own_ref[mine]
+            for ref in refs[: len(others)]:
+                back = back + ref[:, h * columns : (h + 1) * columns].astype(F32)
+            out_ref[mine, :columns] = (back * slope_ref[mine]).astype(BF16)
+            out_ref[mine, columns:] = (back * active_ref[mine]).astype(BF16)
+
+    whole = pl.BlockSpec(memory_space=pltpu.VMEM)
+    return pl.pallas_call(
+        kernel,
+        in_specs=[whole] * (len(total) + 2),
+        out_specs=whole,
         out_shape=jax.ShapeDtypeStruct((rows, 2 * columns), BF16),
         compiler_params=pltpu.CompilerParams(vmem_limit_bytes=VMEM_LIMIT),
         cost_estimate=pl.CostEstimate(
@@ -278,8 +287,8 @@
 
     def kernel(*refs):
         piece_refs, rows_ref = refs[:count], refs[count]
-        out_refs, done_ref = refs[count + 1 : -3], refs[-3]
-        left_ref, turned_ref = refs[-2:]
+        out_refs, done_ref = refs[count + 1 : -2], refs[-2]
+        left_ref = refs[-1]
         done_ref[...] = jnp.zeros_like(done_ref)
 
         @pl.when(pl.program_id(0) == 0)
@@ -288,10 +297,11 @@
                 for n in range(count):
                     to = (p * count + n) * half
                     left_ref[to : to + half] = piece_refs[n][p * half : (p + 1) * half]
-            turned_ref[...] = left_ref[...].T
 
         right = rows_ref[...].reshape(height, wide)
-        product = jnp.dot(turned_ref[...], right, preferred_element_type=F32)
+        product = lax.dot_general(
+            left_ref[...], right, (((0,), (0,)), ((), ())), preferred_element_type=F32
+        )
         for n in range(outs):
             out_refs[n][...] = product[n * hidden : (n + 1) * hidden]
 
@@ -304,7 +314,7 @@
         + [pl.BlockSpec((8, 128), lambda i: (0, 0))],
         out_shape=[jax.ShapeDtypeStruct((hidden, depth), F32)] * outs
         + [jax.ShapeDtypeStruct((8, 128), F32)],
-        scratch_shapes=[pltpu.VMEM((height, columns), BF16), pltpu.VMEM((columns, height), BF16)],
+        scratch_shapes=[pltpu.VMEM((height, columns), BF16)],
         compiler_params=pltpu.CompilerParams(vmem_limit_bytes=3 * VMEM_LIMIT),
         cost_estimate=pl.CostEstimate(
             flops=2 * height * depth * columns,
@@ -376,7 +386,7 @@
     (dy_received,) = follow([dy_received], hidden_all)
 
     dy_rows, keep, send = unpack_and_multiply(place, dy_received, w_down, chips, 0, 2)
-    d_pair = slopes(reduce_rows(keep, send), active, slope, 0)
+    d_pair = slopes(reduce_rows(keep, send), active, slope)
     grad_down, down_done = contract_rows(hidden_all, dy_rows)
     grad_gate, grad_up, _ = contract_rows(gather_rows(d_pair, [down_done]), x_rows)
     return (grad_gate.T, grad_up.T, grad_down.T)

time: 388 us -> 386 us (level)
  no operation moved by 1% of the time
where the time goes in v6:
time: 386 us; the launch traced here: 385 us
  waiting for transfers between devices  160 us (41%)
  blocking collectives  121 us (31%)
  Pallas kernels  54.3 us (14%)
  starting transfers between devices  40.5 us (10%)
  local copies, waits for them, and re-layouts  7.1 us (2%)
    all_to_all x1, blocking collectives, exchange(): lax.all_to_all(send, ('dp', 'expert'), split_axis=0, concat_axis=0, tiled...  121 us
    ppermute x12, waiting for transfers between devices, along_x(): return lax.ppermute(value, 'dp', pairs)  88.3 us
    all_to_all x1, waiting for transfers between devices, per_device(): lax.all_to_all(w_send, 'expert', split_axis=0, concat_axis=0, tiled=True)  46.4 us
    pallas_call x2, Pallas kernels, pack_rows(): pl.pallas_call(kernel, grid=(blocks,), in_specs=[pl.BlockSpec((2, rows),...  16 us
    pallas_call x2, Pallas kernels, contract_rows(): pl.pallas_call(kernel, grid=(depth // wide,), in_specs=[pl.BlockSpec(piec...  16 us
    pallas_call x2, Pallas kernels, unpack_and_multiply(): pl.pallas_call(kernel, grid_spec=pltpu.PrefetchScalarGridSpec(num_scalar_...  15.8 us
    ppermute x10, starting transfers between devices, other_core(): return lax.ppermute(value, 'dp', [(i, i ^ 1) for i in range(blocks)])  14 us
    all_to_all x1, waiting for transfers between devices, exchange(): lax.all_to_all(send, ('dp', 'expert'), split_axis=0, concat_axis=0, tiled...  12.8 us
  transfers between devices with their start and end apart: 24, of which 15 were waited for; matrix products, arithmetic and copies ran while one was open for 0% of the time, Pallas kernels for 8%

profile of v6, /device:TPU:1, one launch (start us, length us, event | category | flops | bytes accessed | tf_op | source)
XLA Modules:
  0.0 384.7 jit_solution(15796143764789592997)
XLA Ops:
  0.6 4.4 %pack_weights.1 = bf16[32,16,2688]{2,1,0:T(8,128)(2,1)} custom-call(bf16[32,14336]{1,0:T(8,128)(2,1)} %gate_ref.1, bf16[32,14336]{1,0:T(8,128)(2,1)} %up_ref.1, bf16[32,14336]{1,0:T(8,128)(2,1)} %down_ref.1), custom_call_target="tpu_custom_call" | custom-call | bytes 5505024 | tf_op jit(solution)/shard_map/pack_weights/pallas_call | solution.py:93
  5.0 12.0 %all-to-all-start.2 = ((bf16[32,16,2688]{2,1,0:T(8,128)(2,1)}), bf16[32,16,2688]{2,1,0:T(8,128)(2,1)S(1)}, u32[]{:S(2)}, u32[]{:S(2)}) async-start(bf16[32,16,2688]{2,1,0:T(8,128)(2,1)} %pack_weights.1), calls=%async_computation.2 | async-start | bytes 5505024 | tf_op jit(solution)/shard_map/all_to_all | solution.py:371
  17.0 8.0 %pack_rows.2.refs_1_ = bf16[8,32,72,128]{3,2,1,0:T(8,128)(2,1)} custom-call(s32[2,128]{1,0:T(2,128)} %bitcast.19, f32[2,128]{1,0:T(2,128)} %bitcast.21, bf16[128,8192]{1,0:T(8,128)(2,1)} %source_ref.2), custom_call_target="tpu_custom_call" | custom-call | flops 1073741824 | bytes 6815744 | tf_op jit(solution)/shard_map/pack_rows/pallas_call | solution.py:59
  25.1 8.0 %pack_rows.3.refs_0_ = bf16[8,32,72,128]{3,2,1,0:T(8,128)(2,1)} custom-call(s32[2,128]{1,0:T(2,128)} %bitcast.20, f32[2,128]{1,0:T(2,128)} %bitcast.22, bf16[128,8192]{1,0:T(8,128)(2,1)} %source_ref.3), custom_call_target="tpu_custom_call" | custom-call | flops 1073741824 | bytes 6815744 | tf_op jit(solution)/shard_map/pack_rows/pallas_call | solution.py:59
  33.1 46.4 %all-to-all-done.2.received_ref = bf16[32,16,2688]{2,1,0:T(8,128)(2,1)S(1)} async-done(((bf16[32,16,2688]{2,1,0:T(8,128)(2,1)}), bf16[32,16,2688]{2,1,0:T(8,128)(2,1)S(1)}, u32[]{:S(2)}, u32[]{:S(2)}) %all-to-all-start.2) | async-done | bytes 2752544 | tf_op jit(solution)/shard_map/all_to_all | solution.py:371
  79.5 121.4 %all_to_all.15.received_ref = bf16[256,72,128]{2,1,0:T(8,128)(2,1)} all-to-all(bf16[256,72,128]{2,1,0:T(8,128)(2,1)} %bitcast.18), channel_id=1, replica_groups=mesh['dp'=8,'expert'=32] {'dp','expert'}, dimensions={0} | all-to-all | bytes 9437184 | tf_op jit(solution)/shard_map/all_to_all | solution.py:354
  200.9 6.8 %all-to-all-start = ((bf16[256,72,128]{2,1,0:T(8,128)(2,1)}), bf16[256,72,128]{2,1,0:T(8,128)(2,1)}, u32[]{:S(2)}, u32[]{:S(2)}) async-start(bf16[256,72,128]{2,1,0:T(8,128)(2,1)} %bitcast.17), calls=%async_computation | async-start | bytes 9437184 | tf_op jit(solution)/shard_map/all_to_all | solution.py:354
  211.8 7.8 %unpack_and_multiply.2 = (bf16[2,4,2,144,1024]{4,3,2,1,0:T(8,128)(2,1)S(1)}, f32[4,2,144,896]{3,2,1,0:T(8,128)S(1)}, f32[4,2,144,896]{3,2,1,0:T(8,128)S(1)}) custom-call(s32[2]{0:T(128)S(1)} %pad_add_fusion.place_ref, bf16[256,72,128]{2,1,0:T(8,128)(2,1)S(1)} %copy-done, bf16[1024,896]{1,0:T(8,128)(2,1)S(1)} %get-tuple-element.23.weight_ref), custom_call_target="tpu_custom_call" | custom-call | flops 4227858432 | bytes 19529728 | tf_op jit(solution)/shard_map/unpack_and_multiply/pallas_call | solution.py:172
  224.1 6.7 %collective-permute-done.two_ref = f32[4,288,896]{2,1,0:T(8,128)S(1)} collective-permute-done((f32[4,288,896]{2,1,0:T(8,128)S(1)}, f32[4,288,896]{2,1,0:T(8,128)S(1)}, u32[]{:S(2)}, u32[]{:S(2)}) %collective-permute-start) | collective-permute-done | bytes 4128800 | tf_op jit(solution)/shard_map/ppermute | solution.py:347
  233.3 19.1 %collective-permute-done.1 = bf16[288,896]{1,0:T(8,128)(2,1)S(1)} collective-permute-done((bf16[288,896]{1,0:T(8,128)(2,1)S(1)}, bf16[288,896]{1,0:T(8,128)(2,1)S(1)}, u32[]{:S(2)}, u32[]{:S(2)}) %collective-permute-start.1) | collective-permute-done | bytes 516128 | tf_op jit(solution)/shard_map/ppermute | solution.py:344
  252.4 2.5 collective-permute-done.2
  254.9 20.6 %collective-permute-done.3 = bf16[288,896]{1,0:T(8,128)(2,1)S(1)} collective-permute-done((bf16[288,896]{1,0:T(8,128)(2,1)S(1)}, bf16[288,896]{1,0:T(8,128)(2,1)S(1)}, u32[]{:S(2)}, u32[]{:S(2)}) %collective-permute-start.3) | collective-permute-done | bytes 516128 | tf_op jit(solution)/shard_map/ppermute | solution.py:344
  278.8 11.0 %collective-permute-done.9.refs_7_.refs_6_ = bf16[288,448]{1,0:T(8,128)(2,1)S(1)} collective-permute-done((bf16[288,448]{1,0:T(8,128)(2,1)S(1)}, bf16[288,448]{1,0:T(8,128)(2,1)S(1)}, u32[]{:S(2)}, u32[]{:S(2)}) %collective-permute-start.9) | collective-permute-done | bytes 258080 | tf_op jit(solution)/shard_map/ppermute | solution.py:344
  291.6 2.5 collective-permute-start.8
  294.1 9.8 %collective-permute-done.5.refs_3_.refs_2_ = bf16[288,448]{1,0:T(8,128)(2,1)S(1)} collective-permute-done((bf16[288,448]{1,0:T(8,128)(2,1)S(1)}, bf16[288,448]{1,0:T(8,128)(2,1)S(1)}, u32[]{:S(2)}, u32[]{:S(2)}) %collective-permute-start.5) | collective-permute-done | bytes 258080 | tf_op jit(solution)/shard_map/ppermute | solution.py:344
  304.2 12.8 %all-to-all-done.refs_0_ = bf16[256,72,128]{2,1,0:T(8,128)(2,1)} async-done(((bf16[256,72,128]{2,1,0:T(8,128)(2,1)}), bf16[256,72,128]{2,1,0:T(8,128)(2,1)}, u32[]{:S(2)}, u32[]{:S(2)}) %all-to-all-start) | async-done | bytes 4718624 | tf_op jit(solution)/shard_map/all_to_all | solution.py:354
  317.1 8.0 %unpack_and_multiply.3 = (bf16[2,4,2,144,1024]{4,3,2,1,0:T(8,128)(2,1)S(1)}, f32[4,2,144,448]{3,2,1,0:T(8,128)S(1)}, f32[4,2,144,448]{3,2,1,0:T(8,128)S(1)}) custom-call(s32[2]{0:T(128)S(1)} %pad_add_fusion.place_ref, bf16[256,72,128]{2,1,0:T(8,128)(2,1)} %follow.4.received_ref, bf16[1024,448]{1,0:T(8,128)(2,1)S(1)} %copy-done.3), custom_call_target="tpu_custom_call" | custom-call | flops 2113929216 | bytes 14483456 | tf_op jit(solution)/shard_map/unpack_and_multiply/pallas_call | solution.py:172
  325.4 4.3 %collective-permute-done.11.two_ref = f32[4,288,448]{2,1,0:T(8,128)S(1)} collective-permute-done((f32[4,288,448]{2,1,0:T(8,128)S(1)}, f32[4,288,448]{2,1,0:T(8,128)S(1)}, u32[]{:S(2)}, u32[]{:S(2)}) %collective-permute-start.11) | collective-permute-done | bytes 2064416 | tf_op jit(solution)/shard_map/ppermute | solution.py:347
  332.1 5.6 %collective-permute-done.12.refs_0_ = bf16[144,896]{1,0:T(8,128)(2,1)S(1)} collective-permute-done((bf16[144,896]{1,0:T(8,128)(2,1)S(1)}, bf16[144,896]{1,0:T(8,128)(2,1)S(1)}, u32[]{:S(2)}, u32[]{:S(2)}) %collective-permute-start.12) | collective-permute-done | bytes 258080 | tf_op jit(solution)/shard_map/ppermute | solution.py:344
  339.5 6.5 %collective-permute-done.14.refs_2_ = bf16[144,896]{1,0:T(8,128)(2,1)S(1)} collective-permute-done((bf16[144,896]{1,0:T(8,128)(2,1)S(1)}, bf16[144,896]{1,0:T(8,128)(2,1)S(1)}, u32[]{:S(2)}, u32[]{:S(2)}) %collective-permute-start.14) | collective-permute-done | bytes 258080 | tf_op jit(solution)/shard_map/ppermute | solution.py:344
  348.6 7.0 %contract_rows.2 = (f32[448,1024]{1,0:T(8,128)}, f32[8,128]{1,0:T(8,128)}) custom-call(bf16[288,448]{1,0:T(8,128)(2,1)} %copy-done.6, bf16[288,448]{1,0:T(8,128)(2,1)} %collective-permute-done.4.refs_2_.refs_1_, bf16[288,448]{1,0:T(8,128)(2,1)} %copy-done.10, bf16[288,448]{1,0:T(8,128)(2,1)} %collective-permute-done.6.refs_4_.refs_3_, ...), custom_call_target="tpu_custom_call" | custom-call | flops 2113929216 | bytes 8617984 | tf_op jit(solution)/shard_map/contract_rows/pallas_call | solution.py:308
  356.9 2.4 collective-permute-done.20.refs_0_
  363.9 9.0 %collective-permute-done.16.refs_2_ = bf16[288,896]{1,0:T(8,128)(2,1)S(1)} collective-permute-done((bf16[288,896]{1,0:T(8,128)(2,1)S(1)}, bf16[288,896]{1,0:T(8,128)(2,1)S(1)}, u32[]{:S(2)}, u32[]{:S(2)}) %collective-permute-start.16) | collective-permute-done | bytes 516128 | tf_op jit(solution)/shard_map/ppermute | solution.py:344
  375.7 9.0 %contract_rows.3 = (f32[448,1024]{1,0:T(8,128)}, f32[448,1024]{1,0:T(8,128)}, f32[8,128]{1,0:T(8,128)}) custom-call(bf16[288,896]{1,0:T(8,128)(2,1)} %copy-done.1, bf16[288,896]{1,0:T(8,128)(2,1)} %copy-done.13, bf16[288,896]{1,0:T(8,128)(2,1)} %copy-done.12, bf16[288,896]{1,0:T(8,128)(2,1)} %copy-done.16, bf16[288,896]{1,0:T(8,128)(2,1)} %copy-done.11, ...), custom_call_target="tpu_custom_call" | custom-call | flops 4227858432 | bytes 12517376 | tf_op jit(solution)/shard_map/contract_rows/pallas_call | solution.py:308
  (76 shorter events, 32.3 us)
Async XLA Ops:
  5.0 74.5 %all-to-all-start.2 = ((bf16[32,16,2688]{2,1,0:T(8,128)(2,1)}), bf16[32,16,2688]{2,1,0:T(8,128)(2,1)S(1)}, u32[]{:S(2)}, u32[]{:S(2)}) async-start(bf16[32,16,2688]{2,1,0:T(8,128)(2,1)} %pack_weights.1), calls=%async_computation.2 | async-start | bytes 5505024 | tf_op jit(solution)/shard_map/all_to_all | solution.py:371
  200.9 116.1 %all-to-all-start = ((bf16[256,72,128]{2,1,0:T(8,128)(2,1)}), bf16[256,72,128]{2,1,0:T(8,128)(2,1)}, u32[]{:S(2)}, u32[]{:S(2)}) async-start(bf16[256,72,128]{2,1,0:T(8,128)(2,1)} %bitcast.17), calls=%async_computation | async-start | bytes 9437184 | tf_op jit(solution)/shard_map/all_to_all | solution.py:354
  221.7 9.0 %collective-permute-start = (f32[4,288,896]{2,1,0:T(8,128)S(1)}, f32[4,288,896]{2,1,0:T(8,128)S(1)}, u32[]{:S(2)}, u32[]{:S(2)}) collective-permute-start(f32[4,288,896]{2,1,0:T(8,128)S(1)} %bitcast.15), channel_id=1, source_target_pairs={{0,32},{32,0},{64,96},{96,64},{128,160},{160,128},{192,224},{224,1... | collective-permute-start | bytes 12386312 | tf_op jit(solution)/shard_map/ppermute | solution.py:347
  231.4 20.9 %collective-permute-start.1 = (bf16[288,896]{1,0:T(8,128)(2,1)S(1)}, bf16[288,896]{1,0:T(8,128)(2,1)S(1)}, u32[]{:S(2)}, u32[]{:S(2)}) collective-permute-start(bf16[288,896]{1,0:T(8,128)(2,1)S(1)} %get-tuple-element.27), channel_id=1, source_target_pairs={{0,192},{32,224},{64,0},{96,32},{128,64},{160,96},{192,128},{224,1... | collective-permute-start | bytes 1548296 | tf_op jit(solution)/shard_map/ppermute | solution.py:344
  232.2 22.7 %collective-permute-start.2 = (bf16[288,896]{1,0:T(8,128)(2,1)S(1)}, bf16[288,896]{1,0:T(8,128)(2,1)S(1)}, u32[]{:S(2)}, u32[]{:S(2)}) collective-permute-start(bf16[288,896]{1,0:T(8,128)(2,1)S(1)} %get-tuple-element.28), channel_id=1, source_target_pairs={{0,128},{32,160},{64,192},{96,224},{128,0},{160,32},{192,64},{224,... | collective-permute-start | bytes 1548296 | tf_op jit(solution)/shard_map/ppermute | solution.py:344
  232.7 42.7 %collective-permute-start.3 = (bf16[288,896]{1,0:T(8,128)(2,1)S(1)}, bf16[288,896]{1,0:T(8,128)(2,1)S(1)}, u32[]{:S(2)}, u32[]{:S(2)}) collective-permute-start(bf16[288,896]{1,0:T(8,128)(2,1)S(1)} %get-tuple-element.29), channel_id=1, source_target_pairs={{0,64},{32,96},{64,128},{96,160},{128,192},{160,224},{192,0},{224,... | collective-permute-start | bytes 1548296 | tf_op jit(solution)/shard_map/ppermute | solution.py:344
  276.1 13.7 %collective-permute-start.9 = (bf16[288,448]{1,0:T(8,128)(2,1)S(1)}, bf16[288,448]{1,0:T(8,128)(2,1)S(1)}, u32[]{:S(2)}, u32[]{:S(2)}) collective-permute-start(bf16[288,448]{1,0:T(8,128)(2,1)S(1)} %get-tuple-element.44.refs_1_.refs_0_), channel_id=1, source_target_pairs={{0,192},{32,224},{64,0},{96,32},{128,64},{160,96},{192,128},{224,1... | collective-permute-start | bytes 774152 | tf_op jit(solution)/shard_map/ppermute | solution.py:344
  276.1 15.4 %collective-permute-start.7 = (bf16[288,448]{1,0:T(8,128)(2,1)S(1)}, bf16[288,448]{1,0:T(8,128)(2,1)S(1)}, u32[]{:S(2)}, u32[]{:S(2)}) collective-permute-start(bf16[288,448]{1,0:T(8,128)(2,1)S(1)} %get-tuple-element.44.refs_1_.refs_0_), channel_id=1, source_target_pairs={{0,128},{32,160},{64,192},{96,224},{128,0},{160,32},{192,64},{224,... | collective-permute-start | bytes 774152 | tf_op jit(solution)/shard_map/ppermute | solution.py:344
  276.6 27.2 %collective-permute-start.5 = (bf16[288,448]{1,0:T(8,128)(2,1)S(1)}, bf16[288,448]{1,0:T(8,128)(2,1)S(1)}, u32[]{:S(2)}, u32[]{:S(2)}) collective-permute-start(bf16[288,448]{1,0:T(8,128)(2,1)S(1)} %get-tuple-element.44.refs_1_.refs_0_), channel_id=1, source_target_pairs={{0,64},{32,96},{64,128},{96,160},{128,192},{160,224},{192,0},{224,... | collective-permute-start | bytes 774152 | tf_op jit(solution)/shard_map/ppermute | solution.py:344
  277.6 39.4 %collective-permute-start.4 = (bf16[288,448]{1,0:T(8,128)(2,1)S(1)}, bf16[288,448]{1,0:T(8,128)(2,1)}, u32[]{:S(2)}, u32[]{:S(2)}) collective-permute-start(bf16[288,448]{1,0:T(8,128)(2,1)S(1)} %get-tuple-element.44.refs_1_.refs_0_), channel_id=1, source_target_pairs={{0,32},{32,0},{64,96},{96,64},{128,160},{160,128},{192,224},{224,1... | collective-permute-start | bytes 774152 | tf_op jit(solution)/shard_map/ppermute | solution.py:347
  289.7 27.3 %collective-permute-start.10 = (bf16[288,448]{1,0:T(8,128)(2,1)S(1)}, bf16[288,448]{1,0:T(8,128)(2,1)}, u32[]{:S(2)}, u32[]{:S(2)}) collective-permute-start(bf16[288,448]{1,0:T(8,128)(2,1)S(1)} %collective-permute-done.9.refs_7_.refs_6_), channel_id=1, source_target_pairs={{0,32},{32,0},{64,96},{96,64},{128,160},{160,128},{192,224},{224,1... | collective-permute-start | bytes 774152 | tf_op jit(solution)/shard_map/ppermute | solution.py:347
  291.6 25.4 %collective-permute-start.8 = (bf16[288,448]{1,0:T(8,128)(2,1)S(1)}, bf16[288,448]{1,0:T(8,128)(2,1)}, u32[]{:S(2)}, u32[]{:S(2)}) collective-permute-start(bf16[288,448]{1,0:T(8,128)(2,1)S(1)} %collective-permute-done.7.refs_5_.refs_4_), channel_id=1, source_target_pairs={{0,32},{32,0},{64,96},{96,64},{128,160},{160,128},{192,224},{224,1... | collective-permute-start | bytes 774152 | tf_op jit(solution)/shard_map/ppermute | solution.py:347
  303.9 13.2 %collective-permute-start.6 = (bf16[288,448]{1,0:T(8,128)(2,1)S(1)}, bf16[288,448]{1,0:T(8,128)(2,1)}, u32[]{:S(2)}, u32[]{:S(2)}) collective-permute-start(bf16[288,448]{1,0:T(8,128)(2,1)S(1)} %collective-permute-done.5.refs_3_.refs_2_), channel_id=1, source_target_pairs={{0,32},{32,0},{64,96},{96,64},{128,160},{160,128},{192,224},{224,1... | collective-permute-start | bytes 774152 | tf_op jit(solution)/shard_map/ppermute | solution.py:347
  325.1 4.6 %collective-permute-start.11 = (f32[4,288,448]{2,1,0:T(8,128)S(1)}, f32[4,288,448]{2,1,0:T(8,128)S(1)}, u32[]{:S(2)}, u32[]{:S(2)}) collective-permute-start(f32[4,288,448]{2,1,0:T(8,128)S(1)} %bitcast.16), channel_id=1, source_target_pairs={{0,32},{32,0},{64,96},{96,64},{128,160},{160,128},{192,224},{224,1... | collective-permute-start | bytes 6193160 | tf_op jit(solution)/shard_map/ppermute | solution.py:347
  330.1 7.7 %collective-permute-start.12 = (bf16[144,896]{1,0:T(8,128)(2,1)S(1)}, bf16[144,896]{1,0:T(8,128)(2,1)S(1)}, u32[]{:S(2)}, u32[]{:S(2)}) collective-permute-start(bf16[144,896]{1,0:T(8,128)(2,1)S(1)} %get-tuple-element.34), channel_id=1, source_target_pairs={{0,192},{32,224},{64,0},{96,32},{128,64},{160,96},{192,128},{224,1... | collective-permute-start | bytes 774152 | tf_op jit(solution)/shard_map/ppermute | solution.py:344
  330.9 8.7 %collective-permute-start.13 = (bf16[144,896]{1,0:T(8,128)(2,1)S(1)}, bf16[144,896]{1,0:T(8,128)(2,1)S(1)}, u32[]{:S(2)}, u32[]{:S(2)}) collective-permute-start(bf16[144,896]{1,0:T(8,128)(2,1)S(1)} %get-tuple-element.35), channel_id=1, source_target_pairs={{0,128},{32,160},{64,192},{96,224},{128,0},{160,32},{192,64},{224,... | collective-permute-start | bytes 774152 | tf_op jit(solution)/shard_map/ppermute | solution.py:344
  332.1 13.9 %collective-permute-start.14 = (bf16[144,896]{1,0:T(8,128)(2,1)S(1)}, bf16[144,896]{1,0:T(8,128)(2,1)S(1)}, u32[]{:S(2)}, u32[]{:S(2)}) collective-permute-start(bf16[144,896]{1,0:T(8,128)(2,1)S(1)} %get-tuple-element.36), channel_id=1, source_target_pairs={{0,64},{32,96},{64,128},{96,160},{128,192},{160,224},{192,0},{224,... | collective-permute-start | bytes 774152 | tf_op jit(solution)/shard_map/ppermute | solution.py:344
  346.5 12.9 %collective-permute-start.20 = (bf16[288,896]{1,0:T(8,128)(2,1)S(1)}, bf16[288,896]{1,0:T(8,128)(2,1)S(1)}, u32[]{:S(2)}, u32[]{:S(2)}) collective-permute-start(bf16[288,896]{1,0:T(8,128)(2,1)S(1)} %slopes.1.refs_0_), channel_id=1, source_target_pairs={{0,192},{32,224},{64,0},{96,32},{128,64},{160,96},{192,128},{224,1... | collective-permute-start | bytes 1548296 | tf_op jit(solution)/shard_map/ppermute | solution.py:344
  346.6 15.9 %collective-permute-start.18 = (bf16[288,896]{1,0:T(8,128)(2,1)S(1)}, bf16[288,896]{1,0:T(8,128)(2,1)S(1)}, u32[]{:S(2)}, u32[]{:S(2)}) collective-permute-start(bf16[288,896]{1,0:T(8,128)(2,1)S(1)} %slopes.1.refs_0_), channel_id=1, source_target_pairs={{0,128},{32,160},{64,192},{96,224},{128,0},{160,32},{192,64},{224,... | collective-permute-start | bytes 1548296 | tf_op jit(solution)/shard_map/ppermute | solution.py:344
  347.9 25.0 %collective-permute-start.16 = (bf16[288,896]{1,0:T(8,128)(2,1)S(1)}, bf16[288,896]{1,0:T(8,128)(2,1)S(1)}, u32[]{:S(2)}, u32[]{:S(2)}) collective-permute-start(bf16[288,896]{1,0:T(8,128)(2,1)S(1)} %slopes.1.refs_0_), channel_id=1, source_target_pairs={{0,64},{32,96},{64,128},{96,160},{128,192},{160,224},{192,0},{224,... | collective-permute-start | bytes 1548296 | tf_op jit(solution)/shard_map/ppermute | solution.py:344
  355.6 17.8 %collective-permute-start.15 = (bf16[288,896]{1,0:T(8,128)(2,1)S(1)}, bf16[288,896]{1,0:T(8,128)(2,1)S(1)}, u32[]{:S(2)}, u32[]{:S(2)}) collective-permute-start(bf16[288,896]{1,0:T(8,128)(2,1)S(1)} %slopes.1.refs_0_), channel_id=1, source_target_pairs={{0,32},{32,0},{64,96},{96,64},{128,160},{160,128},{192,224},{224,1... | collective-permute-start | bytes 1548296 | tf_op jit(solution)/shard_map/ppermute | solution.py:347
  360.2 13.2 %collective-permute-start.21 = (bf16[288,896]{1,0:T(8,128)(2,1)}, bf16[288,896]{1,0:T(8,128)(2,1)S(1)}, u32[]{:S(2)}, u32[]{:S(2)}) collective-permute-start(bf16[288,896]{1,0:T(8,128)(2,1)} %follow.5.refs_6_), channel_id=1, source_target_pairs={{0,32},{32,0},{64,96},{96,64},{128,160},{160,128},{192,224},{224,1... | collective-permute-start | bytes 1548296 | tf_op jit(solution)/shard_map/ppermute | solution.py:347
  362.5 10.9 %collective-permute-start.19 = (bf16[288,896]{1,0:T(8,128)(2,1)S(1)}, bf16[288,896]{1,0:T(8,128)(2,1)S(1)}, u32[]{:S(2)}, u32[]{:S(2)}) collective-permute-start(bf16[288,896]{1,0:T(8,128)(2,1)S(1)} %collective-permute-done.18.refs_4_), channel_id=1, source_target_pairs={{0,32},{32,0},{64,96},{96,64},{128,160},{160,128},{192,224},{224,1... | collective-permute-start | bytes 1548296 | tf_op jit(solution)/shard_map/ppermute | solution.py:347
  372.9 2.0 collective-permute-start.17
  (17 other events, 209.3 us)
